TPU v7x, 32 devices: a whole 2x2x4 slice. The times are simulated.
32 devices in a mesh: gz: 16 (over z, y, x), gy: 2 (over core).
Axes of the slice: x: 2, y: 2, z: 4, core: 2. Of those that a mesh axis runs over, the one named last changes fastest.
Arguments:
- probe_fields: float32 [1, 32, 256, 1024], P(None, 'gz', 'gy'), may hold values from -24 to 24
- root_one: float32 [32, 1024], P('gz'), may hold values from 0.5 to 0.999
- root_two: float32 [32, 1024], P('gz'), may hold values from 0.3 to 0.8
- lateral_kernel_taps: float32 [2, 3], replicated, may hold values from 0.2 to 1
- dilations: int32 [2], replicated, may hold values from 1 to 8, as said below
Outputs:
- covariance_image: float32 [1, 32, 256, 1024], P(None, 'gz', 'gy')
Inputs may be any that keep to these rules, and one draw needn't show every extreme that they name: `dilations`: one entry equals 8 and the other is smaller.
All inputs are finite; a program needn't handle non-finite values.
Results may differ from a plain program's by a relative error of at most 0.000044.
Values sent between devices are 32-bit elements; how exact they have to be, the bound alone decides.
No kernel may reach another device: no remote copies, remote signals or barrier semaphores. Data moves between devices by JAX's collectives and lax.ppermute only.
A program may use at most 64 MiB of HBM per device.

v0:
```python
import jax
import jax.numpy as jnp
from jax import lax
from jax.sharding import PartitionSpec as P

RADIUS = 2
DMAX = 8


def padded_2(array, sides, width):
    for axis, dim in sides:
        size, length = (lax.axis_size(axis), array.shape[dim])
        up = [(i, (i + 1) % size) for i in range(size - 1)]
        down = [(j, i) for i, j in up]
        last = lax.slice_in_dim(array, length - width, length, axis=dim)
        leading = lax.slice_in_dim(array, 0, width, axis=dim)
        before = lax.ppermute(last, axis, up)
        after = lax.ppermute(leading, axis, down)
        array = jnp.concatenate([before, array, after], axis=dim)
    return array


def filter_coefficients(root_one, root_two):
    first = root_one + root_two
    second = -root_one * root_two
    gain = (1.0 - root_one) * (1.0 - root_two)
    return (first, second, gain)


def depth_scan(fields, first, second, pre_gain, post_gain, reverse):
    moved = jnp.moveaxis(fields, 1, 0)
    zero = jnp.zeros(moved.shape[1:], jnp.float32)

    def advance(carry, inputs):
        latest, earlier = carry
        plane, coef_one, coef_two, before, after = inputs
        value = before * plane + coef_one * latest + coef_two * earlier
        return ((value, latest), after * value)

    _, outputs = lax.scan(
        advance, (zero, zero), (moved, first, second, pre_gain, post_gain), reverse=reverse
    )
    return jnp.moveaxis(outputs, 0, 1)


def lateral_padded(padded, weights, dilation, axis, margin, length):
    total = weights[0] + 2.0 * jnp.sum(weights[1:])
    scaled = weights / total
    result = scaled[0] * lax.dynamic_slice_in_dim(padded, margin, length, axis)
    for offset_tap in range(1, weights.shape[0]):
        offset = dilation * offset_tap
        upper = lax.dynamic_slice_in_dim(padded, margin + offset, length, axis)
        lower = lax.dynamic_slice_in_dim(padded, margin - offset, length, axis)
        result = result + scaled[offset_tap] * (upper + lower)
    return result


def lateral_x(fields, weights, dilation):
    margin = RADIUS * DMAX
    padded = jnp.pad(fields, ((0, 0), (0, 0), (0, 0), (margin, margin)))
    return lateral_padded(padded, weights, dilation, 3, margin, fields.shape[3])


def lateral_y_twice(fields, weights, dilation):
    margin = RADIUS * DMAX
    rows = fields.shape[2]
    padded = padded_2(fields, (("gy", 2),), 2 * margin)
    middle = lateral_padded(padded, weights, dilation, 2, margin, rows + 2 * margin)
    global_row = lax.axis_index("gy") * rows - margin + jnp.arange(rows + 2 * margin)
    inside = (global_row >= 0) & (global_row < rows * lax.axis_size("gy"))
    middle = jnp.where(inside[None, None, :, None], middle, 0.0)
    return lateral_padded(middle, weights, dilation, 2, margin, rows)


def target_depth(fields):
    return lax.all_to_all(fields, "gz", split_axis=2, concat_axis=1, tiled=True)


def from_depth(fields):
    return lax.all_to_all(fields, "gz", split_axis=1, concat_axis=2, tiled=True)


def body(probe_fields, root_one, root_two, lateral_kernel_taps, dilations):
    whole_one, whole_two = (
        lax.all_gather(root_one, "gz", axis=0, tiled=True),
        lax.all_gather(root_two, "gz", axis=0, tiled=True),
    )
    first, second, gain = filter_coefficients(whole_one, whole_two)
    unity = jnp.ones_like(gain)
    first_next = jnp.concatenate([first[1:], jnp.zeros_like(first[:1])], 0)
    second_next = jnp.concatenate([second[2:], jnp.zeros_like(second[:2])], 0)
    field = from_depth(
        depth_scan(target_depth(probe_fields), first_next, second_next, unity, gain, True)
    )
    field = lateral_x(field, lateral_kernel_taps[0], dilations[0])
    field = lateral_y_twice(field, lateral_kernel_taps[1], dilations[1])
    field = lateral_x(field, lateral_kernel_taps[0], dilations[0])
    return from_depth(depth_scan(target_depth(field), first, second, gain, unity, False))


def solution(mesh):
    placed = (P(None, "gz", "gy", None), P("gz", None), P("gz", None), P(), P())
    return jax.shard_map(
        body, mesh=mesh, in_specs=placed, out_specs=P(None, "gz", "gy", None), check_vma=False
    )
```

profile of v0, /device:TPU:0, one launch (start us, length us, event | category | flops | bytes accessed | tf_op | source)
XLA Modules:
  0.0 234.3 jit_solution(13808866717618316698)
XLA Ops:
  0.0 3.0 %copy.15 = f32[1,2,128,1024]{3,1,0,2:T(2,128)} copy(f32[1,2,128,1024]{3,2,1,0:T(8,128)} %param.9) | data formatting | bytes 2097152 | tf_op args[0]
  3.0 8.4 %all-to-all-start = ((f32[1,2,128,1024]{3,1,0,2:T(2,128)}), f32[1,2,128,1024]{3,1,0,2:T(2,128)S(1)}, u32[]{:S(2)}, u32[]{:S(2)}) async-start(f32[1,2,128,1024]{3,1,0,2:T(2,128)} %copy.15), calls=%async_computation | async-start | bytes 2097152 | tf_op jit(solution)/shard_map/all_to_all | solution.py:76
  11.5 51.6 %all-gather = f32[16,2,1024]{2,1,0:T(2,128)S(1)} all-gather(f32[1,2,1024]{2,1,0:T(2,128)S(1)} %bitcast.108), channel_id=1, replica_groups=mesh['gz'=16,'gy'=2] {'gz'}, dimensions={0}, use_global_device_ids=true | all-gather | bytes 139264 | tf_op jit(solution)/shard_map/all_gather | solution.py:85
  63.1 0.1 reshape.182
  63.2 38.0 %all-gather.1 = f32[16,2,1024]{2,1,0:T(2,128)S(1)} all-gather(f32[1,2,1024]{2,1,0:T(2,128)S(1)} %bitcast.109), channel_id=1, replica_groups=mesh['gz'=16,'gy'=2] {'gz'}, dimensions={0}, use_global_device_ids=true | all-gather | bytes 139264 | tf_op jit(solution)/shard_map/all_gather | solution.py:86
  101.3 0.1 reshape.184
  101.5 0.3 copy.16
  101.8 1.1 broadcast.96.clone
  102.9 22.0 %while.34 = (s32[]{:T(128)}, f32[1,8,1024]{2,1,0:T(8,128)S(1)}, f32[1,8,1024]{2,1,0:T(8,128)S(1)}, f32[32,1,8,1024]{3,2,1,0:T(8,128)}, f32[32,1,8,1024]{3,2,1,0:...) while((s32[]{:T(128)}, f32[1,8,1024]{2,1,0:T(8,128)S(1)}, ...), condition=%wide.region_3.4_spmd.clone, body=%wide.region_2.3_spmd.clone.sunk | while | flops 49156 | bytes 233615 | solution.py:40
  103.0 0.6 bitcast_dynamic-update-slice_fusion.4
  103.7 0.6 bitcast_dynamic-update-slice_fusion.4
  104.4 0.6 bitcast_dynamic-update-slice_fusion.4
  105.0 0.6 bitcast_dynamic-update-slice_fusion.4
  105.7 0.6 bitcast_dynamic-update-slice_fusion.4
  106.4 0.6 bitcast_dynamic-update-slice_fusion.4
  107.1 0.6 bitcast_dynamic-update-slice_fusion.4
  107.8 0.6 bitcast_dynamic-update-slice_fusion.4
  108.5 0.6 bitcast_dynamic-update-slice_fusion.4
  109.2 0.6 bitcast_dynamic-update-slice_fusion.4
  109.9 0.6 bitcast_dynamic-update-slice_fusion.4
  110.5 0.6 bitcast_dynamic-update-slice_fusion.4
  111.2 0.6 bitcast_dynamic-update-slice_fusion.4
  111.9 0.6 bitcast_dynamic-update-slice_fusion.4
  112.6 0.6 bitcast_dynamic-update-slice_fusion.4
  113.3 0.6 bitcast_dynamic-update-slice_fusion.4
  114.0 0.6 bitcast_dynamic-update-slice_fusion.4
  114.7 0.6 bitcast_dynamic-update-slice_fusion.4
  115.4 0.6 bitcast_dynamic-update-slice_fusion.4
  116.1 0.6 bitcast_dynamic-update-slice_fusion.4
  116.7 0.6 bitcast_dynamic-update-slice_fusion.4
  117.4 0.6 bitcast_dynamic-update-slice_fusion.4
  118.1 0.6 bitcast_dynamic-update-slice_fusion.4
  118.8 0.6 bitcast_dynamic-update-slice_fusion.4
  119.5 0.6 bitcast_dynamic-update-slice_fusion.4
  120.2 0.6 bitcast_dynamic-update-slice_fusion.4
  120.9 0.6 bitcast_dynamic-update-slice_fusion.4
  121.6 0.6 bitcast_dynamic-update-slice_fusion.4
  122.3 0.6 bitcast_dynamic-update-slice_fusion.4
  122.9 0.6 bitcast_dynamic-update-slice_fusion.4
  123.6 0.6 bitcast_dynamic-update-slice_fusion.4
  124.3 0.6 bitcast_dynamic-update-slice_fusion.4
  125.0 3.8 %all-to-all-start.1 = ((f32[1,32,8,1024]{3,2,0,1:T(8,128)}), f32[1,32,8,1024]{3,2,0,1:T(8,128)S(1)}, u32[]{:S(2)}, u32[]{:S(2)}) async-start(f32[1,32,8,1024]{3,2,0,1:T(8,128)} %bitcast.9), calls=%async_computation.1 | async-start | bytes 2097152 | tf_op jit(solution)/shard_map/all_to_all | solution.py:80
  128.8 0.7 fusion.25
  132.9 0.7 slice_reduce_fusion
  135.0 0.5 fusion.23
  136.7 0.7 fusion.24
  137.4 6.9 %all-to-all-done.1 = f32[1,32,8,1024]{3,2,0,1:T(8,128)S(1)} async-done(((f32[1,32,8,1024]{3,2,0,1:T(8,128)}), f32[1,32,8,1024]{3,2,0,1:T(8,128)S(1)}, u32[]{:S(2)}, u32[]{:S(2)}) %all-to-all-start.1) | async-done | bytes 1048608 | tf_op jit(solution)/shard_map/all_to_all | solution.py:80
  144.3 0.1 copy.28
  144.4 3.1 %fusion.9 = f32[1,2,128,1024]{3,2,1,0:T(8,128)S(1)} fusion(s32[]{:T(128)S(6)} %select_n.44, f32[1,2,128,1024]{3,2,1,0:T(8,128)S(1)} %bitcast.94, s32[]{:T(128)S(6)} %select_n.45, s32[]{:T(128)S(6)} %select_n.46, s32[]{:T(128)S(6)} %select_n.47, f32[]{:T(128)} %bitcast.18, f32[]{:T(128)} %bitcast.13, f32[]{:T(128)} %bitcast.3), kind=kLoop, calls=%fused_computation.31 | loop fusion | flops 1835008 | bytes 2097180 | tf_op jit(solution)/shard_map/add | solution.py:54
  147.6 1.3 collective-permute-start
  148.9 1.3 collective-permute-start.1
  155.1 0.2 pad_maximum_fusion
  155.3 2.8 %fusion.5 = f32[1,2,160,1024]{3,2,1,0:T(8,128)S(1)} fusion(f32[1,2,192,1024]{3,2,1,0:T(8,128)S(1)} %pad_maximum_fusion, s32[]{:T(128)S(6)} %select_n.51, s32[]{:T(128)S(6)} %select_n.50, s32[]{:T(128)S(6)} %select_n.49, s32[]{:T(128)S(6)} %select_n.48, f32[]{:T(128)} %bitcast.28, f32[]{:T(128)} %bitcast.23, f32[]{:T(128)} %bitcast.5, ...), kind=kLoop, calls=%fused_computation.19 | loop fusion | flops 2621440 | bytes 7864508 | tf_op jit(solution)/shard_map/jit(_where)/select_n | solution.py:71
  158.1 2.5 %fusion.19 = f32[1,2,128,1024]{3,2,1,0:T(8,128)S(1)} fusion(f32[1,2,160,1024]{3,2,1,0:T(8,128)S(1)} %fusion.5, s32[]{:T(128)S(6)} %select_n.56, s32[]{:T(128)S(6)} %select_n.55, s32[]{:T(128)S(6)} %select_n.54, s32[]{:T(128)S(6)} %select_n.53, f32[]{:T(128)} %bitcast.28, f32[]{:T(128)} %bitcast.23, f32[]{:T(128)} %bitcast.5), kind=kLoop, calls=%fused_computation.42 | loop fusion | flops 1835008 | bytes 6291484 | tf_op jit(solution)/shard_map/add | solution.py:54
  160.6 3.1 %fusion.15 = f32[1,2,128,1024]{3,2,1,0:T(8,128)S(1)} fusion(s32[]{:T(128)S(6)} %select_n.44, f32[1,2,128,1024]{3,2,1,0:T(8,128)S(1)} %fusion.19, s32[]{:T(128)S(6)} %select_n.45, s32[]{:T(128)S(6)} %select_n.46, s32[]{:T(128)S(6)} %select_n.47, f32[]{:T(128)} %bitcast.18, f32[]{:T(128)} %bitcast.13, f32[]{:T(128)} %bitcast.3), kind=kLoop, calls=%fused_computation.37 | loop fusion | flops 1835008 | bytes 2097180 | tf_op jit(solution)/shard_map/add | solution.py:54
  163.7 1.8 copy.18
  165.5 5.2 %all-to-all-start.2 = ((f32[1,2,128,1024]{3,1,0,2:T(2,128)}), f32[1,2,128,1024]{3,1,0,2:T(2,128)S(1)}, u32[]{:S(2)}, u32[]{:S(2)}) async-start(f32[1,2,128,1024]{3,1,0,2:T(2,128)} %copy.18), calls=%async_computation.2 | async-start | bytes 2097152 | tf_op jit(solution)/shard_map/all_to_all | solution.py:76
  170.7 25.6 %all-to-all-done.2 = f32[1,2,128,1024]{3,1,0,2:T(2,128)S(1)} async-done(((f32[1,2,128,1024]{3,1,0,2:T(2,128)}), f32[1,2,128,1024]{3,1,0,2:T(2,128)S(1)}, u32[]{:S(2)}, u32[]{:S(2)}) %all-to-all-start.2) | async-done | bytes 1048608 | tf_op jit(solution)/shard_map/all_to_all | solution.py:76
  196.3 0.3 copy.27
  196.7 0.1 copy.20
  196.7 0.1 broadcast.96
  196.9 3.1 %while.35 = (s32[]{:T(128)}, f32[1,8,1024]{2,1,0:T(8,128)S(1)}, f32[1,8,1024]{2,1,0:T(8,128)S(1)}, f32[32,1,8,1024]{3,2,1,0:T(8,128)S(1)}, f32[32,1024]{1,0:T(8,...) while((s32[]{:T(128)}, f32[1,8,1024]{2,1,0:T(8,128)S(1)}, ...), condition=%wide.region_5.6_spmd.clone, body=%wide.region_4.5_spmd.clone.sunk | while | flops 49155 | bytes 233595 | solution.py:40
  200.0 33.3 %all_to_all.66 = f32[1,32,8,1024]{3,2,0,1:T(8,128)S(1)} all-to-all(f32[1,32,8,1024]{3,2,0,1:T(8,128)S(1)} %bitcast.97), channel_id=1, replica_groups=mesh['gz'=16,'gy'=2] {'gz'}, dimensions={1} | all-to-all | bytes 2097152 | tf_op jit(solution)/shard_map/all_to_all | solution.py:80
  233.2 1.1 copy.26
  (183 shorter events, 2.8 us)
Async XLA Ops:
  3.0 8.5 %copy-start.1 = (f32[2,1024]{1,0:T(2,128)S(1)}, f32[2,1024]{1,0:T(2,128)}, u32[]{:S(2)}) copy-start(f32[2,1024]{1,0:T(2,128)} %param.10) | copy-start | bytes 24580
  3.0 60.2 %copy-start.2 = (f32[2,1024]{1,0:T(2,128)S(1)}, f32[2,1024]{1,0:T(2,128)}, u32[]{:S(2)}) copy-start(f32[2,1024]{1,0:T(2,128)} %param.11) | copy-start | bytes 24580
  3.0 98.5 %all-to-all-start = ((f32[1,2,128,1024]{3,1,0,2:T(2,128)}), f32[1,2,128,1024]{3,1,0,2:T(2,128)S(1)}, u32[]{:S(2)}, u32[]{:S(2)}) async-start(f32[1,2,128,1024]{3,1,0,2:T(2,128)} %copy.15), calls=%async_computation | async-start | bytes 2097152 | tf_op jit(solution)/shard_map/all_to_all | solution.py:76
  125.0 3.8 %copy-start.3 = (s32[2]{0:T(128)S(1)}, s32[2]{0:T(128)}, u32[]{:S(2)}) copy-start(s32[2]{0:T(128)} %param.13) | copy-start | bytes 28
  125.0 7.9 %copy-start = (f32[2,3]{1,0:T(2,128)S(1)}, f32[2,3]{1,0:T(2,128)}, u32[]{:S(2)}) copy-start(f32[2,3]{1,0:T(2,128)} %param.12) | copy-start | bytes 76
  125.0 19.4 %all-to-all-start.1 = ((f32[1,32,8,1024]{3,2,0,1:T(8,128)}), f32[1,32,8,1024]{3,2,0,1:T(8,128)S(1)}, u32[]{:S(2)}, u32[]{:S(2)}) async-start(f32[1,32,8,1024]{3,2,0,1:T(8,128)} %bitcast.9), calls=%async_computation.1 | async-start | bytes 2097152 | tf_op jit(solution)/shard_map/all_to_all | solution.py:80
  147.6 7.5 %collective-permute-start = (f32[1,2,32,1024]{3,2,1,0:T(8,128)S(1)}, f32[1,2,32,1024]{3,2,1,0:T(8,128)S(1)}, u32[]{:S(2)}, u32[]{:S(2)}) collective-permute-start(f32[1,2,32,1024]{3,2,1,0:T(8,128)S(1)} %get-tuple-element.323), channel_id=1, source_target_pairs={{0,1},{2,3},{4,5},{6,7},{8,9},{10,11},{12,13},{14,15},{16,17},{18,... | collective-permute-start | bytes 786440 | tf_op jit(solution)/shard_map/ppermute | solution.py:17
  148.9 6.2 %collective-permute-start.1 = (f32[1,2,32,1024]{3,2,1,0:T(8,128)S(1)}, f32[1,2,32,1024]{3,2,1,0:T(8,128)S(1)}, u32[]{:S(2)}, u32[]{:S(2)}) collective-permute-start(f32[1,2,32,1024]{3,2,1,0:T(8,128)S(1)} %get-tuple-element.324), channel_id=1, source_target_pairs={{1,0},{3,2},{5,4},{7,6},{9,8},{11,10},{13,12},{15,14},{17,16},{19,... | collective-permute-start | bytes 786440 | tf_op jit(solution)/shard_map/ppermute | solution.py:18
  165.5 30.8 %all-to-all-start.2 = ((f32[1,2,128,1024]{3,1,0,2:T(2,128)}), f32[1,2,128,1024]{3,1,0,2:T(2,128)S(1)}, u32[]{:S(2)}, u32[]{:S(2)}) async-start(f32[1,2,128,1024]{3,1,0,2:T(2,128)} %copy.18), calls=%async_computation.2 | async-start | bytes 2097152 | tf_op jit(solution)/shard_map/all_to_all | solution.py:76
where the time goes:
time: 235 us; the launch traced here: 234 us
  blocking collectives  123 us (52%)
  other arithmetic  34.2 us (15%)
  waiting for transfers between devices  32.6 us (14%)
  starting transfers between devices  20 us (9%)
  local copies, waits for them, and re-layouts  11.7 us (5%)
  between operations  11.1 us (5%)
    all_gather x1, blocking collectives, body(): lax.all_gather(root_one, 'gz', axis=0, tiled=True)  51.6 us
    all_gather x1, blocking collectives, body(): lax.all_gather(root_two, 'gz', axis=0, tiled=True)  38 us
    all_to_all x1, blocking collectives, from_depth(): return lax.all_to_all(fields, 'gz', split_axis=1, concat_axis=2, tiled=True)  33.3 us
    all_to_all x2, waiting for transfers between devices, target_depth(): return lax.all_to_all(fields, 'gz', split_axis=2, concat_axis=1, tiled=True)  25.6 us
    dynamic_update_slice x64, other arithmetic, depth_scan(): lax.scan(advance, (zero, zero), (moved, first, second, pre_gain, post_gai...  21.7 us
    all_to_all x2, starting transfers between devices, target_depth(): return lax.all_to_all(fields, 'gz', split_axis=2, concat_axis=1, tiled=True)  13.6 us
    add x3, other arithmetic, lateral_padded(): result = result + scaled[offset_tap] * (upper + lower)  8.73 us
    all_to_all x1, waiting for transfers between devices, from_depth(): return lax.all_to_all(fields, 'gz', split_axis=1, concat_axis=2, tiled=True)  6.93 us
  transfers between devices with their start and end apart: 5, of which 2 were waited for; matrix products, arithmetic and copies ran while one was open for 1% of the time, Pallas kernels for 0%

commit v1 on v0

v1 whole, which is shorter than its diff:
```python
import functools

import jax
import jax.numpy as jnp
from jax import lax
from jax.experimental import pallas as pl
from jax.experimental.pallas import tpu as pltpu
from jax.sharding import PartitionSpec as P

RADIUS = 2
DMAX = 8
MARGIN = RADIUS * DMAX
LANES = 128
SUB = 8


def padded_y(array, width):
    size, length = lax.axis_size("gy"), array.shape[2]
    up = [(i, (i + 1) % size) for i in range(size - 1)]
    down = [(j, i) for i, j in up]
    last = lax.slice_in_dim(array, length - width, length, axis=2)
    leading = lax.slice_in_dim(array, 0, width, axis=2)
    before = lax.ppermute(last, "gy", up)
    after = lax.ppermute(leading, "gy", down)
    return jnp.concatenate([before, array, after], axis=2)


def filter_coefficients(root_one, root_two):
    first = root_one + root_two
    second = -root_one * root_two
    gain = (1.0 - root_one) * (1.0 - root_two)
    return (first, second, gain)


def depth_scan(fields, first, second, pre_gain, post_gain, reverse):
    moved = jnp.moveaxis(fields, 1, 0)
    zero = jnp.zeros(moved.shape[1:], jnp.float32)

    def advance(carry, inputs):
        latest, earlier = carry
        plane, coef_one, coef_two, before, after = inputs
        value = before * plane + coef_one * latest + coef_two * earlier
        return ((value, latest), after * value)

    _, outputs = lax.scan(
        advance, (zero, zero), (moved, first, second, pre_gain, post_gain), reverse=reverse
    )
    return jnp.moveaxis(outputs, 0, 1)


def normalised(weights):
    return weights / (weights[..., :1] + 2.0 * jnp.sum(weights[..., 1:], -1, keepdims=True))


def lateral_padded(padded, scaled, dilation, axis, margin, length):
    result = scaled[0] * lax.dynamic_slice_in_dim(padded, margin, length, axis)
    for offset_tap in range(1, scaled.shape[0]):
        offset = dilation * offset_tap
        upper = lax.dynamic_slice_in_dim(padded, margin + offset, length, axis)
        lower = lax.dynamic_slice_in_dim(padded, margin - offset, length, axis)
        result = result + scaled[offset_tap] * (upper + lower)
    return result


def lateral_x(fields, scaled, dilation):
    padded = jnp.pad(fields, ((0, 0), (0, 0), (0, 0), (MARGIN, MARGIN)))
    return lateral_padded(padded, scaled, dilation, 3, MARGIN, fields.shape[3])


def lateral_y_twice(fields, scaled, dilation):
    rows = fields.shape[2]
    padded = padded_y(fields, 2 * MARGIN)
    middle = lateral_padded(padded, scaled, dilation, 2, MARGIN, rows + 2 * MARGIN)
    global_row = lax.axis_index("gy") * rows - MARGIN + jnp.arange(rows + 2 * MARGIN)
    inside = (global_row >= 0) & (global_row < rows * lax.axis_size("gy"))
    middle = jnp.where(inside[None, None, :, None], middle, 0.0)
    return lateral_padded(middle, scaled, dilation, 2, MARGIN, rows)


def plain_body(probe_fields, root_one, root_two, lateral_kernel_taps, dilations):
    roots = lax.all_gather(jnp.stack([root_one, root_two], 1), "gz", axis=0, tiled=True)
    first, second, gain = filter_coefficients(roots[:, 0], roots[:, 1])
    unity = jnp.ones_like(gain)
    first_next = jnp.concatenate([first[1:], jnp.zeros_like(first[:1])], 0)
    second_next = jnp.concatenate([second[2:], jnp.zeros_like(second[:2])], 0)
    scaled = normalised(lateral_kernel_taps)
    field = lateral_y_twice(probe_fields, scaled[1], dilations[1])
    field = lax.all_to_all(field, "gz", split_axis=2, concat_axis=1, tiled=True)
    field = depth_scan(field, first_next, second_next, unity, gain, True)
    field = lateral_x(field, scaled[0], dilations[0])
    field = lateral_x(field, scaled[0], dilations[0])
    field = depth_scan(field, first, second, gain, unity, False)
    return lax.all_to_all(field, "gz", split_axis=1, concat_axis=2, tiled=True)


def call(kernel, outs, scratch, scalars, arrays, flops=1 << 20):
    arrays = [pltpu.with_memory_space_constraint(a, pltpu.VMEM) for a in arrays]
    return pl.pallas_call(
        kernel,
        out_shape=[pltpu.VMEM(shape, jnp.float32) for shape in outs],
        in_specs=[pl.BlockSpec(memory_space=pltpu.SMEM)] * len(scalars)
        + [pl.BlockSpec(memory_space=pltpu.VMEM)] * len(arrays),
        out_specs=[pl.BlockSpec(memory_space=pltpu.VMEM)] * len(outs),
        scratch_shapes=[pltpu.VMEM(shape, jnp.float32) for shape in scratch],
        compiler_params=pltpu.CompilerParams(vmem_limit_bytes=24 << 20),
        cost_estimate=pl.CostEstimate(flops=flops, bytes_accessed=1 << 20, transcendentals=0),
    )(*scalars, *arrays)


def weighted(centre, pairs, taps):
    total = taps[0] * centre
    for tap, (upper, lower) in zip(taps[1:], pairs):
        total = total + tap * (upper + lower)
    return total


def y_twice_kernel(groups, sizes, ints, taps, x_ref, top_ref, bottom_ref, *rest):
    outs, (wide, middle) = rest[:groups], rest[groups:]
    planes, rows, columns = x_ref.shape
    step, mine, row_at, row_places = ints[1], ints[2] % groups, ints[3], sizes
    taps = [taps[1, i] for i in range(RADIUS + 1)]
    inner = rows + 2 * MARGIN
    row_id = lax.broadcasted_iota(jnp.int32, (inner, LANES), 0) + (row_at * rows - MARGIN)
    inside = (row_id >= 0) & (row_id < rows * row_places)
    has_top, has_bottom = row_at > 0, row_at < row_places - 1
    each = rows // groups

    def block(b, _):
        lanes = pl.ds(pl.multiple_of(b * LANES, LANES), LANES)
        for p in range(planes):
            top, bottom = top_ref[p, :, lanes], bottom_ref[p, :, lanes]
            wide[p, 0 : 2 * MARGIN] = jnp.where(has_top, top, jnp.zeros_like(top))
            wide[p, 2 * MARGIN : 2 * MARGIN + rows] = x_ref[p, :, lanes]
            wide[p, 2 * MARGIN + rows :] = jnp.where(has_bottom, bottom, jnp.zeros_like(bottom))
        for p in range(planes):
            pairs = [
                (
                    wide[p, pl.ds(MARGIN + t * step, inner)],
                    wide[p, pl.ds(MARGIN - t * step, inner)],
                )
                for t in range(1, RADIUS + 1)
            ]
            value = weighted(wide[p, MARGIN : MARGIN + inner], pairs, taps)
            middle[p] = jnp.where(inside, value, jnp.zeros_like(value))
        for p in range(planes):
            for m, out in enumerate(outs):
                at = (mine ^ m) * each + MARGIN
                pairs = [
                    (
                        middle[p, pl.ds(at + t * step, each)],
                        middle[p, pl.ds(at - t * step, each)],
                    )
                    for t in range(1, RADIUS + 1)
                ]
                centre = middle[p, pl.ds(pl.multiple_of(at, SUB), each)]
                out[p, :, lanes] = weighted(centre, pairs, taps)
        return 0

    lax.fori_loop(0, columns // LANES, block, 0)


def x_twice(blocks, step, taps):
    lane = lax.broadcasted_iota(jnp.int32, (SUB, LANES), 1)
    zero = jnp.zeros((SUB, LANES), jnp.float32)
    count = len(blocks)
    for _ in range(2):
        sums = [taps[0] * block for block in blocks]
        for t in range(1, RADIUS + 1):
            shift = t * step
            right = [pltpu.roll(block, shift, 1) for block in blocks]
            left = [pltpu.roll(block, LANES - shift, 1) for block in blocks]
            from_right, from_left = lane >= shift, lane < LANES - shift
            for i in range(count):
                lower = jnp.where(from_right, right[i], right[i - 1] if i else zero)
                upper = jnp.where(from_left, left[i], left[i + 1] if i + 1 < count else zero)
                sums[i] = sums[i] + taps[t] * (upper + lower)
        blocks = sums
    return blocks


def get(ref, *at):
    columns = ref.shape[-1]
    return [ref[(*at, slice(i, i + LANES))] for i in range(0, columns, LANES)]


def put(ref, blocks, *at):
    for i, block in enumerate(blocks):
        ref[(*at, slice(i * LANES, (i + 1) * LANES))] = block


def fma(*terms):
    products = [[x * y for x, y in zip(xs, ys)] for xs, ys in terms]
    return functools.reduce(add, products)


def add(a, b):
    return [x + y for x, y in zip(a, b)]


def store_coefficients(roots, planes, mine, first, second, gain):
    groups = roots.shape[0] // (2 * planes)
    count, columns = groups * planes, roots.shape[1]
    for extra in range(2):
        first[count + extra] = jnp.zeros((SUB, columns), jnp.float32)
        second[count + extra] = jnp.zeros((SUB, columns), jnp.float32)
    for e in range(groups):
        for p in range(planes):
            at = (mine ^ e) * planes + p
            one = roots[pl.ds(2 * planes * e + p, 1), :]
            two = roots[pl.ds(2 * planes * e + planes + p, 1), :]
            wide = (SUB, columns)
            first[at] = jnp.broadcast_to(one + two, wide)
            second[at] = jnp.broadcast_to(-one * two, wide)
            gain[at] = jnp.broadcast_to((1.0 - one) * (1.0 - two), wide)


def down_and_up(count, tile, source, middle, first, second, gain, step, taps, finish, extra=None):
    zeros = get(first, count, slice(None))

    def back(i, carry):
        k = count - 1 - i
        latest, earlier = carry
        value = fma((get(first, k + 1, slice(None)), latest), (get(second, k + 2, slice(None)), earlier))
        if source is not None:
            value = add(value, source(k))
        scaled = [g * v for g, v in zip(get(gain, k, slice(None)), value)]
        put(middle, x_twice(scaled, step, taps), k, slice(None))
        return value, latest

    start = (zeros, zeros)
    begin = 0
    if extra is not None:
        a, b = extra
        k = count - 1
        scaled = [g * v for g, v in zip(get(gain, k, slice(None)), a)]
        put(middle, x_twice(scaled, step, taps), k, slice(None))
        k = count - 2
        value = add(fma((get(first, k + 1, slice(None)), a)), b)
        scaled = [g * v for g, v in zip(get(gain, k, slice(None)), value)]
        put(middle, x_twice(scaled, step, taps), k, slice(None))
        start, begin = (value, a), 2
    back_last = lax.fori_loop(begin, count, back, start)

    def forth(k, carry):
        latest, earlier = carry
        value = fma(
            (get(gain, k, slice(None)), get(middle, k, slice(None))),
            (get(first, k, slice(None)), latest),
            (get(second, k, slice(None)), earlier),
        )
        if finish is not None:
            finish(k, value)
        return value, latest

    forth_last = lax.fori_loop(0, count, forth, (zeros, zeros))
    return back_last, forth_last


def local_kernel(groups, planes, ints, taps, roots, *rest):
    pieces, (result, message, first, second, gain, field, middle) = rest[:groups], rest[groups:]
    mine, half = ints[2] % groups, ints[2] // groups
    step, taps = ints[0], [taps[0, i] for i in range(RADIUS + 1)]
    count = groups * planes
    rows = pieces[0].shape[1]
    store_coefficients(roots, planes, mine, first, second, gain)
    for m, piece in enumerate(pieces):
        for p in range(planes):
            field[(mine ^ m) * planes + p] = piece[p]
    everywhere = slice(None)

    def tile_at(tile, _):
        tile_rows = pl.ds(pl.multiple_of(tile * SUB, SUB), SUB)
        (z0, z1), (y1, y2) = down_and_up(
            count,
            tile,
            lambda k: get(field, k, tile_rows),
            middle,
            first,
            second,
            gain,
            step,
            taps,
            lambda k, value: put(result, value, k, tile_rows),
        )

        @pl.when(half > 0)
        def _():
            ahead = fma(
                (get(first, 0, everywhere), z0),
                (get(second, 1, everywhere), z1),
            )
            put(message, ahead, 0, tile_rows)
            put(message, fma((get(second, 0, everywhere), z0)), 1, tile_rows)

        @pl.when(half == 0)
        def _():
            put(message, y1, 0, tile_rows)
            put(message, y2, 1, tile_rows)

        return 0

    lax.fori_loop(0, rows // SUB, tile_at, 0)


def forward_kernel(groups, planes, ints, taps, roots, message, state, first, second, gain, middle):
    mine, half = ints[2] % groups, ints[2] // groups
    step, taps = ints[0], [taps[0, i] for i in range(RADIUS + 1)]
    count = groups * planes
    rows = message.shape[1]

    @pl.when(half > 0)
    def _():
        store_coefficients(roots, planes, mine, first, second, gain)

        def tile_at(tile, _):
            tile_rows = pl.ds(pl.multiple_of(tile * SUB, SUB), SUB)
            carried = (get(message, 0, tile_rows), get(message, 1, tile_rows))
            _, (y1, y2) = down_and_up(
                count, tile, None, middle, first, second, gain, step, taps, None, carried
            )
            put(state, y1, 0, tile_rows)
            put(state, y2, 1, tile_rows)
            return 0

        lax.fori_loop(0, rows // SUB, tile_at, 0)

    @pl.when(half == 0)
    def _():
        state[...] = jnp.zeros(state.shape, jnp.float32)


def join_kernel(groups, planes, ints, taps, local, received, state, first, second, gain, *rest):
    outs, (total, middle) = rest[:groups], rest[groups:]
    mine, half = ints[2] % groups, ints[2] // groups
    step, taps = ints[0], [taps[0, i] for i in range(RADIUS + 1)]
    count = groups * planes
    rows = received.shape[1]
    everywhere = slice(None)

    def tile_at(tile, _):
        tile_rows = pl.ds(pl.multiple_of(tile * SUB, SUB), SUB)
        a, b = get(received, 0, tile_rows), get(received, 1, tile_rows)

        @pl.when(half == 0)
        def _():
            def finish(k, value):
                put(total, add(value, get(local, k, tile_rows)), k, tile_rows)

            down_and_up(
                count, tile, None, middle, first, second, gain, step, taps, finish, (a, b)
            )

        @pl.when(half > 0)
        def _():
            def forth(k, carry):
                latest, earlier = carry
                value = fma(
                    (get(first, k, everywhere), latest), (get(second, k, everywhere), earlier)
                )
                put(total, add(value, get(local, k, tile_rows)), k, tile_rows)
                return value, latest

            start = (add(a, get(state, 0, tile_rows)), add(b, get(state, 1, tile_rows)))
            lax.fori_loop(0, count, forth, start)

        return 0

    lax.fori_loop(0, rows // SUB, tile_at, 0)
    for m, out in enumerate(outs):
        for p in range(planes):
            out[p] = total[(mine ^ m) * planes + p]


def place_kernel(groups, ints, *rest):
    pieces, out = rest[:groups], rest[groups]
    mine = ints[2] % groups
    each = pieces[0].shape[1]
    for m, piece in enumerate(pieces):
        out[:, pl.ds(pl.multiple_of((mine ^ m) * each, SUB), each), :] = piece[...]


def grouped_body(probe_fields, root_one, root_two, lateral_kernel_taps, dilations):
    _, planes, rows, columns = probe_fields.shape
    places, row_places = lax.axis_size("gz"), lax.axis_size("gy")
    groups = places // 2
    each, count = rows // groups, groups * planes
    at, row_at = lax.axis_index("gz"), lax.axis_index("gy")
    ints = jnp.stack([dilations[0], dilations[1], at, row_at]).astype(jnp.int32)
    taps = normalised(lateral_kernel_taps)

    def across(array, m):
        return lax.ppermute(array, "gz", [(i, i ^ m) for i in range(places)])

    field = probe_fields[0]
    width = 2 * MARGIN
    start = jnp.where(row_at == 0, rows - width, 0)
    edge = lax.dynamic_slice_in_dim(field, start, width, axis=1)
    edge = lax.ppermute(edge, "gy", [(0, 1), (1, 0)])

    roots = jnp.concatenate([root_one, root_two], 0)
    for bit in range(groups.bit_length() - 1):
        roots = jnp.concatenate([roots, across(roots, 1 << bit)], 0)
    other_roots = across(roots, groups)

    piece, tile = (planes, each, columns), (count, SUB, columns)
    coefficients = (count + 2, SUB, columns)
    pieces = call(
        functools.partial(y_twice_kernel, groups, row_places),
        [piece] * groups,
        [(planes, rows + 4 * MARGIN, LANES), (planes, rows + 2 * MARGIN, LANES)],
        [ints, taps],
        [field, edge, edge],
    )
    pieces = [pieces[0]] + [across(pieces[m], m) for m in range(1, groups)]
    local, message, first, second, gain = call(
        functools.partial(local_kernel, groups, planes),
        [(count, each, columns), (2, each, columns), coefficients, coefficients, coefficients],
        [(count, each, columns), tile],
        [ints, taps],
        [roots, *pieces],
    )
    received = across(message, groups)
    (state,) = call(
        functools.partial(forward_kernel, groups, planes),
        [(2, each, columns)],
        [coefficients, coefficients, coefficients, tile],
        [ints, taps],
        [other_roots, message],
    )
    pieces = call(
        functools.partial(join_kernel, groups, planes),
        [piece] * groups,
        [(count, each, columns), tile],
        [ints, taps],
        [local, received, state, first, second, gain],
    )
    pieces = [pieces[0]] + [across(pieces[m], m) for m in range(1, groups)]
    (out,) = call(
        functools.partial(place_kernel, groups),
        [(planes, rows, columns)],
        [],
        [ints],
        pieces,
    )
    return out[None]


def body(*arrays):
    probes, planes, rows, columns = arrays[0].shape
    places, row_places = lax.axis_size("gz"), lax.axis_size("gy")
    fits = (
        probes == 1
        and row_places == 2
        and places >= 4
        and places & (places - 1) == 0
        and rows % (SUB * (places // 2)) == 0
        and rows >= 2 * MARGIN
        and columns % LANES == 0
        and planes * places >= 4
    )
    return grouped_body(*arrays) if fits else plain_body(*arrays)


def solution(mesh):
    placed = (P(None, "gz", "gy", None), P("gz", None), P("gz", None), P(), P())
    return jax.shard_map(
        body, mesh=mesh, in_specs=placed, out_specs=P(None, "gz", "gy", None), check_vma=False
    )
```

time: 235 us -> 72.6 us (0.31)
  blocking collectives: 123 us -> 0 us
  other arithmetic: 34.2 us -> 0.39 us
  Pallas kernels: 0 us -> 18.4 us
  between operations: 11.1 us -> 0.09 us
  waiting for transfers between devices: 32.6 us -> 22.6 us
  local copies, waits for them, and re-layouts: 11.7 us -> 3.99 us
  starting transfers between devices: 20 us -> 27 us
    all_gather x2 -> x0, blocking collectives: 89.7 us -> none  [the longest x1 51.6 us: body(): lax.all_gather(root_one, 'gz', axis=0, tiled=True)]
    all_to_all x1 -> x0, blocking collectives: 33.3 us -> none  [from_depth(): return lax.all_to_all(fields, 'gz', split_axis=1, concat_axis=2, tiled=True)]
    all_to_all x3 -> x0, waiting for transfers between devices: 32.6 us -> none  [the longest x2 25.6 us: target_depth(): return lax.all_to_all(fields, 'gz', split_axis=2, concat_axis=1, tiled=True)]
    ppermute x2 -> x20, starting transfers between devices: 2.6 us -> 27 us  [the longest x19 26.5 us: across(): return lax.ppermute(array, 'gz', [(i, i ^ m) for i in range(places)])]
    ppermute x2 -> x20, waiting for transfers between devices: 0.01 us -> 22.6 us  [the longest x19 22.6 us: across(): return lax.ppermute(array, 'gz', [(i, i ^ m) for i in range(places)])]
    dynamic_update_slice x64 -> x0, other arithmetic: 21.7 us -> none  [depth_scan(): lax.scan(advance, (zero, zero), (moved, first, second, pre_gain, post_gai...]
    pallas_call x0 -> x5, Pallas kernels: none -> 18.4 us  [call(): pl.pallas_call(kernel, out_shape=[pltpu.VMEM(shape, jnp.float32) for shap...]
    all_to_all x3 -> x0, starting transfers between devices: 17.4 us -> none  [the longest x2 13.6 us: target_depth(): return lax.all_to_all(fields, 'gz', split_axis=2, concat_axis=1, tiled=True)]
  transfers between devices with their start and end apart: 5 -> 20, of which waited for: 2 -> 9; matrix products, arithmetic and copies ran while one was open for 1% -> 1% of each run, Pallas kernels for 0% -> 14%
where the time goes in v1:
time: 72.6 us; the launch traced here: 72.5 us
  starting transfers between devices  27 us (37%)
  waiting for transfers between devices  22.6 us (31%)
  Pallas kernels  18.4 us (25%)
  local copies, waits for them, and re-layouts  3.99 us (5%)
    ppermute x19, starting transfers between devices, across(): return lax.ppermute(array, 'gz', [(i, i ^ m) for i in range(places)])  26.5 us
    ppermute x19, waiting for transfers between devices, across(): return lax.ppermute(array, 'gz', [(i, i ^ m) for i in range(places)])  22.6 us
    pallas_call x5, Pallas kernels, call(): pl.pallas_call(kernel, out_shape=[pltpu.VMEM(shape, jnp.float32) for shap...  18.4 us
    unnamed x12, local copies, waits for them, and re-layouts  2.96 us
  transfers between devices with their start and end apart: 20, of which 9 were waited for; matrix products, arithmetic and copies ran while one was open for 1% of the time, Pallas kernels for 14%

profile of v1, /device:TPU:0, one launch (start us, length us, event | category | flops | bytes accessed | tf_op | source)
XLA Modules:
  0.0 72.5 jit_solution(5228799960925917873)
XLA Ops:
  0.0 0.0 copy-start.1
  0.0 0.0 copy-start.2
  0.0 1.0 %dynamic-slice_bitcast_fusion = f32[2,32,1024]{2,1,0:T(8,128)S(1)} fusion(f32[1,2,128,1024]{3,2,1,0:T(8,128)} %param.5, s32[]{:T(128)S(6)} %select_n.5), kind=kLoop, calls=%fused_computation | loop fusion | bytes 524292 | tf_op jit(solution)/shard_map/dynamic_slice | solution.py:397
  1.0 0.0 copy-start.3
  1.0 0.5 collective-permute-start.3
  1.5 0.0 copy-done.1
  1.5 0.0 copy-done.2
  1.6 2.6 %collective-permute-start = (f32[4,1024]{1,0:T(4,128)S(1)}, f32[4,1024]{1,0:T(4,128)S(1)}, u32[]{:S(2)}, u32[]{:S(2)}) collective-permute-start(f32[4,1024]{1,0:T(4,128)S(1)} %pad_maximum_fusion.2), channel_id=1, source_target_pairs={{0,2},{2,0},{4,6},{6,4},{8,10},{10,8},{12,14},{14,12},{16,18},{18,... | collective-permute-start | bytes 49160 | tf_op jit(solution)/shard_map/ppermute | solution.py:392
  4.1 0.0 copy-done.3
  4.1 0.2 slice_reduce_fusion
  4.3 0.1 copy.7
  4.4 0.1 broadcast_divide_fusion.taps
  4.5 1.4 %collective-permute-done = f32[4,1024]{1,0:T(4,128)S(1)} collective-permute-done((f32[4,1024]{1,0:T(4,128)S(1)}, f32[4,1024]{1,0:T(4,128)S(1)}, u32[]{:S(2)}, u32[]{:S(2)}) %collective-permute-start) | collective-permute-done | bytes 16416 | tf_op jit(solution)/shard_map/ppermute | solution.py:392
  5.9 2.1 %collective-permute-start.1 = (f32[8,1024]{1,0:T(8,128)S(1)}, f32[8,1024]{1,0:T(8,128)S(1)}, u32[]{:S(2)}, u32[]{:S(2)}) collective-permute-start(f32[8,1024]{1,0:T(8,128)S(1)} %pad_maximum_fusion.1), channel_id=1, source_target_pairs={{0,4},{2,6},{4,0},{6,2},{8,12},{10,14},{12,8},{14,10},{16,20},{18,... | collective-permute-start | bytes 98312 | tf_op jit(solution)/shard_map/ppermute | solution.py:392
  8.0 0.0 copy-start.4
  8.0 0.7 copy-done.4
  8.6 0.1 pad_add_fusion.ints
  8.7 0.0 collective-permute-done.3.top_ref.bottom_ref
  8.7 0.0 copy-start
  8.7 1.2 %copy-done = f32[1,2,128,1024]{3,2,1,0:T(8,128)S(1)} copy-done((f32[1,2,128,1024]{3,2,1,0:T(8,128)S(1)}, f32[1,2,128,1024]{3,2,1,0:T(8,128)}, u32[]{:S(2)}) %copy-start) | copy-done | bytes 1048600
  10.0 1.8 %shard_map.55 = (f32[2,16,1024]{2,1,0:T(8,128)S(1)}, f32[2,16,1024]{2,1,0:T(8,128)S(1)}, f32[2,16,1024]{2,1,0:T(8,128)S(1)}, f32[2,16,1024]{2,1,0:T(8,128)S(1)},...) custom-call(s32[4]{0:T(128)S(1)} %pad_add_fusion.ints, ...), custom_call_target="tpu_custom_call" | custom-call | flops 1048576 | bytes 1048576 | tf_op jit(solution)/shard_map/pallas_call | solution.py:98
  11.8 2.5 %collective-permute-start.10 = (f32[2,16,1024]{2,1,0:T(8,128)S(1)}, f32[2,16,1024]{2,1,0:T(8,128)S(1)}, u32[]{:S(2)}, u32[]{:S(2)}) collective-permute-start(f32[2,16,1024]{2,1,0:T(8,128)S(1)} %get-tuple-element.33), channel_id=1, source_target_pairs={{0,14},{2,12},{4,10},{6,8},{8,6},{10,4},{12,2},{14,0},{16,30},{18,... | collective-permute-start | bytes 393224 | tf_op jit(solution)/shard_map/ppermute | solution.py:392
  14.3 0.5 collective-permute-start.4
  14.8 0.0 collective-permute-done.1
  14.9 0.2 collective-permute-start.2
  15.1 1.8 %collective-permute-start.5 = (f32[2,16,1024]{2,1,0:T(8,128)S(1)}, f32[2,16,1024]{2,1,0:T(8,128)S(1)}, u32[]{:S(2)}, u32[]{:S(2)}) collective-permute-start(f32[2,16,1024]{2,1,0:T(8,128)S(1)} %get-tuple-element.28), channel_id=1, source_target_pairs={{0,4},{2,6},{4,0},{6,2},{8,12},{10,14},{12,8},{14,10},{16,20},{18,... | collective-permute-start | bytes 393224 | tf_op jit(solution)/shard_map/ppermute | solution.py:392
  16.9 1.4 %collective-permute-start.6 = (f32[2,16,1024]{2,1,0:T(8,128)S(1)}, f32[2,16,1024]{2,1,0:T(8,128)S(1)}, u32[]{:S(2)}, u32[]{:S(2)}) collective-permute-start(f32[2,16,1024]{2,1,0:T(8,128)S(1)} %get-tuple-element.29), channel_id=1, source_target_pairs={{0,6},{2,4},{4,2},{6,0},{8,14},{10,12},{12,10},{14,8},{16,22},{18,... | collective-permute-start | bytes 393224 | tf_op jit(solution)/shard_map/ppermute | solution.py:392
  18.3 0.9 %collective-permute-done.2 = f32[16,1024]{1,0:T(8,128)S(1)} collective-permute-done((f32[16,1024]{1,0:T(8,128)S(1)}, f32[16,1024]{1,0:T(8,128)S(1)}, u32[]{:S(2)}, u32[]{:S(2)}) %collective-permute-start.2) | collective-permute-done | bytes 65568 | tf_op jit(solution)/shard_map/ppermute | solution.py:392
  19.2 1.1 %collective-permute-start.7 = (f32[2,16,1024]{2,1,0:T(8,128)S(1)}, f32[2,16,1024]{2,1,0:T(8,128)S(1)}, u32[]{:S(2)}, u32[]{:S(2)}) collective-permute-start(f32[2,16,1024]{2,1,0:T(8,128)S(1)} %get-tuple-element.30), channel_id=1, source_target_pairs={{0,8},{2,10},{4,12},{6,14},{8,0},{10,2},{12,4},{14,6},{16,24},{18,... | collective-permute-start | bytes 393224 | tf_op jit(solution)/shard_map/ppermute | solution.py:392
  20.2 0.0 collective-permute-done.10.rest_7_
  20.2 1.9 %collective-permute-start.8 = (f32[2,16,1024]{2,1,0:T(8,128)S(1)}, f32[2,16,1024]{2,1,0:T(8,128)S(1)}, u32[]{:S(2)}, u32[]{:S(2)}) collective-permute-start(f32[2,16,1024]{2,1,0:T(8,128)S(1)} %get-tuple-element.31), channel_id=1, source_target_pairs={{0,10},{2,8},{4,14},{6,12},{8,2},{10,0},{12,6},{14,4},{16,26},{18,... | collective-permute-start | bytes 393224 | tf_op jit(solution)/shard_map/ppermute | solution.py:392
  22.1 0.0 collective-permute-done.4.rest_1_
  22.1 1.4 %collective-permute-start.9 = (f32[2,16,1024]{2,1,0:T(8,128)S(1)}, f32[2,16,1024]{2,1,0:T(8,128)S(1)}, u32[]{:S(2)}, u32[]{:S(2)}) collective-permute-start(f32[2,16,1024]{2,1,0:T(8,128)S(1)} %get-tuple-element.32), channel_id=1, source_target_pairs={{0,12},{2,14},{4,8},{6,10},{8,4},{10,6},{12,0},{14,2},{16,28},{18,... | collective-permute-start | bytes 393224 | tf_op jit(solution)/shard_map/ppermute | solution.py:392
  23.6 0.0 collective-permute-done.5.rest_2_
  23.6 2.7 %collective-permute-start.12 = (f32[32,1024]{1,0:T(8,128)S(1)}, f32[32,1024]{1,0:T(8,128)S(1)}, u32[]{:S(2)}, u32[]{:S(2)}) collective-permute-start(f32[32,1024]{1,0:T(8,128)S(1)} %concatenate.18.roots), channel_id=1, source_target_pairs={{0,16},{2,18},{4,20},{6,22},{8,24},{10,26},{12,28},{14,30},{16,0},... | collective-permute-start | bytes 393224 | tf_op jit(solution)/shard_map/ppermute | solution.py:392
  26.3 0.0 collective-permute-done.6.rest_3_
  26.3 0.0 collective-permute-done.7.rest_4_
  26.3 3.6 %collective-permute-done.8.rest_5_ = f32[2,16,1024]{2,1,0:T(8,128)S(1)} collective-permute-done((f32[2,16,1024]{2,1,0:T(8,128)S(1)}, f32[2,16,1024]{2,1,0:T(8,128)S(1)}, u32[]{:S(2)}, u32[]{:S(2)}) %collective-permute-start.8) | collective-permute-done | bytes 131104 | tf_op jit(solution)/shard_map/ppermute | solution.py:392
  29.9 2.2 %collective-permute-done.9.rest_6_ = f32[2,16,1024]{2,1,0:T(8,128)S(1)} collective-permute-done((f32[2,16,1024]{2,1,0:T(8,128)S(1)}, f32[2,16,1024]{2,1,0:T(8,128)S(1)}, u32[]{:S(2)}, u32[]{:S(2)}) %collective-permute-start.9) | collective-permute-done | bytes 131104 | tf_op jit(solution)/shard_map/ppermute | solution.py:392
  32.1 7.9 %shard_map.56 = (f32[16,16,1024]{2,1,0:T(8,128)S(1)}, f32[2,16,1024]{2,1,0:T(8,128)S(1)}, f32[18,8,1024]{2,1,0:T(8,128)S(1)}, f32[18,8,1024]{2,1,0:T(8,128)S(1)}, f32[18,8,1024]{2,1,0:T(8,128)S(1)}) custom-call(s32[4]{0:T(128)S(1)} %pad_add_fusion.ints, f32[2,3]{1,0:T(2,128)S(1)} %broadcast_divide_fusion.taps, f32[32,1024]{1,0:T(8,128)S(1)} %concatenate.18.roots, ...), custom_call_target="tpu_custom_call" | custom-call | flops 1048576 | bytes 1048576 | tf_op jit(solution)/shard_map/pallas_call | solution.py:98
  40.0 1.3 %collective-permute-start.11 = (f32[2,16,1024]{2,1,0:T(8,128)S(1)}, f32[2,16,1024]{2,1,0:T(8,128)S(1)}, u32[]{:S(2)}, u32[]{:S(2)}) collective-permute-start(f32[2,16,1024]{2,1,0:T(8,128)S(1)} %get-tuple-element.35.message), channel_id=1, source_target_pairs={{0,16},{2,18},{4,20},{6,22},{8,24},{10,26},{12,28},{14,30},{16,0},... | collective-permute-start | bytes 393224 | tf_op jit(solution)/shard_map/ppermute | solution.py:392
  41.2 0.0 collective-permute-done.12.roots
  41.2 0.6 shard_map.57.state
  41.8 5.5 %collective-permute-done.11.received = f32[2,16,1024]{2,1,0:T(8,128)S(1)} collective-permute-done((f32[2,16,1024]{2,1,0:T(8,128)S(1)}, f32[2,16,1024]{2,1,0:T(8,128)S(1)}, u32[]{:S(2)}, u32[]{:S(2)}) %collective-permute-start.11) | collective-permute-done | bytes 131104 | tf_op jit(solution)/shard_map/ppermute | solution.py:392
  47.3 7.5 %shard_map.58 = (f32[2,16,1024]{2,1,0:T(8,128)S(1)}, f32[2,16,1024]{2,1,0:T(8,128)S(1)}, f32[2,16,1024]{2,1,0:T(8,128)S(1)}, f32[2,16,1024]{2,1,0:T(8,128)S(1)},...) custom-call(s32[4]{0:T(128)S(1)} %pad_add_fusion.ints, ...), custom_call_target="tpu_custom_call" | custom-call | flops 1048576 | bytes 1048576 | tf_op jit(solution)/shard_map/pallas_call | solution.py:98
  54.8 0.4 collective-permute-start.13
  55.2 0.9 %collective-permute-start.14 = (f32[2,16,1024]{2,1,0:T(8,128)S(1)}, f32[2,16,1024]{2,1,0:T(8,128)S(1)}, u32[]{:S(2)}, u32[]{:S(2)}) collective-permute-start(f32[2,16,1024]{2,1,0:T(8,128)S(1)} %get-tuple-element.41), channel_id=1, source_target_pairs={{0,4},{2,6},{4,0},{6,2},{8,12},{10,14},{12,8},{14,10},{16,20},{18,... | collective-permute-start | bytes 393224 | tf_op jit(solution)/shard_map/ppermute | solution.py:392
  56.1 2.2 %collective-permute-start.15 = (f32[2,16,1024]{2,1,0:T(8,128)S(1)}, f32[2,16,1024]{2,1,0:T(8,128)S(1)}, u32[]{:S(2)}, u32[]{:S(2)}) collective-permute-start(f32[2,16,1024]{2,1,0:T(8,128)S(1)} %get-tuple-element.42), channel_id=1, source_target_pairs={{0,6},{2,4},{4,2},{6,0},{8,14},{10,12},{12,10},{14,8},{16,22},{18,... | collective-permute-start | bytes 393224 | tf_op jit(solution)/shard_map/ppermute | solution.py:392
  58.4 0.0 collective-permute-start.16
  58.4 1.8 %collective-permute-start.17 = (f32[2,16,1024]{2,1,0:T(8,128)S(1)}, f32[2,16,1024]{2,1,0:T(8,128)S(1)}, u32[]{:S(2)}, u32[]{:S(2)}) collective-permute-start(f32[2,16,1024]{2,1,0:T(8,128)S(1)} %get-tuple-element.44), channel_id=1, source_target_pairs={{0,10},{2,8},{4,14},{6,12},{8,2},{10,0},{12,6},{14,4},{16,26},{18,... | collective-permute-start | bytes 393224 | tf_op jit(solution)/shard_map/ppermute | solution.py:392
  60.1 0.2 collective-permute-done.13.rest_1_
  60.3 0.6 collective-permute-start.18
  60.9 3.2 %collective-permute-done.14.rest_2_ = f32[2,16,1024]{2,1,0:T(8,128)S(1)} collective-permute-done((f32[2,16,1024]{2,1,0:T(8,128)S(1)}, f32[2,16,1024]{2,1,0:T(8,128)S(1)}, u32[]{:S(2)}, u32[]{:S(2)}) %collective-permute-start.14) | collective-permute-done | bytes 131104 | tf_op jit(solution)/shard_map/ppermute | solution.py:392
  64.1 1.1 %collective-permute-start.19 = (f32[2,16,1024]{2,1,0:T(8,128)S(1)}, f32[2,16,1024]{2,1,0:T(8,128)S(1)}, u32[]{:S(2)}, u32[]{:S(2)}) collective-permute-start(f32[2,16,1024]{2,1,0:T(8,128)S(1)} %get-tuple-element.46), channel_id=1, source_target_pairs={{0,14},{2,12},{4,10},{6,8},{8,6},{10,4},{12,2},{14,0},{16,30},{18,... | collective-permute-start | bytes 393224 | tf_op jit(solution)/shard_map/ppermute | solution.py:392
  65.2 0.0 collective-permute-done.15.rest_3_
  65.2 0.0 collective-permute-done.16.rest_4_
  65.2 0.0 collective-permute-done.17.rest_5_
  65.2 1.0 %collective-permute-done.18.rest_6_ = f32[2,16,1024]{2,1,0:T(8,128)S(1)} collective-permute-done((f32[2,16,1024]{2,1,0:T(8,128)S(1)}, f32[2,16,1024]{2,1,0:T(8,128)S(1)}, u32[]{:S(2)}, u32[]{:S(2)}) %collective-permute-start.18) | collective-permute-done | bytes 131104 | tf_op jit(solution)/shard_map/ppermute | solution.py:392
  66.2 4.7 %collective-permute-done.19.rest_7_ = f32[2,16,1024]{2,1,0:T(8,128)S(1)} collective-permute-done((f32[2,16,1024]{2,1,0:T(8,128)S(1)}, f32[2,16,1024]{2,1,0:T(8,128)S(1)}, u32[]{:S(2)}, u32[]{:S(2)}) %collective-permute-start.19) | collective-permute-done | bytes 131104 | tf_op jit(solution)/shard_map/ppermute | solution.py:392
  70.9 0.6 shard_map.59
  71.5 1.0 %copy.8 = f32[1,2,128,1024]{3,2,1,0:T(8,128)} copy(f32[1,2,128,1024]{3,2,1,0:T(8,128)S(1)} %bitcast.13) | data formatting | bytes 2097152
  (5 shorter events, 0.1 us)
Async XLA Ops:
  0.0 1.5 %copy-start.1 = (f32[2,1024]{1,0:T(2,128)S(1)}, f32[2,1024]{1,0:T(2,128)}, u32[]{:S(2)}) copy-start(f32[2,1024]{1,0:T(2,128)} %param.6) | copy-start | bytes 24580
  0.0 1.5 %copy-start.2 = (f32[2,1024]{1,0:T(2,128)S(1)}, f32[2,1024]{1,0:T(2,128)}, u32[]{:S(2)}) copy-start(f32[2,1024]{1,0:T(2,128)} %param.7) | copy-start | bytes 24580
  1.0 3.1 %copy-start.3 = (f32[2,3]{1,0:T(2,128)S(1)}, f32[2,3]{1,0:T(2,128)}, u32[]{:S(2)}) copy-start(f32[2,3]{1,0:T(2,128)} %param.8) | copy-start | bytes 76
  1.0 7.7 %collective-permute-start.3 = (f32[2,32,1024]{2,1,0:T(8,128)S(1)}, f32[2,32,1024]{2,1,0:T(8,128)S(1)}, u32[]{:S(2)}, u32[]{:S(2)}) collective-permute-start(f32[2,32,1024]{2,1,0:T(8,128)S(1)} %dynamic-slice_bitcast_fusion), channel_id=1, source_target_pairs={{0,1},{1,0},{2,3},{3,2},{4,5},{5,4},{6,7},{7,6},{8,9},{9,8},{10,11... | collective-permute-start | bytes 786440 | tf_op jit(solution)/shard_map/ppermute | solution.py:398
  1.6 4.3 %collective-permute-start = (f32[4,1024]{1,0:T(4,128)S(1)}, f32[4,1024]{1,0:T(4,128)S(1)}, u32[]{:S(2)}, u32[]{:S(2)}) collective-permute-start(f32[4,1024]{1,0:T(4,128)S(1)} %pad_maximum_fusion.2), channel_id=1, source_target_pairs={{0,2},{2,0},{4,6},{6,4},{8,10},{10,8},{12,14},{14,12},{16,18},{18,... | collective-permute-start | bytes 49160 | tf_op jit(solution)/shard_map/ppermute | solution.py:392
  5.9 8.9 %collective-permute-start.1 = (f32[8,1024]{1,0:T(8,128)S(1)}, f32[8,1024]{1,0:T(8,128)S(1)}, u32[]{:S(2)}, u32[]{:S(2)}) collective-permute-start(f32[8,1024]{1,0:T(8,128)S(1)} %pad_maximum_fusion.1), channel_id=1, source_target_pairs={{0,4},{2,6},{4,0},{6,2},{8,12},{10,14},{12,8},{14,10},{16,20},{18,... | collective-permute-start | bytes 98312 | tf_op jit(solution)/shard_map/ppermute | solution.py:392
  8.0 0.7 copy-start.4
  8.7 1.2 %copy-start = (f32[1,2,128,1024]{3,2,1,0:T(8,128)S(1)}, f32[1,2,128,1024]{3,2,1,0:T(8,128)}, u32[]{:S(2)}) copy-start(f32[1,2,128,1024]{3,2,1,0:T(8,128)} %param.5) | copy-start | bytes 3145732
  11.8 8.5 %collective-permute-start.10 = (f32[2,16,1024]{2,1,0:T(8,128)S(1)}, f32[2,16,1024]{2,1,0:T(8,128)S(1)}, u32[]{:S(2)}, u32[]{:S(2)}) collective-permute-start(f32[2,16,1024]{2,1,0:T(8,128)S(1)} %get-tuple-element.33), channel_id=1, source_target_pairs={{0,14},{2,12},{4,10},{6,8},{8,6},{10,4},{12,2},{14,0},{16,30},{18,... | collective-permute-start | bytes 393224 | tf_op jit(solution)/shard_map/ppermute | solution.py:392
  14.3 7.9 %collective-permute-start.4 = (f32[2,16,1024]{2,1,0:T(8,128)S(1)}, f32[2,16,1024]{2,1,0:T(8,128)S(1)}, u32[]{:S(2)}, u32[]{:S(2)}) collective-permute-start(f32[2,16,1024]{2,1,0:T(8,128)S(1)} %get-tuple-element.27), channel_id=1, source_target_pairs={{0,2},{2,0},{4,6},{6,4},{8,10},{10,8},{12,14},{14,12},{16,18},{18,... | collective-permute-start | bytes 393224 | tf_op jit(solution)/shard_map/ppermute | solution.py:392
  14.9 4.3 %collective-permute-start.2 = (f32[16,1024]{1,0:T(8,128)S(1)}, f32[16,1024]{1,0:T(8,128)S(1)}, u32[]{:S(2)}, u32[]{:S(2)}) collective-permute-start(f32[16,1024]{1,0:T(8,128)S(1)} %pad_maximum_fusion), channel_id=1, source_target_pairs={{0,8},{2,10},{4,12},{6,14},{8,0},{10,2},{12,4},{14,6},{16,24},{18,... | collective-permute-start | bytes 196616 | tf_op jit(solution)/shard_map/ppermute | solution.py:392
  15.1 8.5 %collective-permute-start.5 = (f32[2,16,1024]{2,1,0:T(8,128)S(1)}, f32[2,16,1024]{2,1,0:T(8,128)S(1)}, u32[]{:S(2)}, u32[]{:S(2)}) collective-permute-start(f32[2,16,1024]{2,1,0:T(8,128)S(1)} %get-tuple-element.28), channel_id=1, source_target_pairs={{0,4},{2,6},{4,0},{6,2},{8,12},{10,14},{12,8},{14,10},{16,20},{18,... | collective-permute-start | bytes 393224 | tf_op jit(solution)/shard_map/ppermute | solution.py:392
  16.9 9.4 %collective-permute-start.6 = (f32[2,16,1024]{2,1,0:T(8,128)S(1)}, f32[2,16,1024]{2,1,0:T(8,128)S(1)}, u32[]{:S(2)}, u32[]{:S(2)}) collective-permute-start(f32[2,16,1024]{2,1,0:T(8,128)S(1)} %get-tuple-element.29), channel_id=1, source_target_pairs={{0,6},{2,4},{4,2},{6,0},{8,14},{10,12},{12,10},{14,8},{16,22},{18,... | collective-permute-start | bytes 393224 | tf_op jit(solution)/shard_map/ppermute | solution.py:392
  19.2 7.1 %collective-permute-start.7 = (f32[2,16,1024]{2,1,0:T(8,128)S(1)}, f32[2,16,1024]{2,1,0:T(8,128)S(1)}, u32[]{:S(2)}, u32[]{:S(2)}) collective-permute-start(f32[2,16,1024]{2,1,0:T(8,128)S(1)} %get-tuple-element.30), channel_id=1, source_target_pairs={{0,8},{2,10},{4,12},{6,14},{8,0},{10,2},{12,4},{14,6},{16,24},{18,... | collective-permute-start | bytes 393224 | tf_op jit(solution)/shard_map/ppermute | solution.py:392
  20.2 9.6 %collective-permute-start.8 = (f32[2,16,1024]{2,1,0:T(8,128)S(1)}, f32[2,16,1024]{2,1,0:T(8,128)S(1)}, u32[]{:S(2)}, u32[]{:S(2)}) collective-permute-start(f32[2,16,1024]{2,1,0:T(8,128)S(1)} %get-tuple-element.31), channel_id=1, source_target_pairs={{0,10},{2,8},{4,14},{6,12},{8,2},{10,0},{12,6},{14,4},{16,26},{18,... | collective-permute-start | bytes 393224 | tf_op jit(solution)/shard_map/ppermute | solution.py:392
  22.1 9.9 %collective-permute-start.9 = (f32[2,16,1024]{2,1,0:T(8,128)S(1)}, f32[2,16,1024]{2,1,0:T(8,128)S(1)}, u32[]{:S(2)}, u32[]{:S(2)}) collective-permute-start(f32[2,16,1024]{2,1,0:T(8,128)S(1)} %get-tuple-element.32), channel_id=1, source_target_pairs={{0,12},{2,14},{4,8},{6,10},{8,4},{10,6},{12,0},{14,2},{16,28},{18,... | collective-permute-start | bytes 393224 | tf_op jit(solution)/shard_map/ppermute | solution.py:392
  23.6 17.6 %collective-permute-start.12 = (f32[32,1024]{1,0:T(8,128)S(1)}, f32[32,1024]{1,0:T(8,128)S(1)}, u32[]{:S(2)}, u32[]{:S(2)}) collective-permute-start(f32[32,1024]{1,0:T(8,128)S(1)} %concatenate.18.roots), channel_id=1, source_target_pairs={{0,16},{2,18},{4,20},{6,22},{8,24},{10,26},{12,28},{14,30},{16,0},... | collective-permute-start | bytes 393224 | tf_op jit(solution)/shard_map/ppermute | solution.py:392
  40.0 7.3 %collective-permute-start.11 = (f32[2,16,1024]{2,1,0:T(8,128)S(1)}, f32[2,16,1024]{2,1,0:T(8,128)S(1)}, u32[]{:S(2)}, u32[]{:S(2)}) collective-permute-start(f32[2,16,1024]{2,1,0:T(8,128)S(1)} %get-tuple-element.35.message), channel_id=1, source_target_pairs={{0,16},{2,18},{4,20},{6,22},{8,24},{10,26},{12,28},{14,30},{16,0},... | collective-permute-start | bytes 393224 | tf_op jit(solution)/shard_map/ppermute | solution.py:392
  54.8 5.5 %collective-permute-start.13 = (f32[2,16,1024]{2,1,0:T(8,128)S(1)}, f32[2,16,1024]{2,1,0:T(8,128)S(1)}, u32[]{:S(2)}, u32[]{:S(2)}) collective-permute-start(f32[2,16,1024]{2,1,0:T(8,128)S(1)} %get-tuple-element.40), channel_id=1, source_target_pairs={{0,2},{2,0},{4,6},{6,4},{8,10},{10,8},{12,14},{14,12},{16,18},{18,... | collective-permute-start | bytes 393224 | tf_op jit(solution)/shard_map/ppermute | solution.py:392
  55.2 8.9 %collective-permute-start.14 = (f32[2,16,1024]{2,1,0:T(8,128)S(1)}, f32[2,16,1024]{2,1,0:T(8,128)S(1)}, u32[]{:S(2)}, u32[]{:S(2)}) collective-permute-start(f32[2,16,1024]{2,1,0:T(8,128)S(1)} %get-tuple-element.41), channel_id=1, source_target_pairs={{0,4},{2,6},{4,0},{6,2},{8,12},{10,14},{12,8},{14,10},{16,20},{18,... | collective-permute-start | bytes 393224 | tf_op jit(solution)/shard_map/ppermute | solution.py:392
  56.1 9.1 %collective-permute-start.15 = (f32[2,16,1024]{2,1,0:T(8,128)S(1)}, f32[2,16,1024]{2,1,0:T(8,128)S(1)}, u32[]{:S(2)}, u32[]{:S(2)}) collective-permute-start(f32[2,16,1024]{2,1,0:T(8,128)S(1)} %get-tuple-element.42), channel_id=1, source_target_pairs={{0,6},{2,4},{4,2},{6,0},{8,14},{10,12},{12,10},{14,8},{16,22},{18,... | collective-permute-start | bytes 393224 | tf_op jit(solution)/shard_map/ppermute | solution.py:392
  58.4 6.9 %collective-permute-start.16 = (f32[2,16,1024]{2,1,0:T(8,128)S(1)}, f32[2,16,1024]{2,1,0:T(8,128)S(1)}, u32[]{:S(2)}, u32[]{:S(2)}) collective-permute-start(f32[2,16,1024]{2,1,0:T(8,128)S(1)} %get-tuple-element.43), channel_id=1, source_target_pairs={{0,8},{2,10},{4,12},{6,14},{8,0},{10,2},{12,4},{14,6},{16,24},{18,... | collective-permute-start | bytes 393224 | tf_op jit(solution)/shard_map/ppermute | solution.py:392
  58.4 6.9 %collective-permute-start.17 = (f32[2,16,1024]{2,1,0:T(8,128)S(1)}, f32[2,16,1024]{2,1,0:T(8,128)S(1)}, u32[]{:S(2)}, u32[]{:S(2)}) collective-permute-start(f32[2,16,1024]{2,1,0:T(8,128)S(1)} %get-tuple-element.44), channel_id=1, source_target_pairs={{0,10},{2,8},{4,14},{6,12},{8,2},{10,0},{12,6},{14,4},{16,26},{18,... | collective-permute-start | bytes 393224 | tf_op jit(solution)/shard_map/ppermute | solution.py:392
  60.3 5.9 %collective-permute-start.18 = (f32[2,16,1024]{2,1,0:T(8,128)S(1)}, f32[2,16,1024]{2,1,0:T(8,128)S(1)}, u32[]{:S(2)}, u32[]{:S(2)}) collective-permute-start(f32[2,16,1024]{2,1,0:T(8,128)S(1)} %get-tuple-element.45), channel_id=1, source_target_pairs={{0,12},{2,14},{4,8},{6,10},{8,4},{10,6},{12,0},{14,2},{16,28},{18,... | collective-permute-start | bytes 393224 | tf_op jit(solution)/shard_map/ppermute | solution.py:392
  64.1 6.8 %collective-permute-start.19 = (f32[2,16,1024]{2,1,0:T(8,128)S(1)}, f32[2,16,1024]{2,1,0:T(8,128)S(1)}, u32[]{:S(2)}, u32[]{:S(2)}) collective-permute-start(f32[2,16,1024]{2,1,0:T(8,128)S(1)} %get-tuple-element.46), channel_id=1, source_target_pairs={{0,14},{2,12},{4,10},{6,8},{8,6},{10,4},{12,2},{14,0},{16,30},{18,... | collective-permute-start | bytes 393224 | tf_op jit(solution)/shard_map/ppermute | solution.py:392

commit v2 on v0

v2 whole, which is shorter than its diff:
```python
import functools

import jax
import jax.numpy as jnp
from jax import lax
from jax.experimental import pallas as pl
from jax.experimental.pallas import tpu as pltpu
from jax.sharding import PartitionSpec as P

RADIUS = 2
DMAX = 8
MARGIN = RADIUS * DMAX
LANES = 128
SUB = 8


def padded_y(array, width):
    size, length = lax.axis_size("gy"), array.shape[2]
    up = [(i, (i + 1) % size) for i in range(size - 1)]
    down = [(j, i) for i, j in up]
    last = lax.slice_in_dim(array, length - width, length, axis=2)
    leading = lax.slice_in_dim(array, 0, width, axis=2)
    before = lax.ppermute(last, "gy", up)
    after = lax.ppermute(leading, "gy", down)
    return jnp.concatenate([before, array, after], axis=2)


def filter_coefficients(root_one, root_two):
    first = root_one + root_two
    second = -root_one * root_two
    gain = (1.0 - root_one) * (1.0 - root_two)
    return (first, second, gain)


def depth_scan(fields, first, second, pre_gain, post_gain, reverse):
    moved = jnp.moveaxis(fields, 1, 0)
    zero = jnp.zeros(moved.shape[1:], jnp.float32)

    def advance(carry, inputs):
        latest, earlier = carry
        plane, coef_one, coef_two, before, after = inputs
        value = before * plane + coef_one * latest + coef_two * earlier
        return ((value, latest), after * value)

    _, outputs = lax.scan(
        advance, (zero, zero), (moved, first, second, pre_gain, post_gain), reverse=reverse
    )
    return jnp.moveaxis(outputs, 0, 1)


def normalised(weights):
    return weights / (weights[..., :1] + 2.0 * jnp.sum(weights[..., 1:], -1, keepdims=True))


def lateral_padded(padded, scaled, dilation, axis, margin, length):
    result = scaled[0] * lax.dynamic_slice_in_dim(padded, margin, length, axis)
    for offset_tap in range(1, scaled.shape[0]):
        offset = dilation * offset_tap
        upper = lax.dynamic_slice_in_dim(padded, margin + offset, length, axis)
        lower = lax.dynamic_slice_in_dim(padded, margin - offset, length, axis)
        result = result + scaled[offset_tap] * (upper + lower)
    return result


def lateral_x(fields, scaled, dilation):
    padded = jnp.pad(fields, ((0, 0), (0, 0), (0, 0), (MARGIN, MARGIN)))
    return lateral_padded(padded, scaled, dilation, 3, MARGIN, fields.shape[3])


def lateral_y_twice(fields, scaled, dilation):
    rows = fields.shape[2]
    padded = padded_y(fields, 2 * MARGIN)
    middle = lateral_padded(padded, scaled, dilation, 2, MARGIN, rows + 2 * MARGIN)
    global_row = lax.axis_index("gy") * rows - MARGIN + jnp.arange(rows + 2 * MARGIN)
    inside = (global_row >= 0) & (global_row < rows * lax.axis_size("gy"))
    middle = jnp.where(inside[None, None, :, None], middle, 0.0)
    return lateral_padded(middle, scaled, dilation, 2, MARGIN, rows)


def plain_body(probe_fields, root_one, root_two, lateral_kernel_taps, dilations):
    roots = lax.all_gather(jnp.stack([root_one, root_two], 1), "gz", axis=0, tiled=True)
    first, second, gain = filter_coefficients(roots[:, 0], roots[:, 1])
    unity = jnp.ones_like(gain)
    first_next = jnp.concatenate([first[1:], jnp.zeros_like(first[:1])], 0)
    second_next = jnp.concatenate([second[2:], jnp.zeros_like(second[:2])], 0)
    scaled = normalised(lateral_kernel_taps)
    field = lateral_y_twice(probe_fields, scaled[1], dilations[1])
    field = lax.all_to_all(field, "gz", split_axis=2, concat_axis=1, tiled=True)
    field = depth_scan(field, first_next, second_next, unity, gain, True)
    field = lateral_x(field, scaled[0], dilations[0])
    field = lateral_x(field, scaled[0], dilations[0])
    field = depth_scan(field, first, second, gain, unity, False)
    return lax.all_to_all(field, "gz", split_axis=1, concat_axis=2, tiled=True)


def call(kernel, outs, scratch, scalars, arrays, cost):
    arrays = [pltpu.with_memory_space_constraint(a, pltpu.VMEM) for a in arrays]
    outs = [out if len(out) == 2 else (out, jnp.float32) for out in outs]
    return pl.pallas_call(
        kernel,
        out_shape=[pltpu.VMEM(shape, dtype) for shape, dtype in outs],
        in_specs=[pl.BlockSpec(memory_space=pltpu.SMEM)] * len(scalars)
        + [pl.BlockSpec(memory_space=pltpu.VMEM)] * len(arrays),
        out_specs=[pl.BlockSpec(memory_space=pltpu.VMEM)] * len(outs),
        scratch_shapes=[pltpu.VMEM(shape, jnp.float32) for shape in scratch],
        compiler_params=pltpu.CompilerParams(vmem_limit_bytes=24 << 20),
        cost_estimate=pl.CostEstimate(flops=cost, bytes_accessed=1 << 16, transcendentals=0),
    )(*scalars, *arrays)


def tap_vectors(taps, axis, shape):
    raw = [taps[axis, i] for i in range(RADIUS + 1)]
    total = raw[0] + 2.0 * functools.reduce(lambda a, b: a + b, raw[1:])
    scale = 1.0 / jnp.full(shape, total, jnp.float32)
    return [jnp.full(shape, tap, jnp.float32) * scale for tap in raw]


def split(value):
    high = value.astype(jnp.bfloat16)
    return high, (value - high.astype(jnp.float32)).astype(jnp.bfloat16)


def product(left, right):
    dot = functools.partial(jnp.dot, preferred_element_type=jnp.float32)
    return dot(left[0], right[0]) + (dot(left[0], right[1]) + dot(left[1], right[0]))


OFFSETS = range(-RADIUS, RADIUS + 1)


def double_taps(at, length, step, taps):
    sums = {}
    for a in OFFSETS:
        middle = at + a * step
        tap = jnp.where((middle >= 0) & (middle < length), taps[abs(a)], 0.0)
        for b in OFFSETS:
            sums[a + b] = sums.get(a + b, 0.0) + tap * taps[abs(b)]
    return sums


def fill_band(high, low, row_places, step, taps, begin, from_begin):
    part = 2 * SUB
    for i in range(0, high.shape[0], part):
        shape = (part, high.shape[1])
        at = lax.broadcasted_iota(jnp.int32, shape, 0) + (begin + i)
        apart = lax.broadcasted_iota(jnp.int32, shape, 1) + from_begin - at
        value = jnp.zeros(shape, jnp.float32)
        for o, total in double_taps(at, row_places, step, taps).items():
            value = jnp.where(apart == o * step, total, value)
        high[i : i + part], low[i : i + part] = split(value)


def load_kernel(
    x_ref, one_ref, two_ref, dilations_ref, taps_ref,
    whole, edge, roots, high, low, edge_high, edge_low, one, two, dilations, taps, sems,
):
    row_at, row_places = lax.axis_index("gy"), lax.axis_size("gy")
    planes, tiles = x_ref.shape[:2]
    depth, blocks = edge.shape[1:3]
    rows = tiles * SUB
    start = jnp.where(row_at == 0, tiles - depth, 0)
    copies = [
        pltpu.make_async_copy(x_ref.at[:, pl.ds(start, depth)], edge, sems.at[0]),
        pltpu.make_async_copy(one_ref, one, sems.at[1]),
        pltpu.make_async_copy(two_ref, two, sems.at[2]),
        pltpu.make_async_copy(dilations_ref, dilations, sems.at[3]),
        pltpu.make_async_copy(taps_ref, taps, sems.at[4]),
    ]
    copies += [
        pltpu.make_async_copy(x_ref.at[p], whole.at[p], sems.at[5 + p]) for p in range(planes)
    ]
    for copy in copies:
        copy.start()
    for copy in copies[1:5]:
        copy.wait()
    for p in range(planes):
        for b in range(blocks):
            lanes = slice(b * LANES, (b + 1) * LANES)
            roots[p, b : b + 1] = one[p : p + 1, lanes]
            roots[planes + p, b : b + 1] = two[p : p + 1, lanes]
    step, weights = dilations[1], tap_vectors(taps, 1, (1, 1))
    length, begin = rows * row_places, row_at * rows
    fill_band(high, low, length, step, weights, begin, begin)
    near = begin + jnp.where(row_at == 0, rows - 2 * MARGIN, 0)
    beyond = begin + jnp.where(row_at == 0, rows, -2 * MARGIN)
    fill_band(edge_high, edge_low, length, step, weights, near, beyond)
    copies[0].wait()
    for copy in copies[5:]:
        copy.wait()


def columns_of(ref, p, b, width):
    rows = ref.shape[1] * SUB
    return jnp.concatenate([ref[p, :, b + i].reshape(rows, LANES) for i in range(width)], axis=1)


def y_inner_kernel(groups, high, low, x_ref, pieces):
    planes, tiles, blocks = x_ref.shape[:3]
    chunks, width = tiles // groups, 2
    for p in range(planes):
        for b in range(0, blocks, width):
            value = product((high[...], low[...]), split(columns_of(x_ref, p, b, width)))
            for i in range(tiles):
                for w in range(width):
                    tile = value[i * SUB : (i + 1) * SUB, w * LANES : (w + 1) * LANES]
                    pieces[i // chunks, (p * chunks + i % chunks) * blocks + b + w] = tile


def y_outer_kernel(groups, tiles, high, low, edge, roots, other_roots, given, pieces):
    planes, halo, blocks = edge.shape[:3]
    chunks, width = tiles // groups, 2
    base = chunks * planes * blocks
    pieces[:, :base] = given[...]
    first = jnp.where(lax.axis_index("gy") == 0, (tiles - halo) // chunks, 0)
    for p in range(planes):
        for b in range(0, blocks, width):
            value = product((high[...], low[...]), split(columns_of(edge, p, b, width)))
            for i in range(halo):
                for w in range(width):
                    tile = value[i * SUB : (i + 1) * SUB, w * LANES : (w + 1) * LANES]
                    to, at = first + i // chunks, (p * chunks + i % chunks) * blocks
                    pieces[to, at + b + w] = given[to, at + b + w] + tile
    for i in range(groups):
        for r in range(2 * planes):
            pieces[i, base + r] = roots[r]
            pieces[i, base + 2 * planes + r] = other_roots[r]


def band_kernel(columns, dilations, taps, high, low):
    count, depth, width = high.shape
    step, taps = dilations[0], tap_vectors(taps, 0, (1, width))
    part = 2 * SUB
    lane = lax.broadcasted_iota(jnp.int32, (part, width), 1)
    row = lax.broadcasted_iota(jnp.int32, (part, width), 0)
    for n in range(count):
        at = lax.broadcasted_iota(jnp.int32, (1, width), 1) + n * width
        sums = double_taps(at, columns, step, taps)

        def rows_at(i, _):
            apart = row + (i * part - LANES) - lane
            value = jnp.zeros((part, width), jnp.float32)
            for o, total in sums.items():
                value = jnp.where(apart == o * step, total, value)
            at_rows = pl.ds(pl.multiple_of(i * part, part), part)
            high[n, at_rows], low[n, at_rows] = split(value)
            return 0

        lax.fori_loop(0, depth // part, rows_at, 0)


def x_twice(source, result, high, low):
    for n in range(high.shape[0]):
        depth, width = high.shape[1:]
        value = split(source[:, n * width : n * width + depth])
        result[:, n * width : (n + 1) * width] = product(value, (high[n], low[n]))


def add(a, b):
    return [x + y for x, y in zip(a, b)]


def times(ref, k, values):
    return [ref[k, b : b + 1] * value for b, value in enumerate(values)]


def tiles_of(ref, *at):
    return [ref[(*at, b)] for b in range(ref.shape[len(at)])]


def put(ref, values, *at):
    for b, value in enumerate(values):
        ref[(*at, b)] = value


def clear_sides(field):
    columns = field.shape[1] - 2 * LANES
    none = jnp.zeros((field.shape[0], LANES), jnp.float32)
    field[:, :LANES] = none
    field[:, LANES + columns :] = none


def row_tile(k):
    return pl.ds(pl.multiple_of(k * SUB, SUB), SUB)


def filter_back(count, planes, source, coefficients, field, start):
    first, second, gain = coefficients
    after, beyond = start

    def at(d, carry):
        for p in reversed(range(planes)):
            ahead, pending = carry
            k = d * planes + p
            value = ahead if source is None else add(source(d, p), ahead)
            for b, scaled in enumerate(times(gain, k, value)):
                field[row_tile(k), (b + 1) * LANES : (b + 2) * LANES] = scaled
            carry = (add(times(first, k, value), pending), times(second, k, value))
        return carry

    steps = count // planes
    return lax.fori_loop(0, steps, lambda i, c: at(steps - 1 - i, c), (after, beyond))


def filter_forth(count, planes, field, coefficients, start, finish):
    first, second, gain = coefficients

    def at(d, carry):
        for p in range(planes):
            latest, earlier = carry
            k = d * planes + p
            value = add(times(first, k, latest), times(second, k, earlier))
            if field is not None:
                blocks = len(value)
                there = [
                    field[row_tile(k), b * LANES : (b + 1) * LANES] for b in range(blocks)
                ]
                value = add(value, times(gain, k, there))
            finish(d, p, value)
            carry = (value, latest)
        return carry

    return lax.fori_loop(0, count // planes, at, start)


def store_coefficients(k, one, two, first, second, gain):
    first[k] = one + two
    second[k] = -one * two
    gain[k] = (1.0 - one) * (1.0 - two)


def local_kernel(groups, planes, chunks, chunk, *refs):
    if chunk == 0:
        pieces, high, low, local, message, *coefficients, field, middle = refs
    else:
        pieces, high, low, *coefficients, local, message, field, middle = refs
    half = lax.axis_index("gz") // groups
    blocks = message.shape[1]
    count = groups * planes
    own = coefficients[:3]
    if chunk == 0:
        base = chunks * planes * blocks
        for d in range(groups):
            for p in range(planes):
                k = d * planes + p
                one, two = (pieces[d, base + i * planes + p] for i in range(2))
                store_coefficients(k, one, two, *own)
                other_one, other_two = (pieces[d, base + (2 + i) * planes + p] for i in range(2))
                one = jnp.where(half == 0, one, other_one)
                two = jnp.where(half == 0, two, other_two)
                store_coefficients(k, one, two, *coefficients[3:])
    clear_sides(field)
    zeros = [field[0:SUB, 0:LANES]] * blocks

    def source(d, p):
        return [pieces[d, (p * chunks + chunk) * blocks + b] for b in range(blocks)]

    ahead, pending = filter_back(count, planes, source, own, field, (zeros, zeros))
    x_twice(field, middle, high, low)

    def finish(d, p, value):
        for b, v in enumerate(value):
            local[d, p * blocks + b] = v

    latest, earlier = filter_forth(count, planes, middle, own, (zeros, zeros), finish)
    for b in range(blocks):
        message[0, b] = jnp.where(half > 0, ahead[b], latest[b])
        message[1, b] = jnp.where(half > 0, pending[b], earlier[b])


def join_kernel(groups, planes, chunks, chunk, local, sent, received, high, low, *refs):
    own, lower, before = refs[:3], refs[3:6], refs[6:-4]
    out, carried, field, middle = refs[-4:]
    half = lax.axis_index("gz") // groups
    blocks = sent.shape[1]
    count = groups * planes
    for ref in before:
        out[...] = ref[...]
    for i in range(2):
        for b in range(blocks):
            carried[i, b] = jnp.where(half == 0, received[i, b], sent[i, b])
    clear_sides(field)
    zeros = [field[0:SUB, 0:LANES]] * blocks
    start = (tiles_of(carried, 0), tiles_of(carried, 1))
    filter_back(count, planes, None, lower, field, start)
    x_twice(field, middle, high, low)

    def finish(d, p, value):
        for b, v in enumerate(value):
            out[d, (p * chunks + chunk) * blocks + b] = v + local[d, p * blocks + b]

    latest, earlier = filter_forth(count, planes, middle, lower, (zeros, zeros), finish)
    put(carried, latest, 0)
    put(carried, earlier, 1)

    @pl.when(half > 0)
    def _():
        begin = (
            add(tiles_of(carried, 0), tiles_of(received, 0)),
            add(tiles_of(carried, 1), tiles_of(received, 1)),
        )
        filter_forth(count, planes, None, own, begin, finish)


def place_kernel(pieces, out, sem):
    groups, planes = pieces.shape[0], out.shape[0]
    each = pieces.shape[1] // planes
    for i in range(groups):
        for p in range(planes):
            pltpu.make_async_copy(
                pieces.at[i, pl.ds(p * each, each)], out.at[p, pl.ds(i * each, each)], sem
            ).start()
    pltpu.make_async_copy(out, out, sem).wait()


def grouped_body(probe_fields, root_one, root_two, lateral_kernel_taps, dilations):
    _, planes, rows, columns = probe_fields.shape
    places = lax.axis_size("gz")
    groups = places // 2
    tiles, blocks, count = rows // SUB, columns // LANES, groups * planes
    chunks = tiles // groups
    members = [list(range(groups)), list(range(groups, places))]
    scalars = [dilations, lateral_kernel_taps]

    def across(array, axis, m):
        return lax.ppermute(array, axis, [(i, i ^ m) for i in range(lax.axis_size(axis))])

    def exchange(array):
        return lax.all_to_all(
            array, "gz", split_axis=0, concat_axis=0, axis_index_groups=members, tiled=True
        )

    field = probe_fields.reshape(planes, tiles, SUB, blocks, LANES).transpose(0, 1, 3, 2, 4)
    tile, halo = (SUB, LANES), 2 * MARGIN // SUB
    hbm, vmem = pl.BlockSpec(memory_space=pltpu.HBM), pl.BlockSpec(memory_space=pltpu.VMEM)
    matrix = [pltpu.VMEM((rows, rows), jnp.bfloat16)] * 2
    edge_matrix = [pltpu.VMEM((2 * MARGIN, 2 * MARGIN), jnp.bfloat16)] * 2
    inputs = (field, root_one, root_two, dilations, lateral_kernel_taps)
    field, edge, roots, *matrices = pl.pallas_call(
        load_kernel,
        out_shape=[
            pltpu.VMEM((planes, tiles, blocks, *tile), jnp.float32),
            pltpu.VMEM((planes, halo, blocks, *tile), jnp.float32),
            pltpu.VMEM((2 * planes, *tile), jnp.float32),
            *matrix,
            *edge_matrix,
        ],
        in_specs=[hbm] * len(inputs),
        out_specs=[vmem] * 7,
        scratch_shapes=[
            pltpu.VMEM((planes, columns), jnp.float32),
            pltpu.VMEM((planes, columns), jnp.float32),
            pltpu.SMEM(dilations.shape, jnp.int32),
            pltpu.SMEM(lateral_kernel_taps.shape, jnp.float32),
            pltpu.SemaphoreType.DMA((5 + planes,)),
        ],
        compiler_params=pltpu.CompilerParams(vmem_limit_bytes=24 << 20),
    )(*[pltpu.with_memory_space_constraint(a, pltpu.HBM) for a in inputs])
    edge = across(edge, "gy", 1)
    other_roots = across(roots, "gz", groups)

    body_tiles = chunks * planes * blocks
    piece = (groups, body_tiles + 4 * planes, *tile)
    (pieces,) = call(
        functools.partial(y_inner_kernel, groups),
        [(groups, body_tiles, *tile)],
        [],
        [],
        [*matrices[:2], field],
        1 << 28,
    )
    (pieces,) = call(
        functools.partial(y_outer_kernel, groups, tiles),
        [piece],
        [],
        [],
        [*matrices[2:], edge, roots, other_roots, pieces],
        1 << 20,
    )
    pieces = exchange(pieces)

    width = 2 * LANES
    band = ((columns // width, 2 * width, width), jnp.bfloat16)
    high, low = call(
        functools.partial(band_kernel, columns), [band, band], [], scalars, [], 1 << 30
    )

    shared, scratch = (count, *tile), [(count * SUB, columns + 2 * LANES), (count * SUB, columns)]
    message, local = (2, blocks, *tile), (groups, planes * blocks, *tile)
    parts, coefficients = [], []
    for t in range(chunks):
        results = call(
            functools.partial(local_kernel, groups, planes, chunks, t),
            [local, message] + [shared] * (0 if t else 6),
            scratch,
            [],
            [pieces, high, low, *coefficients],
            1 << 28,
        )
        coefficients = coefficients or results[2:]
        parts.append((*results[:2], across(results[1], "gz", groups)))
    out = []
    for t, part in enumerate(parts):
        out = call(
            functools.partial(join_kernel, groups, planes, chunks, t),
            [(groups, body_tiles, *tile)],
            [message] + scratch,
            [],
            [*part, high, low, *coefficients, *out],
            1 << 28,
        )
    out = pl.pallas_call(
        place_kernel,
        out_shape=pltpu.HBM((planes, tiles * blocks, *tile), jnp.float32),
        in_specs=[vmem],
        out_specs=hbm,
        scratch_shapes=[pltpu.SemaphoreType.DMA],
        compiler_params=pltpu.CompilerParams(vmem_limit_bytes=24 << 20),
    )(pltpu.with_memory_space_constraint(exchange(out[0]), pltpu.VMEM))
    out = out.reshape(planes, tiles, blocks, *tile).transpose(0, 1, 3, 2, 4)
    return out.reshape(probe_fields.shape)


def body(*arrays):
    probes, planes, rows, columns = arrays[0].shape
    places, row_places = lax.axis_size("gz"), lax.axis_size("gy")
    fits = (
        probes == 1
        and row_places == 2
        and places >= 4
        and places & (places - 1) == 0
        and rows % (SUB * (places // 2)) == 0
        and rows >= 4 * MARGIN
        and columns == SUB * LANES
        and planes * places >= 4
    )
    return grouped_body(*arrays) if fits else plain_body(*arrays)


def solution(mesh):
    placed = (P(None, "gz", "gy", None), P("gz", None), P("gz", None), P(), P())
    return jax.shard_map(
        body, mesh=mesh, in_specs=placed, out_specs=P(None, "gz", "gy", None), check_vma=False
    )
```

time: 235 us -> 60 us (0.26)
  blocking collectives: 123 us -> 16.4 us
  other arithmetic: 34.2 us -> 0 us
  waiting for transfers between devices: 32.6 us -> 20.1 us
  local copies, waits for them, and re-layouts: 11.7 us -> 0.01 us
  between operations: 11.1 us -> 0.06 us
  Pallas kernels: 0 us -> 10.8 us
  starting transfers between devices: 20 us -> 12.4 us
    all_gather x2 -> x0, blocking collectives: 89.7 us -> none  [the longest x1 51.6 us: body(): lax.all_gather(root_one, 'gz', axis=0, tiled=True)]
    dynamic_update_slice x64 -> x0, other arithmetic: 21.7 us -> none  [depth_scan(): lax.scan(advance, (zero, zero), (moved, first, second, pre_gain, post_gai...]
    all_to_all x3 -> x1, waiting for transfers between devices: 32.6 us -> 14.2 us  [exchange(): lax.all_to_all(array, 'gz', split_axis=0, concat_axis=0, axis_index_group...]
    all_to_all x1, blocking collectives: 33.3 us -> 16.4 us  [exchange(): lax.all_to_all(array, 'gz', split_axis=0, concat_axis=0, axis_index_group...]
    all_to_all x3 -> x1, starting transfers between devices: 17.4 us -> 5.2 us  [exchange(): lax.all_to_all(array, 'gz', split_axis=0, concat_axis=0, axis_index_group...]
    pallas_call x0 -> x9, Pallas kernels: none -> 10.8 us  [the longest x7 8.47 us: call(): pl.pallas_call(kernel, out_shape=[pltpu.VMEM(shape, dtype) for shape, dty...]
    add x3 -> x0, other arithmetic: 8.73 us -> none  [lateral_padded(): result = result + scaled[offset_tap] * (upper + lower)]
    ppermute x2 -> x4, waiting for transfers between devices: 0.01 us -> 5.87 us  [across(): lax.ppermute(array, axis, [(i, i ^ m) for i in range(lax.axis_size(axis))])]
  transfers between devices with their start and end apart: 5 -> 5, of which waited for: 2 -> 4; matrix products, arithmetic and copies ran while one was open for 1% -> 0% of each run, Pallas kernels for 0% -> 9%
where the time goes in v2:
time: 60 us; the launch traced here: 59.7 us
  waiting for transfers between devices  20.1 us (34%)
  blocking collectives  16.4 us (27%)
  starting transfers between devices  12.4 us (21%)
  Pallas kernels  10.8 us (18%)
    all_to_all x1, blocking collectives, exchange(): lax.all_to_all(array, 'gz', split_axis=0, concat_axis=0, axis_index_group...  16.4 us
    all_to_all x1, waiting for transfers between devices, exchange(): lax.all_to_all(array, 'gz', split_axis=0, concat_axis=0, axis_index_group...  14.2 us
    pallas_call x7, Pallas kernels, call(): pl.pallas_call(kernel, out_shape=[pltpu.VMEM(shape, dtype) for shape, dty...  8.47 us
    ppermute x4, starting transfers between devices, across(): lax.ppermute(array, axis, [(i, i ^ m) for i in range(lax.axis_size(axis))])  7.24 us
    ppermute x4, waiting for transfers between devices, across(): lax.ppermute(array, axis, [(i, i ^ m) for i in range(lax.axis_size(axis))])  5.87 us
    all_to_all x1, starting transfers between devices, exchange(): lax.all_to_all(array, 'gz', split_axis=0, concat_axis=0, axis_index_group...  5.2 us
    pallas_call x1, Pallas kernels, grouped_body(): pl.pallas_call(load_kernel, out_shape=[pltpu.VMEM((planes, tiles, blocks,...  1.37 us
  transfers between devices with their start and end apart: 5, of which 4 were waited for; matrix products, arithmetic and copies ran while one was open for 0% of the time, Pallas kernels for 9%

profile of v2, /device:TPU:0, one launch (start us, length us, event | category | flops | bytes accessed | tf_op | source)
XLA Modules:
  0.0 59.7 jit_solution(5929554919193005312)
XLA Ops:
  0.0 1.4 %shard_map.55 = (f32[2,16,8,8,128]{4,3,2,1,0:T(8,128)S(1)}, f32[2,4,8,8,128]{4,3,2,1,0:T(8,128)S(1)}, f32[4,8,128]{2,1,0:T(8,128)S(1)}, bf16[128,128]{1,0:T(8,12...) custom-call(f32[2,16,8,8,128]{4,3,2,1,0:T(8,128)} %bitcast.8, ...), custom_call_target="tpu_custom_call" | custom-call | tf_op jit(solution)/shard_map/pallas_call | solution.py:438
  1.4 0.5 collective-permute-start
  1.9 3.7 %collective-permute-start.1 = (f32[4,8,128]{2,1,0:T(8,128)S(1)}, f32[4,8,128]{2,1,0:T(8,128)S(1)}, u32[]{:S(2)}, u32[]{:S(2)}) collective-permute-start(f32[4,8,128]{2,1,0:T(8,128)S(1)} %get-tuple-element.27.roots), channel_id=1, source_target_pairs={{0,16},{2,18},{4,20},{6,22},{8,24},{10,26},{12,28},{14,30},{16,0},... | collective-permute-start | bytes 49160 | tf_op jit(solution)/shard_map/ppermute | solution.py:425
  5.6 0.6 shard_map.56.given
  6.1 1.2 %collective-permute-done.1.other_roots = f32[4,8,128]{2,1,0:T(8,128)S(1)} collective-permute-done((f32[4,8,128]{2,1,0:T(8,128)S(1)}, f32[4,8,128]{2,1,0:T(8,128)S(1)}, u32[]{:S(2)}, u32[]{:S(2)}) %collective-permute-start.1) | collective-permute-done | bytes 16416 | tf_op jit(solution)/shard_map/ppermute | solution.py:425
  7.3 0.0 collective-permute-done.edge
  7.3 1.3 %shard_map.57 = f32[8,40,8,128]{3,2,1,0:T(8,128)} custom-call(bf16[32,32]{1,0:T(8,128)(2,1)S(1)} %get-tuple-element.24.high, bf16[32,32]{1,0:T(8,128)(2,1)S(1)} %get-tuple-element.25.low, f32[2,4,8,8,128]{4,3,2,1,0:T(8,128)S(1)} %collective-permute-done.edge, f32[4,8,128]{2,1,0:T(8,128)S(1)} %get-tuple-element.27.roots, ...), custom_call_target="tpu_custom_call" | custom-call | flops 1048576 | bytes 65536 | tf_op jit(solution)/shard_map/pallas_call | solution.py:99
  8.6 0.0 copy-start
  8.6 0.0 copy-start.1
  8.6 5.2 %all-to-all-start = ((f32[8,40,8,128]{3,2,1,0:T(8,128)}), f32[8,40,8,128]{3,2,1,0:T(8,128)S(1)}, u32[]{:S(2)}, u32[]{:S(2)}) async-start(f32[8,40,8,128]{3,2,1,0:T(8,128)} %shard_map.57), calls=%async_computation | async-start | bytes 2621440 | tf_op jit(solution)/shard_map/all_to_all | solution.py:428
  13.8 0.0 copy-done
  13.8 0.0 copy-done.1
  13.8 2.9 %shard_map.58 = (bf16[4,512,256]{2,1,0:T(8,128)(2,1)S(1)}, bf16[4,512,256]{2,1,0:T(8,128)(2,1)S(1)}) custom-call(s32[2]{0:T(128)S(1)} %copy-done.1, f32[2,3]{1,0:T(2,128)S(1)} %copy-done), custom_call_target="tpu_custom_call" | custom-call | flops 1073741824 | bytes 65536 | tf_op jit(solution)/shard_map/pallas_call | solution.py:99
  16.8 14.2 %all-to-all-done.refs_0_ = f32[8,40,8,128]{3,2,1,0:T(8,128)S(1)} async-done(((f32[8,40,8,128]{3,2,1,0:T(8,128)}), f32[8,40,8,128]{3,2,1,0:T(8,128)S(1)}, u32[]{:S(2)}, u32[]{:S(2)}) %all-to-all-start) | async-done | bytes 1310752 | tf_op jit(solution)/shard_map/all_to_all | solution.py:428
  31.0 0.9 %shard_map.59 = (f32[8,16,8,128]{3,2,1,0:T(8,128)S(1)}, f32[2,8,8,128]{3,2,1,0:T(8,128)S(1)}, f32[16,8,128]{2,1,0:T(8,128)S(1)}, f32[16,8,128]{2,1,0:T(8,128)S(1...) custom-call(f32[8,40,8,128]{3,2,1,0:T(8,128)S(1)} %all-to-all-done.r, ...), custom_call_target="tpu_custom_call" | custom-call | flops 268435456 | bytes 65536 | tf_op jit(solution)/shard_map/pallas_call | solution.py:99
  31.9 2.7 %collective-permute-start.3 = (f32[2,8,8,128]{3,2,1,0:T(8,128)S(1)}, f32[2,8,8,128]{3,2,1,0:T(8,128)S(1)}, u32[]{:S(2)}, u32[]{:S(2)}) collective-permute-start(f32[2,8,8,128]{3,2,1,0:T(8,128)S(1)} %get-tuple-element.42.sent), channel_id=1, source_target_pairs={{0,16},{2,18},{4,20},{6,22},{8,24},{10,26},{12,28},{14,30},{16,0},... | collective-permute-start | bytes 196616 | tf_op jit(solution)/shard_map/ppermute | solution.py:425
  34.6 0.9 %shard_map.60 = (f32[8,16,8,128]{3,2,1,0:T(8,128)S(1)}, f32[2,8,8,128]{3,2,1,0:T(8,128)S(1)}) custom-call(f32[8,40,8,128]{3,2,1,0:T(8,128)S(1)} %all-to-all-done.refs_0_, bf16[4,512,256]{2,1,0:T(8,128)(2,1)S(1)} %get-tuple-element.31.refs_1_.high, bf16[4,512,256]{2,1,0:T(8,128)(2,1)S(1)} %get-tuple-element.32.refs_2_.low, ...), custom_call_target="tpu_custom_call" | custom-call | flops 268435456 | bytes 65536 | tf_op jit(solution)/shard_map/pallas_call | solution.py:99
  35.5 0.3 collective-permute-start.2
  35.9 2.3 %collective-permute-done.3.received = f32[2,8,8,128]{3,2,1,0:T(8,128)S(1)} collective-permute-done((f32[2,8,8,128]{3,2,1,0:T(8,128)S(1)}, f32[2,8,8,128]{3,2,1,0:T(8,128)S(1)}, u32[]{:S(2)}, u32[]{:S(2)}) %collective-permute-start.3) | collective-permute-done | bytes 65568 | tf_op jit(solution)/shard_map/ppermute | solution.py:425
  38.2 0.9 %shard_map.61.refs_6_ = f32[8,32,8,128]{3,2,1,0:T(8,128)S(1)} custom-call(f32[8,16,8,128]{3,2,1,0:T(8,128)S(1)} %get-tuple-element.41.local, f32[2,8,8,128]{3,2,1,0:T(8,128)S(1)} %get-tuple-element.42.sent, f32[2,8,8,128]{3,2,1,0:T(8,128)S(1)} %collective-permute-done.3.received, bf16[4,512,256]{2,1,0:T(8,128)(2,1)S(1)} %get-tuple-element.31.refs_1_.high, ...), custom_call_target="tpu_custom_call" | custom-call | flops 268435456 | bytes 65536 | tf_op jit(solution)/shard_map/pallas_call | solution.py:99
  39.1 2.4 %collective-permute-done.2.received = f32[2,8,8,128]{3,2,1,0:T(8,128)S(1)} collective-permute-done((f32[2,8,8,128]{3,2,1,0:T(8,128)S(1)}, f32[2,8,8,128]{3,2,1,0:T(8,128)S(1)}, u32[]{:S(2)}, u32[]{:S(2)}) %collective-permute-start.2) | collective-permute-done | bytes 65568 | tf_op jit(solution)/shard_map/ppermute | solution.py:425
  41.5 0.9 %shard_map.62 = f32[8,32,8,128]{3,2,1,0:T(8,128)S(1)} custom-call(f32[8,16,8,128]{3,2,1,0:T(8,128)S(1)} %get-tuple-element.39.local, f32[2,8,8,128]{3,2,1,0:T(8,128)S(1)} %get-tuple-element.40.sent, f32[2,8,8,128]{3,2,1,0:T(8,128)S(1)} %collective-permute-done.2.received, bf16[4,512,256]{2,1,0:T(8,128)(2,1)S(1)} %get-tuple-element.31.refs_1_.high, ...), custom_call_target="tpu_custom_call" | custom-call | flops 268435456 | bytes 65536 | tf_op jit(solution)/shard_map/pallas_call | solution.py:99
  42.4 16.4 %all_to_all.10.pieces = f32[8,32,8,128]{3,2,1,0:T(8,128)S(1)} all-to-all(f32[8,32,8,128]{3,2,1,0:T(8,128)S(1)} %shard_map.62), channel_id=1, replica_groups={{0,2,4,6,8,10,12,14},{16,18,20,22,24,26,28,30},{1,3,5,7,9,11,13,15},{17..., dimensions={0} | all-to-all | bytes 2097152 | tf_op jit(solution)/shard_map/all_to_all | solution.py:428
  58.8 1.0 %shard_map.63 = f32[2,128,8,128]{3,2,1,0:T(8,128)} custom-call(f32[8,32,8,128]{3,2,1,0:T(8,128)S(1)} %all_to_all.10.pieces), custom_call_target="tpu_custom_call" | custom-call | tf_op jit(solution)/shard_map/pallas_call | solution.py:511
Async XLA Ops:
  1.4 5.9 %collective-permute-start = (f32[2,4,8,8,128]{4,3,2,1,0:T(8,128)S(1)}, f32[2,4,8,8,128]{4,3,2,1,0:T(8,128)S(1)}, u32[]{:S(2)}, u32[]{:S(2)}) collective-permute-start(f32[2,4,8,8,128]{4,3,2,1,0:T(8,128)S(1)} %get-tuple-element.26), channel_id=1, source_target_pairs={{0,1},{1,0},{2,3},{3,2},{4,5},{5,4},{6,7},{7,6},{8,9},{9,8},{10,11... | collective-permute-start | bytes 786440 | tf_op jit(solution)/shard_map/ppermute | solution.py:425
  1.9 5.4 %collective-permute-start.1 = (f32[4,8,128]{2,1,0:T(8,128)S(1)}, f32[4,8,128]{2,1,0:T(8,128)S(1)}, u32[]{:S(2)}, u32[]{:S(2)}) collective-permute-start(f32[4,8,128]{2,1,0:T(8,128)S(1)} %get-tuple-element.27.roots), channel_id=1, source_target_pairs={{0,16},{2,18},{4,20},{6,22},{8,24},{10,26},{12,28},{14,30},{16,0},... | collective-permute-start | bytes 49160 | tf_op jit(solution)/shard_map/ppermute | solution.py:425
  8.6 5.2 %copy-start = (f32[2,3]{1,0:T(2,128)S(1)}, f32[2,3]{1,0:T(2,128)}, u32[]{:S(2)}) copy-start(f32[2,3]{1,0:T(2,128)} %taps.1) | copy-start | bytes 76
  8.6 5.2 %copy-start.1 = (s32[2]{0:T(128)S(1)}, s32[2]{0:T(128)}, u32[]{:S(2)}) copy-start(s32[2]{0:T(128)} %dilations.1) | copy-start | bytes 28
  8.6 22.3 %all-to-all-start = ((f32[8,40,8,128]{3,2,1,0:T(8,128)}), f32[8,40,8,128]{3,2,1,0:T(8,128)S(1)}, u32[]{:S(2)}, u32[]{:S(2)}) async-start(f32[8,40,8,128]{3,2,1,0:T(8,128)} %shard_map.57), calls=%async_computation | async-start | bytes 2621440 | tf_op jit(solution)/shard_map/all_to_all | solution.py:428
  31.9 6.3 %collective-permute-start.3 = (f32[2,8,8,128]{3,2,1,0:T(8,128)S(1)}, f32[2,8,8,128]{3,2,1,0:T(8,128)S(1)}, u32[]{:S(2)}, u32[]{:S(2)}) collective-permute-start(f32[2,8,8,128]{3,2,1,0:T(8,128)S(1)} %get-tuple-element.42.sent), channel_id=1, source_target_pairs={{0,16},{2,18},{4,20},{6,22},{8,24},{10,26},{12,28},{14,30},{16,0},... | collective-permute-start | bytes 196616 | tf_op jit(solution)/shard_map/ppermute | solution.py:425
  35.5 5.9 %collective-permute-start.2 = (f32[2,8,8,128]{3,2,1,0:T(8,128)S(1)}, f32[2,8,8,128]{3,2,1,0:T(8,128)S(1)}, u32[]{:S(2)}, u32[]{:S(2)}) collective-permute-start(f32[2,8,8,128]{3,2,1,0:T(8,128)S(1)} %get-tuple-element.40.sent), channel_id=1, source_target_pairs={{0,16},{2,18},{4,20},{6,22},{8,24},{10,26},{12,28},{14,30},{16,0},... | collective-permute-start | bytes 196616 | tf_op jit(solution)/shard_map/ppermute | solution.py:425

commit v3 on v2

--- a/solution.py
+++ b/solution.py
@@ -93,19 +93,24 @@
     return lax.all_to_all(field, "gz", split_axis=1, concat_axis=2, tiled=True)
 
 
-def call(kernel, outs, scratch, scalars, arrays, cost):
+NO_COST = pl.CostEstimate(flops=0, bytes_accessed=0, transcendentals=0)
+
+
+def call(kernel, outs, scratch, arrays):
     arrays = [pltpu.with_memory_space_constraint(a, pltpu.VMEM) for a in arrays]
-    outs = [out if len(out) == 2 else (out, jnp.float32) for out in outs]
+    outs, scratch = (
+        [item if len(item) == 2 and isinstance(item[0], tuple) else (item, jnp.float32) for item in items]
+        for items in (outs, scratch)
+    )
     return pl.pallas_call(
         kernel,
         out_shape=[pltpu.VMEM(shape, dtype) for shape, dtype in outs],
-        in_specs=[pl.BlockSpec(memory_space=pltpu.SMEM)] * len(scalars)
-        + [pl.BlockSpec(memory_space=pltpu.VMEM)] * len(arrays),
+        in_specs=[pl.BlockSpec(memory_space=pltpu.VMEM)] * len(arrays),
         out_specs=[pl.BlockSpec(memory_space=pltpu.VMEM)] * len(outs),
-        scratch_shapes=[pltpu.VMEM(shape, jnp.float32) for shape in scratch],
+        scratch_shapes=[pltpu.VMEM(shape, dtype) for shape, dtype in scratch],
         compiler_params=pltpu.CompilerParams(vmem_limit_bytes=24 << 20),
-        cost_estimate=pl.CostEstimate(flops=cost, bytes_accessed=1 << 16, transcendentals=0),
-    )(*scalars, *arrays)
+        cost_estimate=NO_COST,
+    )(*arrays)
 
 
 def tap_vectors(taps, axis, shape):
@@ -150,42 +155,55 @@
         high[i : i + part], low[i : i + part] = split(value)
 
 
+def edge_kernel(x_ref, one_ref, two_ref, edge, roots, rows, sems):
+    depth = edge.shape[1]
+    start = jnp.where(lax.axis_index("gy") == 0, x_ref.shape[1] - depth, 0)
+    copies = [
+        pltpu.make_async_copy(one_ref, rows.at[0], sems.at[0]),
+        pltpu.make_async_copy(two_ref, rows.at[1], sems.at[1]),
+        pltpu.make_async_copy(x_ref.at[:, pl.ds(start, depth)], edge, sems.at[2]),
+    ]
+    for copy in copies:
+        copy.start()
+    copies[0].wait()
+    copies[1].wait()
+    planes, blocks = rows.shape[1], rows.shape[2] // LANES
+    for i in range(2):
+        for p in range(planes):
+            for b in range(blocks):
+                lanes = slice(b * LANES, (b + 1) * LANES)
+                roots[i * planes + p, b : b + 1] = rows[i, p : p + 1, lanes]
+    copies[2].wait()
+
+
 def load_kernel(
-    x_ref, one_ref, two_ref, dilations_ref, taps_ref,
-    whole, edge, roots, high, low, edge_high, edge_low, one, two, dilations, taps, sems,
+    x_ref, dilations_ref, taps_ref, _,
+    whole, high, low, edge_high, edge_low, x_step, x_taps, dilations, taps, sems,
 ):
     row_at, row_places = lax.axis_index("gy"), lax.axis_size("gy")
     planes, tiles = x_ref.shape[:2]
-    depth, blocks = edge.shape[1:3]
     rows = tiles * SUB
-    start = jnp.where(row_at == 0, tiles - depth, 0)
     copies = [
-        pltpu.make_async_copy(x_ref.at[:, pl.ds(start, depth)], edge, sems.at[0]),
-        pltpu.make_async_copy(one_ref, one, sems.at[1]),
-        pltpu.make_async_copy(two_ref, two, sems.at[2]),
-        pltpu.make_async_copy(dilations_ref, dilations, sems.at[3]),
-        pltpu.make_async_copy(taps_ref, taps, sems.at[4]),
+        pltpu.make_async_copy(dilations_ref, dilations, sems.at[0]),
+        pltpu.make_async_copy(taps_ref, taps, sems.at[1]),
     ]
     copies += [
-        pltpu.make_async_copy(x_ref.at[p], whole.at[p], sems.at[5 + p]) for p in range(planes)
+        pltpu.make_async_copy(x_ref.at[p], whole.at[p], sems.at[2 + p]) for p in range(planes)
     ]
     for copy in copies:
         copy.start()
-    for copy in copies[1:5]:
-        copy.wait()
-    for p in range(planes):
-        for b in range(blocks):
-            lanes = slice(b * LANES, (b + 1) * LANES)
-            roots[p, b : b + 1] = one[p : p + 1, lanes]
-            roots[planes + p, b : b + 1] = two[p : p + 1, lanes]
+    copies[0].wait()
+    copies[1].wait()
+    x_step[...] = jnp.full(x_step.shape, dilations[0], jnp.int32)
+    for i, tap in enumerate(tap_vectors(taps, 0, (1, LANES))):
+        x_taps[i : i + 1] = tap
     step, weights = dilations[1], tap_vectors(taps, 1, (1, 1))
     length, begin = rows * row_places, row_at * rows
     fill_band(high, low, length, step, weights, begin, begin)
     near = begin + jnp.where(row_at == 0, rows - 2 * MARGIN, 0)
     beyond = begin + jnp.where(row_at == 0, rows, -2 * MARGIN)
     fill_band(edge_high, edge_low, length, step, weights, near, beyond)
-    copies[0].wait()
-    for copy in copies[5:]:
+    for copy in copies[2:]:
         copy.wait()
 
 
@@ -206,11 +224,14 @@
                     pieces[i // chunks, (p * chunks + i % chunks) * blocks + b + w] = tile
 
 
-def y_outer_kernel(groups, tiles, high, low, edge, roots, other_roots, given, pieces):
+def y_outer_kernel(groups, tiles, high, low, edge, given, roots, other_roots, _, pieces):
     planes, halo, blocks = edge.shape[:3]
     chunks, width = tiles // groups, 2
     base = chunks * planes * blocks
     pieces[:, :base] = given[...]
+    for i in range(groups):
+        pieces[i, base : base + 2 * planes] = roots[...]
+        pieces[i, base + 2 * planes :] = other_roots[...]
     first = jnp.where(lax.axis_index("gy") == 0, (tiles - halo) // chunks, 0)
     for p in range(planes):
         for b in range(0, blocks, width):
@@ -220,39 +241,49 @@
                     tile = value[i * SUB : (i + 1) * SUB, w * LANES : (w + 1) * LANES]
                     to, at = first + i // chunks, (p * chunks + i % chunks) * blocks
                     pieces[to, at + b + w] = given[to, at + b + w] + tile
-    for i in range(groups):
-        for r in range(2 * planes):
-            pieces[i, base + r] = roots[r]
-            pieces[i, base + 2 * planes + r] = other_roots[r]
-
-
-def band_kernel(columns, dilations, taps, high, low):
-    count, depth, width = high.shape
-    step, taps = dilations[0], tap_vectors(taps, 0, (1, width))
-    part = 2 * SUB
-    lane = lax.broadcasted_iota(jnp.int32, (part, width), 1)
-    row = lax.broadcasted_iota(jnp.int32, (part, width), 0)
-    for n in range(count):
-        at = lax.broadcasted_iota(jnp.int32, (1, width), 1) + n * width
-        sums = double_taps(at, columns, step, taps)
-
-        def rows_at(i, _):
-            apart = row + (i * part - LANES) - lane
-            value = jnp.zeros((part, width), jnp.float32)
-            for o, total in sums.items():
-                value = jnp.where(apart == o * step, total, value)
-            at_rows = pl.ds(pl.multiple_of(i * part, part), part)
-            high[n, at_rows], low[n, at_rows] = split(value)
-            return 0
-
-        lax.fori_loop(0, depth // part, rows_at, 0)
-
-
-def x_twice(source, result, high, low):
-    for n in range(high.shape[0]):
-        depth, width = high.shape[1:]
-        value = split(source[:, n * width : n * width + depth])
-        result[:, n * width : (n + 1) * width] = product(value, (high[n], low[n]))
+
+
+def band_kinds(count):
+    kinds = sorted({0, min(1, count - 1), count - 1})
+    return kinds, [0 if n == 0 else len(kinds) - 1 if n == count - 1 else 1 for n in range(count)]
+
+
+def band_kernel(columns, x_step, x_taps, high, low):
+    depth, width = high.shape[1:]
+    step, taps = x_step[0:1], [x_taps[i : i + 1] for i in range(RADIUS + 1)]
+    part, reach = 2 * SUB, 2 * MARGIN
+    lane = lax.broadcasted_iota(jnp.int32, (part, LANES), 1)
+    row = lax.broadcasted_iota(jnp.int32, (part, LANES), 0)
+    high[...] = jnp.zeros(high.shape, high.dtype)
+    low[...] = jnp.zeros(low.shape, low.dtype)
+    for kind, n in enumerate(band_kinds(columns // width)[0]):
+        for w in range(0, width, LANES):
+            at = lax.broadcasted_iota(jnp.int32, (1, LANES), 1) + (n * width + w)
+            sums = double_taps(at, columns, step, taps)
+            lanes = slice(w, w + LANES)
+
+            def rows_at(i, _):
+                start = w + LANES - reach + i * part
+                apart = row + (start - LANES - w) - lane
+                value = jnp.zeros((part, LANES), jnp.float32)
+                for o, total in sums.items():
+                    value = jnp.where(apart == o * step, total, value)
+                at_rows = pl.ds(pl.multiple_of(start, part), part)
+                high[kind, at_rows, lanes], low[kind, at_rows, lanes] = split(value)
+                return 0
+
+            lax.fori_loop(0, (LANES + 2 * reach) // part, rows_at, 0, unroll=2)
+
+
+def x_twice(source, result, high, low, parts):
+    rows, (depth, width) = source.shape[0], high.shape[1:]
+    parts[:rows], parts[rows:] = split(source[...])
+    dot = functools.partial(jnp.dot, preferred_element_type=jnp.float32)
+    for n, kind in enumerate(band_kinds(result.shape[1] // width)[1]):
+        lanes = slice(n * width, n * width + depth)
+        total = dot(parts[:, lanes], high[kind])
+        total = total[:rows] + (total[rows:] + dot(parts[:rows, lanes], low[kind]))
+        result[:, n * width : (n + 1) * width] = total
 
 
 def add(a, b):
@@ -330,9 +361,9 @@
 
 def local_kernel(groups, planes, chunks, chunk, *refs):
     if chunk == 0:
-        pieces, high, low, local, message, *coefficients, field, middle = refs
+        pieces, high, low, local, message, *coefficients, field, middle, halves = refs
     else:
-        pieces, high, low, *coefficients, local, message, field, middle = refs
+        pieces, high, low, *coefficients, local, message, field, middle, halves = refs
     half = lax.axis_index("gz") // groups
     blocks = message.shape[1]
     count = groups * planes
@@ -355,7 +386,7 @@
         return [pieces[d, (p * chunks + chunk) * blocks + b] for b in range(blocks)]
 
     ahead, pending = filter_back(count, planes, source, own, field, (zeros, zeros))
-    x_twice(field, middle, high, low)
+    x_twice(field, middle, high, low, halves)
 
     def finish(d, p, value):
         for b, v in enumerate(value):
@@ -368,8 +399,8 @@
 
 
 def join_kernel(groups, planes, chunks, chunk, local, sent, received, high, low, *refs):
-    own, lower, before = refs[:3], refs[3:6], refs[6:-4]
-    out, carried, field, middle = refs[-4:]
+    own, lower, before = refs[:3], refs[3:6], refs[6:-5]
+    out, carried, field, middle, halves = refs[-5:]
     half = lax.axis_index("gz") // groups
     blocks = sent.shape[1]
     count = groups * planes
@@ -382,7 +413,7 @@
     zeros = [field[0:SUB, 0:LANES]] * blocks
     start = (tiles_of(carried, 0), tiles_of(carried, 1))
     filter_back(count, planes, None, lower, field, start)
-    x_twice(field, middle, high, low)
+    x_twice(field, middle, high, low, halves)
 
     def finish(d, p, value):
         for b, v in enumerate(value):
@@ -419,7 +450,6 @@
     tiles, blocks, count = rows // SUB, columns // LANES, groups * planes
     chunks = tiles // groups
     members = [list(range(groups)), list(range(groups, places))]
-    scalars = [dilations, lateral_kernel_taps]
 
     def across(array, axis, m):
         return lax.ppermute(array, axis, [(i, i ^ m) for i in range(lax.axis_size(axis))])
@@ -434,57 +464,76 @@
     hbm, vmem = pl.BlockSpec(memory_space=pltpu.HBM), pl.BlockSpec(memory_space=pltpu.VMEM)
     matrix = [pltpu.VMEM((rows, rows), jnp.bfloat16)] * 2
     edge_matrix = [pltpu.VMEM((2 * MARGIN, 2 * MARGIN), jnp.bfloat16)] * 2
-    inputs = (field, root_one, root_two, dilations, lateral_kernel_taps)
-    field, edge, roots, *matrices = pl.pallas_call(
+    params = pltpu.CompilerParams(vmem_limit_bytes=24 << 20)
+
+    def in_hbm(*arrays):
+        return [pltpu.with_memory_space_constraint(array, pltpu.HBM) for array in arrays]
+
+    edge, roots = pl.pallas_call(
+        edge_kernel,
+        out_shape=[
+            pltpu.VMEM((planes, halo, blocks, *tile), jnp.float32),
+            pltpu.VMEM((2 * planes, *tile), jnp.float32),
+        ],
+        in_specs=[hbm] * 3,
+        out_specs=[vmem] * 2,
+        scratch_shapes=[
+            pltpu.VMEM((2, planes, columns), jnp.float32),
+            pltpu.SemaphoreType.DMA((3,)),
+        ],
+        compiler_params=params,
+        cost_estimate=NO_COST,
+    )(*in_hbm(field, root_one, root_two))
+    field, *matrices, x_step, x_taps = pl.pallas_call(
         load_kernel,
         out_shape=[
             pltpu.VMEM((planes, tiles, blocks, *tile), jnp.float32),
-            pltpu.VMEM((planes, halo, blocks, *tile), jnp.float32),
-            pltpu.VMEM((2 * planes, *tile), jnp.float32),
             *matrix,
             *edge_matrix,
+            pltpu.VMEM(tile, jnp.int32),
+            pltpu.VMEM(tile, jnp.float32),
         ],
-        in_specs=[hbm] * len(inputs),
+        in_specs=[hbm] * 3 + [vmem],
         out_specs=[vmem] * 7,
         scratch_shapes=[
-            pltpu.VMEM((planes, columns), jnp.float32),
-            pltpu.VMEM((planes, columns), jnp.float32),
             pltpu.SMEM(dilations.shape, jnp.int32),
             pltpu.SMEM(lateral_kernel_taps.shape, jnp.float32),
-            pltpu.SemaphoreType.DMA((5 + planes,)),
+            pltpu.SemaphoreType.DMA((2 + planes,)),
         ],
-        compiler_params=pltpu.CompilerParams(vmem_limit_bytes=24 << 20),
-    )(*[pltpu.with_memory_space_constraint(a, pltpu.HBM) for a in inputs])
+        compiler_params=params,
+        cost_estimate=NO_COST,
+    )(
+        *in_hbm(field, dilations, lateral_kernel_taps),
+        pltpu.with_memory_space_constraint(roots, pltpu.VMEM),
+    )
+    other_roots = across(roots, "gz", groups)
     edge = across(edge, "gy", 1)
-    other_roots = across(roots, "gz", groups)
-
+
+    width = 2 * LANES
+
+    band = ((len(band_kinds(columns // width)[0]), 2 * width, width), jnp.bfloat16)
+    high, low = call(
+        functools.partial(band_kernel, columns), [band, band], [], [x_step, x_taps]
+    )
     body_tiles = chunks * planes * blocks
     piece = (groups, body_tiles + 4 * planes, *tile)
     (pieces,) = call(
         functools.partial(y_inner_kernel, groups),
         [(groups, body_tiles, *tile)],
         [],
-        [],
         [*matrices[:2], field],
-        1 << 28,
     )
     (pieces,) = call(
         functools.partial(y_outer_kernel, groups, tiles),
         [piece],
         [],
-        [],
-        [*matrices[2:], edge, roots, other_roots, pieces],
-        1 << 20,
+        [*matrices[2:], edge, pieces, roots, other_roots, low],
     )
     pieces = exchange(pieces)
 
-    width = 2 * LANES
-    band = ((columns // width, 2 * width, width), jnp.bfloat16)
-    high, low = call(
-        functools.partial(band_kernel, columns), [band, band], [], scalars, [], 1 << 30
-    )
-
-    shared, scratch = (count, *tile), [(count * SUB, columns + 2 * LANES), (count * SUB, columns)]
+    all_rows, wide = count * SUB, columns + 2 * LANES
+    shared = (count, *tile)
+    scratch = [(all_rows, wide), (all_rows, columns), ((2 * all_rows, wide), jnp.bfloat16)]
     message, local = (2, blocks, *tile), (groups, planes * blocks, *tile)
     parts, coefficients = [], []
     for t in range(chunks):
@@ -492,9 +541,7 @@
             functools.partial(local_kernel, groups, planes, chunks, t),
             [local, message] + [shared] * (0 if t else 6),
             scratch,
-            [],
             [pieces, high, low, *coefficients],
-            1 << 28,
         )
         coefficients = coefficients or results[2:]
         parts.append((*results[:2], across(results[1], "gz", groups)))
@@ -504,9 +551,7 @@
             functools.partial(join_kernel, groups, planes, chunks, t),
             [(groups, body_tiles, *tile)],
             [message] + scratch,
-            [],
             [*part, high, low, *coefficients, *out],
-            1 << 28,
         )
     out = pl.pallas_call(
         place_kernel,
@@ -514,7 +559,7 @@
         in_specs=[vmem],
         out_specs=hbm,
         scratch_shapes=[pltpu.SemaphoreType.DMA],
-        compiler_params=pltpu.CompilerParams(vmem_limit_bytes=24 << 20),
+        compiler_params=params,
     )(pltpu.with_memory_space_constraint(exchange(out[0]), pltpu.VMEM))
     out = out.reshape(planes, tiles, blocks, *tile).transpose(0, 1, 3, 2, 4)
     return out.reshape(probe_fields.shape)

time: 60 us -> 58 us (0.967)
  blocking collectives: 16.4 us -> 38.7 us
  waiting for transfers between devices: 20.1 us -> 3.17 us
  starting transfers between devices: 12.4 us -> 7.24 us
  Pallas kernels: 10.8 us -> 8.55 us
    all_to_all x1 -> x2, blocking collectives: 16.4 us -> 38.7 us  [exchange(): lax.all_to_all(array, 'gz', split_axis=0, concat_axis=0, axis_index_group...]
    all_to_all x1 -> x0, waiting for transfers between devices: 14.2 us -> none  [exchange(): lax.all_to_all(array, 'gz', split_axis=0, concat_axis=0, axis_index_group...]
    all_to_all x1 -> x0, starting transfers between devices: 5.2 us -> none  [exchange(): lax.all_to_all(array, 'gz', split_axis=0, concat_axis=0, axis_index_group...]
    pallas_call x7, Pallas kernels: 8.47 us -> 5.36 us  [call(): pl.pallas_call(kernel, out_shape=[pltpu.VMEM(shape, dtype) for shape, dty...]
    ppermute x4, waiting for transfers between devices: 5.87 us -> 3.17 us  [across(): lax.ppermute(array, axis, [(i, i ^ m) for i in range(lax.axis_size(axis))])]
    pallas_call x0 -> x1, Pallas kernels: none -> 1.01 us  [grouped_body(): pl.pallas_call(edge_kernel, out_shape=[pltpu.VMEM((planes, halo, blocks,...]
  transfers between devices with their start and end apart: 5 -> 4, of which waited for: 4 -> 2; matrix products, arithmetic and copies ran while one was open for 0% -> 0% of each run, Pallas kernels for 9% -> 8%
where the time goes in v3:
time: 58 us; the launch traced here: 57.8 us
  blocking collectives  38.7 us (67%)
  Pallas kernels  8.55 us (15%)
  starting transfers between devices  7.24 us (12%)
  waiting for transfers between devices  3.17 us (5%)
    all_to_all x2, blocking collectives, exchange(): lax.all_to_all(array, 'gz', split_axis=0, concat_axis=0, axis_index_group...  38.7 us
    ppermute x4, starting transfers between devices, across(): lax.ppermute(array, axis, [(i, i ^ m) for i in range(lax.axis_size(axis))])  7.24 us
    pallas_call x7, Pallas kernels, call(): pl.pallas_call(kernel, out_shape=[pltpu.VMEM(shape, dtype) for shape, dty...  5.36 us
    ppermute x4, waiting for transfers between devices, across(): lax.ppermute(array, axis, [(i, i ^ m) for i in range(lax.axis_size(axis))])  3.17 us
    pallas_call x1, Pallas kernels, grouped_body(): pl.pallas_call(load_kernel, out_shape=[pltpu.VMEM((planes, tiles, blocks,...  1.23 us
  transfers between devices with their start and end apart: 4, of which 2 were waited for; matrix products, arithmetic and copies ran while one was open for 0% of the time, Pallas kernels for 8%

profile of v3, /device:TPU:0, one launch (start us, length us, event | category | flops | bytes accessed | tf_op | source)
XLA Modules:
  0.0 57.8 jit_solution(2987520488023609676)
XLA Ops:
  0.0 1.0 %shard_map.55 = (f32[2,4,8,8,128]{4,3,2,1,0:T(8,128)S(1)}, f32[4,8,128]{2,1,0:T(8,128)S(1)}) custom-call(f32[2,16,8,8,128]{4,3,2,1,0:T(8,128)} %bitcast.8, f32[2,1024]{1,0:T(2,128)} %one_ref.1, f32[2,1024]{1,0:T(2,128)} %two_ref.1), custom_call_target="tpu_custom_call" | custom-call | tf_op jit(solution)/shard_map/pallas_call | solution.py:472
  1.0 0.5 collective-permute-start
  1.5 3.7 %collective-permute-start.1 = (f32[4,8,128]{2,1,0:T(8,128)S(1)}, f32[4,8,128]{2,1,0:T(8,128)S(1)}, u32[]{:S(2)}, u32[]{:S(2)}) collective-permute-start(f32[4,8,128]{2,1,0:T(8,128)S(1)} %get-tuple-element.26._.roots), channel_id=1, source_target_pairs={{0,16},{2,18},{4,20},{6,22},{8,24},{10,26},{12,28},{14,30},{16,0},... | collective-permute-start | bytes 49160 | tf_op jit(solution)/shard_map/ppermute | solution.py:455
  5.2 1.2 %shard_map.56 = (f32[2,16,8,8,128]{4,3,2,1,0:T(8,128)S(1)}, bf16[128,128]{1,0:T(8,128)(2,1)S(1)}, bf16[128,128]{1,0:T(8,128)(2,1)S(1)}, bf16[32,32]{1,0:T(8,128)...) custom-call(f32[2,16,8,8,128]{4,3,2,1,0:T(8,128)} %bitcast.9, s32[2]{0:T(128)} %dilations_ref.1, ...), custom_call_target="tpu_custom_call" | custom-call | tf_op jit(solution)/shard_map/pallas_call | solution.py:487
  6.4 0.9 %shard_map.58 = (bf16[3,512,256]{2,1,0:T(8,128)(2,1)S(1)}, bf16[3,512,256]{2,1,0:T(8,128)(2,1)S(1)}) custom-call(s32[8,128]{1,0:T(8,128)S(1)} %get-tuple-element.33.x_step, f32[8,128]{1,0:T(8,128)S(1)} %get-tuple-element.34.x_taps), custom_call_target="tpu_custom_call" | custom-call | tf_op jit(solution)/shard_map/pallas_call | solution.py:105
  7.3 0.6 shard_map.57.given
  7.9 0.0 collective-permute-done.1.other_roots
  7.9 0.0 collective-permute-done.edge
  7.9 0.3 shard_map.59
  8.2 22.7 %all_to_all.10.refs_0_ = f32[8,40,8,128]{3,2,1,0:T(8,128)S(1)} all-to-all(f32[8,40,8,128]{3,2,1,0:T(8,128)S(1)} %shard_map.59), channel_id=1, replica_groups={{0,2,4,6,8,10,12,14},{16,18,20,22,24,26,28,30},{1,3,5,7,9,11,13,15},{17..., dimensions={0} | all-to-all | bytes 2621440 | tf_op jit(solution)/shard_map/all_to_all | solution.py:458
  30.9 0.9 %shard_map.60 = (f32[8,16,8,128]{3,2,1,0:T(8,128)S(1)}, f32[2,8,8,128]{3,2,1,0:T(8,128)S(1)}, f32[16,8,128]{2,1,0:T(8,128)S(1)}, f32[16,8,128]{2,1,0:T(8,128)S(1...) custom-call(f32[8,40,8,128]{3,2,1,0:T(8,128)S(1)} %all_to_all.10.ref, ...), custom_call_target="tpu_custom_call" | custom-call | tf_op jit(solution)/shard_map/pallas_call | solution.py:105
  31.8 1.2 %collective-permute-start.3 = (f32[2,8,8,128]{3,2,1,0:T(8,128)S(1)}, f32[2,8,8,128]{3,2,1,0:T(8,128)S(1)}, u32[]{:S(2)}, u32[]{:S(2)}) collective-permute-start(f32[2,8,8,128]{3,2,1,0:T(8,128)S(1)} %get-tuple-element.46.sent), channel_id=1, source_target_pairs={{0,16},{2,18},{4,20},{6,22},{8,24},{10,26},{12,28},{14,30},{16,0},... | collective-permute-start | bytes 196616 | tf_op jit(solution)/shard_map/ppermute | solution.py:455
  33.0 0.9 %shard_map.61 = (f32[8,16,8,128]{3,2,1,0:T(8,128)S(1)}, f32[2,8,8,128]{3,2,1,0:T(8,128)S(1)}) custom-call(f32[8,40,8,128]{3,2,1,0:T(8,128)S(1)} %all_to_all.10.refs_0_, bf16[3,512,256]{2,1,0:T(8,128)(2,1)S(1)} %get-tuple-element.36.refs_1_.high, bf16[3,512,256]{2,1,0:T(8,128)(2,1)S(1)} %get-tuple-element.35._.refs_2_.low, ...), custom_call_target="tpu_custom_call" | custom-call | tf_op jit(solution)/shard_map/pallas_call | solution.py:105
  33.9 1.9 %collective-permute-start.2 = (f32[2,8,8,128]{3,2,1,0:T(8,128)S(1)}, f32[2,8,8,128]{3,2,1,0:T(8,128)S(1)}, u32[]{:S(2)}, u32[]{:S(2)}) collective-permute-start(f32[2,8,8,128]{3,2,1,0:T(8,128)S(1)} %get-tuple-element.44.sent), channel_id=1, source_target_pairs={{0,16},{2,18},{4,20},{6,22},{8,24},{10,26},{12,28},{14,30},{16,0},... | collective-permute-start | bytes 196616 | tf_op jit(solution)/shard_map/ppermute | solution.py:455
  35.8 2.6 %collective-permute-done.3.received = f32[2,8,8,128]{3,2,1,0:T(8,128)S(1)} collective-permute-done((f32[2,8,8,128]{3,2,1,0:T(8,128)S(1)}, f32[2,8,8,128]{3,2,1,0:T(8,128)S(1)}, u32[]{:S(2)}, u32[]{:S(2)}) %collective-permute-start.3) | collective-permute-done | bytes 65568 | tf_op jit(solution)/shard_map/ppermute | solution.py:455
  38.4 0.9 %shard_map.62.refs_6_ = f32[8,32,8,128]{3,2,1,0:T(8,128)S(1)} custom-call(f32[8,16,8,128]{3,2,1,0:T(8,128)S(1)} %get-tuple-element.45.local, f32[2,8,8,128]{3,2,1,0:T(8,128)S(1)} %get-tuple-element.46.sent, f32[2,8,8,128]{3,2,1,0:T(8,128)S(1)} %collective-permute-done.3.received, bf16[3,512,256]{2,1,0:T(8,128)(2,1)S(1)} %get-tuple-element.36.refs_1_.high, ...), custom_call_target="tpu_custom_call" | custom-call | tf_op jit(solution)/shard_map/pallas_call | solution.py:105
  39.3 0.5 collective-permute-done.2.received
  39.8 0.9 %shard_map.63 = f32[8,32,8,128]{3,2,1,0:T(8,128)S(1)} custom-call(f32[8,16,8,128]{3,2,1,0:T(8,128)S(1)} %get-tuple-element.43.local, f32[2,8,8,128]{3,2,1,0:T(8,128)S(1)} %get-tuple-element.44.sent, f32[2,8,8,128]{3,2,1,0:T(8,128)S(1)} %collective-permute-done.2.received, bf16[3,512,256]{2,1,0:T(8,128)(2,1)S(1)} %get-tuple-element.36.refs_1_.high, ...), custom_call_target="tpu_custom_call" | custom-call | tf_op jit(solution)/shard_map/pallas_call | solution.py:105
  40.8 16.0 %all_to_all.11.pieces = f32[8,32,8,128]{3,2,1,0:T(8,128)S(1)} all-to-all(f32[8,32,8,128]{3,2,1,0:T(8,128)S(1)} %shard_map.63), channel_id=1, replica_groups={{0,2,4,6,8,10,12,14},{16,18,20,22,24,26,28,30},{1,3,5,7,9,11,13,15},{17..., dimensions={0} | all-to-all | bytes 2097152 | tf_op jit(solution)/shard_map/all_to_all | solution.py:458
  56.8 1.0 %shard_map.64 = f32[2,128,8,128]{3,2,1,0:T(8,128)} custom-call(f32[8,32,8,128]{3,2,1,0:T(8,128)S(1)} %all_to_all.11.pieces), custom_call_target="tpu_custom_call" | custom-call | tf_op jit(solution)/shard_map/pallas_call | solution.py:556
Async XLA Ops:
  1.0 6.9 %collective-permute-start = (f32[2,4,8,8,128]{4,3,2,1,0:T(8,128)S(1)}, f32[2,4,8,8,128]{4,3,2,1,0:T(8,128)S(1)}, u32[]{:S(2)}, u32[]{:S(2)}) collective-permute-start(f32[2,4,8,8,128]{4,3,2,1,0:T(8,128)S(1)} %get-tuple-element.29), channel_id=1, source_target_pairs={{0,1},{1,0},{2,3},{3,2},{4,5},{5,4},{6,7},{7,6},{8,9},{9,8},{10,11... | collective-permute-start | bytes 786440 | tf_op jit(solution)/shard_map/ppermute | solution.py:455
  1.5 6.4 %collective-permute-start.1 = (f32[4,8,128]{2,1,0:T(8,128)S(1)}, f32[4,8,128]{2,1,0:T(8,128)S(1)}, u32[]{:S(2)}, u32[]{:S(2)}) collective-permute-start(f32[4,8,128]{2,1,0:T(8,128)S(1)} %get-tuple-element.26._.roots), channel_id=1, source_target_pairs={{0,16},{2,18},{4,20},{6,22},{8,24},{10,26},{12,28},{14,30},{16,0},... | collective-permute-start | bytes 49160 | tf_op jit(solution)/shard_map/ppermute | solution.py:455
  31.8 6.6 %collective-permute-start.3 = (f32[2,8,8,128]{3,2,1,0:T(8,128)S(1)}, f32[2,8,8,128]{3,2,1,0:T(8,128)S(1)}, u32[]{:S(2)}, u32[]{:S(2)}) collective-permute-start(f32[2,8,8,128]{3,2,1,0:T(8,128)S(1)} %get-tuple-element.46.sent), channel_id=1, source_target_pairs={{0,16},{2,18},{4,20},{6,22},{8,24},{10,26},{12,28},{14,30},{16,0},... | collective-permute-start | bytes 196616 | tf_op jit(solution)/shard_map/ppermute | solution.py:455
  33.9 5.9 %collective-permute-start.2 = (f32[2,8,8,128]{3,2,1,0:T(8,128)S(1)}, f32[2,8,8,128]{3,2,1,0:T(8,128)S(1)}, u32[]{:S(2)}, u32[]{:S(2)}) collective-permute-start(f32[2,8,8,128]{3,2,1,0:T(8,128)S(1)} %get-tuple-element.44.sent), channel_id=1, source_target_pairs={{0,16},{2,18},{4,20},{6,22},{8,24},{10,26},{12,28},{14,30},{16,0},... | collective-permute-start | bytes 196616 | tf_op jit(solution)/shard_map/ppermute | solution.py:455

commit v4 on v3

--- a/solution.py
+++ b/solution.py
@@ -432,15 +432,42 @@
         filter_forth(count, planes, None, own, begin, finish)
 
 
-def place_kernel(pieces, out, sem):
-    groups, planes = pieces.shape[0], out.shape[0]
-    each = pieces.shape[1] // planes
-    for i in range(groups):
+def partner(pair):
+    groups = lax.axis_size("gz") // 2
+    m = jnp.where(lax.axis_index("gy") == 0, pair[0], pair[1])
+    return (lax.axis_index("gz") % groups) ^ m
+
+
+def split_kernel(pairs, pieces, *outs):
+    for pair, out in zip(pairs, outs):
+        out[...] = pieces[partner(pair)]
+
+
+def merge_kernel(pairs, *refs):
+    for pair, piece in zip(pairs, refs[:-1]):
+        refs[-1][partner(pair)] = piece[...]
+
+
+def place_kernel(pairs, *refs):
+    pieces, (out, sems) = refs[: len(pairs)], refs[-2:]
+    planes = out.shape[0]
+    each = pieces[0].shape[0] // planes
+    for i, (pair, piece) in enumerate(zip(pairs, pieces)):
+        at = partner(pair) * each
         for p in range(planes):
             pltpu.make_async_copy(
-                pieces.at[i, pl.ds(p * each, each)], out.at[p, pl.ds(i * each, each)], sem
+                piece.at[pl.ds(p * each, each)], out.at[p, pl.ds(at, each)], sems.at[i]
             ).start()
-    pltpu.make_async_copy(out, out, sem).wait()
+    for i, piece in enumerate(pieces):
+        pltpu.make_async_copy(piece, piece, sems.at[i]).wait()
+
+
+def exchange_order(groups):
+    order, last = [], groups - 1
+    for m in sorted(range(1, last), key=lambda m: (m.bit_count(), m)):
+        if m not in order:
+            order += [m, last ^ m]
+    return [m for i, m in enumerate(order) if m not in order[:i]] + [last]
 
 
 def grouped_body(probe_fields, root_one, root_two, lateral_kernel_taps, dilations):
@@ -449,15 +476,24 @@
     groups = places // 2
     tiles, blocks, count = rows // SUB, columns // LANES, groups * planes
     chunks = tiles // groups
-    members = [list(range(groups)), list(range(groups, places))]
 
     def across(array, axis, m):
         return lax.ppermute(array, axis, [(i, i ^ m) for i in range(lax.axis_size(axis))])
 
+    first = exchange_order(groups)
+    second = [m ^ (groups - 1) or groups - 1 for m in first]
+    pairs = [(0, 0), *zip(first, second)]
+
+    def across_pair(array, pair):
+        moves = [
+            (2 * i + core, 2 * (i ^ m) + core) for i in range(places) for core, m in enumerate(pair)
+        ]
+        return lax.ppermute(array, ("gz", "gy"), moves)
+
     def exchange(array):
-        return lax.all_to_all(
-            array, "gz", split_axis=0, concat_axis=0, axis_index_groups=members, tiled=True
-        )
+        kernel = functools.partial(split_kernel, pairs)
+        parts = call(kernel, [array.shape[1:]] * groups, [], [array])
+        return [parts[0]] + [across_pair(*part) for part in zip(parts[1:], pairs[1:])]
 
     field = probe_fields.reshape(planes, tiles, SUB, blocks, LANES).transpose(0, 1, 3, 2, 4)
     tile, halo = (SUB, LANES), 2 * MARGIN // SUB
@@ -529,7 +565,8 @@
         [],
         [*matrices[2:], edge, pieces, roots, other_roots, low],
     )
-    pieces = exchange(pieces)
+    kernel = functools.partial(merge_kernel, pairs)
+    (pieces,) = call(kernel, [piece], [], exchange(pieces))
 
     all_rows, wide = count * SUB, columns + 2 * LANES
     shared = (count, *tile)
@@ -553,14 +590,23 @@
             [message] + scratch,
             [*part, high, low, *coefficients, *out],
         )
-    out = pl.pallas_call(
-        place_kernel,
-        out_shape=pltpu.HBM((planes, tiles * blocks, *tile), jnp.float32),
-        in_specs=[vmem],
-        out_specs=hbm,
-        scratch_shapes=[pltpu.SemaphoreType.DMA],
-        compiler_params=params,
-    )(pltpu.with_memory_space_constraint(exchange(out[0]), pltpu.VMEM))
+    pieces = exchange(out[0])
+    out, half = [], groups // 2 + 1
+    for part in (slice(0, half), slice(half, groups)):
+        arrays = [pltpu.with_memory_space_constraint(a, pltpu.VMEM) for a in pieces[part]]
+        out = [
+            pl.pallas_call(
+                functools.partial(place_kernel, pairs[part]),
+                out_shape=pltpu.HBM((planes, tiles * blocks, *tile), jnp.float32),
+                in_specs=[vmem] * len(arrays) + [hbm] * len(out),
+                out_specs=hbm,
+                scratch_shapes=[pltpu.SemaphoreType.DMA((len(arrays),))],
+                input_output_aliases={len(arrays): 0} if out else {},
+                compiler_params=params,
+                cost_estimate=NO_COST,
+            )(*arrays, *out)
+        ]
+    (out,) = out
     out = out.reshape(planes, tiles, blocks, *tile).transpose(0, 1, 3, 2, 4)
     return out.reshape(probe_fields.shape)
 

time: 58 us -> 54.7 us (0.943)
  blocking collectives: 38.7 us -> 0 us
  starting transfers between devices: 7.24 us -> 32.6 us
  waiting for transfers between devices: 3.17 us -> 12.2 us
  Pallas kernels: 8.55 us -> 9.52 us
    all_to_all x2 -> x0, blocking collectives: 38.7 us -> none  [exchange(): lax.all_to_all(array, 'gz', split_axis=0, concat_axis=0, axis_index_group...]
    ppermute x0 -> x14, starting transfers between devices: none -> 25.4 us  [across_pair(): return lax.ppermute(array, ('gz', 'gy'), moves)]
    ppermute x0 -> x14, waiting for transfers between devices: none -> 9.08 us  [across_pair(): return lax.ppermute(array, ('gz', 'gy'), moves)]
    pallas_call x1 -> x2, Pallas kernels: 0.95 us -> 1.62 us  [grouped_body(): pl.pallas_call(functools.partial(place_kernel, pairs[part]), out_shape=pl...]
    pallas_call x7 -> x10, Pallas kernels: 5.36 us -> 5.66 us  [call(): pl.pallas_call(kernel, out_shape=[pltpu.VMEM(shape, dtype) for shape, dty...]
  transfers between devices with their start and end apart: 4 -> 18, of which waited for: 2 -> 7; matrix products, arithmetic and copies ran while one was open for 0% -> 0% of each run, Pallas kernels for 8% -> 10%
where the time goes in v4:
time: 54.7 us; the launch traced here: 54.5 us
  starting transfers between devices  32.6 us (60%)
  waiting for transfers between devices  12.2 us (22%)
  Pallas kernels  9.52 us (17%)
    ppermute x14, starting transfers between devices, across_pair(): return lax.ppermute(array, ('gz', 'gy'), moves)  25.4 us
    ppermute x14, waiting for transfers between devices, across_pair(): return lax.ppermute(array, ('gz', 'gy'), moves)  9.08 us
    ppermute x4, starting transfers between devices, across(): lax.ppermute(array, axis, [(i, i ^ m) for i in range(lax.axis_size(axis))])  7.23 us
    pallas_call x10, Pallas kernels, call(): pl.pallas_call(kernel, out_shape=[pltpu.VMEM(shape, dtype) for shape, dty...  5.66 us
    ppermute x4, waiting for transfers between devices, across(): lax.ppermute(array, axis, [(i, i ^ m) for i in range(lax.axis_size(axis))])  3.16 us
    pallas_call x2, Pallas kernels, grouped_body(): pl.pallas_call(functools.partial(place_kernel, pairs[part]), out_shape=pl...  1.62 us
    pallas_call x1, Pallas kernels, grouped_body(): pl.pallas_call(load_kernel, out_shape=[pltpu.VMEM((planes, tiles, blocks,...  1.23 us
  transfers between devices with their start and end apart: 18, of which 7 were waited for; matrix products, arithmetic and copies ran while one was open for 0% of the time, Pallas kernels for 10%

profile of v4, /device:TPU:0, one launch (start us, length us, event | category | flops | bytes accessed | tf_op | source)
XLA Modules:
  0.0 54.5 jit_solution(18434426994920280539)
XLA Ops:
  0.0 1.0 %shard_map.55 = (f32[2,4,8,8,128]{4,3,2,1,0:T(8,128)S(1)}, f32[4,8,128]{2,1,0:T(8,128)S(1)}) custom-call(f32[2,16,8,8,128]{4,3,2,1,0:T(8,128)} %bitcast.8, f32[2,1024]{1,0:T(2,128)} %one_ref.1, f32[2,1024]{1,0:T(2,128)} %two_ref.1), custom_call_target="tpu_custom_call" | custom-call | tf_op jit(solution)/shard_map/pallas_call | solution.py:508
  1.0 0.5 collective-permute-start
  1.5 3.7 %collective-permute-start.1 = (f32[4,8,128]{2,1,0:T(8,128)S(1)}, f32[4,8,128]{2,1,0:T(8,128)S(1)}, u32[]{:S(2)}, u32[]{:S(2)}) collective-permute-start(f32[4,8,128]{2,1,0:T(8,128)S(1)} %get-tuple-element.42._.roots), channel_id=1, source_target_pairs={{0,16},{2,18},{4,20},{6,22},{8,24},{10,26},{12,28},{14,30},{16,0},... | collective-permute-start | bytes 49160 | tf_op jit(solution)/shard_map/ppermute | solution.py:481
  5.2 1.2 %shard_map.56 = (f32[2,16,8,8,128]{4,3,2,1,0:T(8,128)S(1)}, bf16[128,128]{1,0:T(8,128)(2,1)S(1)}, bf16[128,128]{1,0:T(8,128)(2,1)S(1)}, bf16[32,32]{1,0:T(8,128)...) custom-call(f32[2,16,8,8,128]{4,3,2,1,0:T(8,128)} %bitcast.9, s32[2]{0:T(128)} %dilations_ref.1, ...), custom_call_target="tpu_custom_call" | custom-call | tf_op jit(solution)/shard_map/pallas_call | solution.py:523
  6.4 0.9 %shard_map.58 = (bf16[3,512,256]{2,1,0:T(8,128)(2,1)S(1)}, bf16[3,512,256]{2,1,0:T(8,128)(2,1)S(1)}) custom-call(s32[8,128]{1,0:T(8,128)S(1)} %get-tuple-element.49.x_step, f32[8,128]{1,0:T(8,128)S(1)} %get-tuple-element.50.x_taps), custom_call_target="tpu_custom_call" | custom-call | tf_op jit(solution)/shard_map/pallas_call | solution.py:105
  7.3 0.6 %shard_map.57.given = f32[8,32,8,128]{3,2,1,0:T(8,128)S(1)} custom-call(bf16[128,128]{1,0:T(8,128)(2,1)S(1)} %get-tuple-element.46.high, bf16[128,128]{1,0:T(8,128)(2,1)S(1)} %get-tuple-element.47.low, f32[2,16,8,8,128]{4,3,2,1,0:T(8,128)S(1)} %get-tuple-element.48.x_ref), custom_call_target="tpu_custom_call" | custom-call | tf_op jit(solution)/shard_map/pallas_call | solution.py:105
  7.9 0.0 collective-permute-done.1.other_roots
  7.9 0.0 collective-permute-done.edge
  7.9 0.3 shard_map.59.pieces
  8.2 0.1 shard_map.60
  8.3 1.6 %collective-permute-start.2 = (f32[40,8,128]{2,1,0:T(8,128)S(1)}, f32[40,8,128]{2,1,0:T(8,128)S(1)}, u32[]{:S(2)}, u32[]{:S(2)}) collective-permute-start(f32[40,8,128]{2,1,0:T(8,128)S(1)} %get-tuple-element.53), channel_id=1, source_target_pairs={{0,2},{1,13},{2,0},{3,15},{4,6},{5,9},{6,4},{7,11},{8,10},{9,5},{1... | collective-permute-start | bytes 491528 | tf_op jit(solution)/shard_map/ppermute | solution.py:491
  9.8 2.5 %collective-permute-start.3 = (f32[40,8,128]{2,1,0:T(8,128)S(1)}, f32[40,8,128]{2,1,0:T(8,128)S(1)}, u32[]{:S(2)}, u32[]{:S(2)}) collective-permute-start(f32[40,8,128]{2,1,0:T(8,128)S(1)} %get-tuple-element.54), channel_id=1, source_target_pairs={{0,12},{1,3},{2,14},{3,1},{4,8},{5,7},{6,10},{7,5},{8,4},{9,11},{1... | collective-permute-start | bytes 491528 | tf_op jit(solution)/shard_map/ppermute | solution.py:491
  12.4 0.5 collective-permute-start.4
  12.9 0.4 collective-permute-start.5
  13.3 1.6 %collective-permute-start.6 = (f32[40,8,128]{2,1,0:T(8,128)S(1)}, f32[40,8,128]{2,1,0:T(8,128)S(1)}, u32[]{:S(2)}, u32[]{:S(2)}) collective-permute-start(f32[40,8,128]{2,1,0:T(8,128)S(1)} %get-tuple-element.57), channel_id=1, source_target_pairs={{0,8},{1,7},{2,10},{3,5},{4,12},{5,3},{6,14},{7,1},{8,0},{9,15},{1... | collective-permute-start | bytes 491528 | tf_op jit(solution)/shard_map/ppermute | solution.py:491
  14.9 0.0 collective-permute-done.2.refs_1_
  14.9 4.2 %collective-permute-start.7 = (f32[40,8,128]{2,1,0:T(8,128)S(1)}, f32[40,8,128]{2,1,0:T(8,128)S(1)}, u32[]{:S(2)}, u32[]{:S(2)}) collective-permute-start(f32[40,8,128]{2,1,0:T(8,128)S(1)} %get-tuple-element.58), channel_id=1, source_target_pairs={{0,6},{1,9},{2,4},{3,11},{4,2},{5,13},{6,0},{7,15},{8,14},{9,1},{1... | collective-permute-start | bytes 491528 | tf_op jit(solution)/shard_map/ppermute | solution.py:491
  19.1 0.0 collective-permute-done.3.refs_2_
  19.1 2.3 %collective-permute-start.8 = (f32[40,8,128]{2,1,0:T(8,128)S(1)}, f32[40,8,128]{2,1,0:T(8,128)S(1)}, u32[]{:S(2)}, u32[]{:S(2)}) collective-permute-start(f32[40,8,128]{2,1,0:T(8,128)S(1)} %get-tuple-element.59), channel_id=1, source_target_pairs={{0,14},{1,15},{2,12},{3,13},{4,10},{5,11},{6,8},{7,9},{8,6},{9,7},... | collective-permute-start | bytes 491528 | tf_op jit(solution)/shard_map/ppermute | solution.py:491
  21.4 0.0 collective-permute-done.4.refs_3_
  21.4 0.0 collective-permute-done.5.refs_4_
  21.4 2.5 %collective-permute-done.6.refs_5_ = f32[40,8,128]{2,1,0:T(8,128)S(1)} collective-permute-done((f32[40,8,128]{2,1,0:T(8,128)S(1)}, f32[40,8,128]{2,1,0:T(8,128)S(1)}, u32[]{:S(2)}, u32[]{:S(2)}) %collective-permute-start.6) | collective-permute-done | bytes 163872 | tf_op jit(solution)/shard_map/ppermute | solution.py:491
  23.9 0.7 %collective-permute-done.7.refs_6_ = f32[40,8,128]{2,1,0:T(8,128)S(1)} collective-permute-done((f32[40,8,128]{2,1,0:T(8,128)S(1)}, f32[40,8,128]{2,1,0:T(8,128)S(1)}, u32[]{:S(2)}, u32[]{:S(2)}) %collective-permute-start.7) | collective-permute-done | bytes 163872 | tf_op jit(solution)/shard_map/ppermute | solution.py:491
  24.6 2.4 %collective-permute-done.8.refs_7_ = f32[40,8,128]{2,1,0:T(8,128)S(1)} collective-permute-done((f32[40,8,128]{2,1,0:T(8,128)S(1)}, f32[40,8,128]{2,1,0:T(8,128)S(1)}, u32[]{:S(2)}, u32[]{:S(2)}) %collective-permute-start.8) | collective-permute-done | bytes 163872 | tf_op jit(solution)/shard_map/ppermute | solution.py:491
  27.1 0.1 shard_map.61.refs_0_
  27.2 0.9 %shard_map.62 = (f32[8,16,8,128]{3,2,1,0:T(8,128)S(1)}, f32[2,8,8,128]{3,2,1,0:T(8,128)S(1)}, f32[16,8,128]{2,1,0:T(8,128)S(1)}, f32[16,8,128]{2,1,0:T(8,128)S(1...) custom-call(f32[8,40,8,128]{3,2,1,0:T(8,128)S(1)} %shard_map.61.refs, ...), custom_call_target="tpu_custom_call" | custom-call | tf_op jit(solution)/shard_map/pallas_call | solution.py:105
  28.1 1.9 %collective-permute-start.10 = (f32[2,8,8,128]{3,2,1,0:T(8,128)S(1)}, f32[2,8,8,128]{3,2,1,0:T(8,128)S(1)}, u32[]{:S(2)}, u32[]{:S(2)}) collective-permute-start(f32[2,8,8,128]{3,2,1,0:T(8,128)S(1)} %get-tuple-element.70.sent), channel_id=1, source_target_pairs={{0,16},{2,18},{4,20},{6,22},{8,24},{10,26},{12,28},{14,30},{16,0},... | collective-permute-start | bytes 196616 | tf_op jit(solution)/shard_map/ppermute | solution.py:481
  30.0 0.9 %shard_map.63 = (f32[8,16,8,128]{3,2,1,0:T(8,128)S(1)}, f32[2,8,8,128]{3,2,1,0:T(8,128)S(1)}) custom-call(f32[8,40,8,128]{3,2,1,0:T(8,128)S(1)} %shard_map.61.refs_0_, bf16[3,512,256]{2,1,0:T(8,128)(2,1)S(1)} %get-tuple-element.60.refs_1_.high, bf16[3,512,256]{2,1,0:T(8,128)(2,1)S(1)} %get-tuple-element.51._.refs_2_.low, ...), custom_call_target="tpu_custom_call" | custom-call | tf_op jit(solution)/shard_map/pallas_call | solution.py:105
  30.9 1.2 %collective-permute-start.9 = (f32[2,8,8,128]{3,2,1,0:T(8,128)S(1)}, f32[2,8,8,128]{3,2,1,0:T(8,128)S(1)}, u32[]{:S(2)}, u32[]{:S(2)}) collective-permute-start(f32[2,8,8,128]{3,2,1,0:T(8,128)S(1)} %get-tuple-element.68.sent), channel_id=1, source_target_pairs={{0,16},{2,18},{4,20},{6,22},{8,24},{10,26},{12,28},{14,30},{16,0},... | collective-permute-start | bytes 196616 | tf_op jit(solution)/shard_map/ppermute | solution.py:481
  32.1 1.8 %collective-permute-done.10.received = f32[2,8,8,128]{3,2,1,0:T(8,128)S(1)} collective-permute-done((f32[2,8,8,128]{3,2,1,0:T(8,128)S(1)}, f32[2,8,8,128]{3,2,1,0:T(8,128)S(1)}, u32[]{:S(2)}, u32[]{:S(2)}) %collective-permute-start.10) | collective-permute-done | bytes 65568 | tf_op jit(solution)/shard_map/ppermute | solution.py:481
  33.9 0.9 %shard_map.64.refs_6_ = f32[8,32,8,128]{3,2,1,0:T(8,128)S(1)} custom-call(f32[8,16,8,128]{3,2,1,0:T(8,128)S(1)} %get-tuple-element.69.local, f32[2,8,8,128]{3,2,1,0:T(8,128)S(1)} %get-tuple-element.70.sent, f32[2,8,8,128]{3,2,1,0:T(8,128)S(1)} %collective-permute-done.10.received, bf16[3,512,256]{2,1,0:T(8,128)(2,1)S(1)} %get-tuple-element.60.refs_1_.high, ...), custom_call_target="tpu_custom_call" | custom-call | tf_op jit(solution)/shard_map/pallas_call | solution.py:105
  34.8 1.3 %collective-permute-done.9.received = f32[2,8,8,128]{3,2,1,0:T(8,128)S(1)} collective-permute-done((f32[2,8,8,128]{3,2,1,0:T(8,128)S(1)}, f32[2,8,8,128]{3,2,1,0:T(8,128)S(1)}, u32[]{:S(2)}, u32[]{:S(2)}) %collective-permute-start.9) | collective-permute-done | bytes 65568 | tf_op jit(solution)/shard_map/ppermute | solution.py:481
  36.1 0.9 %shard_map.65.pieces = f32[8,32,8,128]{3,2,1,0:T(8,128)S(1)} custom-call(f32[8,16,8,128]{3,2,1,0:T(8,128)S(1)} %get-tuple-element.67.local, f32[2,8,8,128]{3,2,1,0:T(8,128)S(1)} %get-tuple-element.68.sent, f32[2,8,8,128]{3,2,1,0:T(8,128)S(1)} %collective-permute-done.9.received, bf16[3,512,256]{2,1,0:T(8,128)(2,1)S(1)} %get-tuple-element.60.refs_1_.high, ...), custom_call_target="tpu_custom_call" | custom-call | tf_op jit(solution)/shard_map/pallas_call | solution.py:105
  37.1 0.1 shard_map.66
  37.2 1.1 %collective-permute-start.14 = (f32[32,8,128]{2,1,0:T(8,128)S(1)}, f32[32,8,128]{2,1,0:T(8,128)S(1)}, u32[]{:S(2)}, u32[]{:S(2)}) collective-permute-start(f32[32,8,128]{2,1,0:T(8,128)S(1)} %get-tuple-element.75), channel_id=1, source_target_pairs={{0,2},{1,13},{2,0},{3,15},{4,6},{5,9},{6,4},{7,11},{8,10},{9,5},{1... | collective-permute-start | bytes 393224 | tf_op jit(solution)/shard_map/ppermute | solution.py:491
  38.3 2.7 %collective-permute-start.15 = (f32[32,8,128]{2,1,0:T(8,128)S(1)}, f32[32,8,128]{2,1,0:T(8,128)S(1)}, u32[]{:S(2)}, u32[]{:S(2)}) collective-permute-start(f32[32,8,128]{2,1,0:T(8,128)S(1)} %get-tuple-element.76), channel_id=1, source_target_pairs={{0,12},{1,3},{2,14},{3,1},{4,8},{5,7},{6,10},{7,5},{8,4},{9,11},{1... | collective-permute-start | bytes 393224 | tf_op jit(solution)/shard_map/ppermute | solution.py:491
  41.0 0.5 collective-permute-start.11
  41.5 0.3 collective-permute-start.16
  41.8 3.2 %collective-permute-start.17 = (f32[32,8,128]{2,1,0:T(8,128)S(1)}, f32[32,8,128]{2,1,0:T(8,128)S(1)}, u32[]{:S(2)}, u32[]{:S(2)}) collective-permute-start(f32[32,8,128]{2,1,0:T(8,128)S(1)} %get-tuple-element.78), channel_id=1, source_target_pairs={{0,10},{1,5},{2,8},{3,7},{4,14},{5,1},{6,12},{7,3},{8,2},{9,13},{1... | collective-permute-start | bytes 393224 | tf_op jit(solution)/shard_map/ppermute | solution.py:491
  45.0 0.0 collective-permute-done.14.refs_1_
  45.0 1.1 %collective-permute-start.12 = (f32[32,8,128]{2,1,0:T(8,128)S(1)}, f32[32,8,128]{2,1,0:T(8,128)S(1)}, u32[]{:S(2)}, u32[]{:S(2)}) collective-permute-start(f32[32,8,128]{2,1,0:T(8,128)S(1)} %get-tuple-element.72), channel_id=1, source_target_pairs={{0,6},{1,9},{2,4},{3,11},{4,2},{5,13},{6,0},{7,15},{8,14},{9,1},{1... | collective-permute-start | bytes 393224 | tf_op jit(solution)/shard_map/ppermute | solution.py:491
  46.1 0.0 collective-permute-done.15.refs_2_
  46.1 3.4 %collective-permute-start.13 = (f32[32,8,128]{2,1,0:T(8,128)S(1)}, f32[32,8,128]{2,1,0:T(8,128)S(1)}, u32[]{:S(2)}, u32[]{:S(2)}) collective-permute-start(f32[32,8,128]{2,1,0:T(8,128)S(1)} %get-tuple-element.73), channel_id=1, source_target_pairs={{0,14},{1,15},{2,12},{3,13},{4,10},{5,11},{6,8},{7,9},{8,6},{9,7},... | collective-permute-start | bytes 393224 | tf_op jit(solution)/shard_map/ppermute | solution.py:491
  49.5 0.0 collective-permute-done.16.refs_3_
  49.5 1.5 %collective-permute-done.17.refs_4_ = f32[32,8,128]{2,1,0:T(8,128)S(1)} collective-permute-done((f32[32,8,128]{2,1,0:T(8,128)S(1)}, f32[32,8,128]{2,1,0:T(8,128)S(1)}, u32[]{:S(2)}, u32[]{:S(2)}) %collective-permute-start.17) | collective-permute-done | bytes 131104 | tf_op jit(solution)/shard_map/ppermute | solution.py:491
  51.0 0.9 %shard_map.67.refs_3_ = f32[2,128,8,128]{3,2,1,0:T(8,128)} custom-call(f32[32,8,128]{2,1,0:T(8,128)S(1)} %get-tuple-element.74.refs_0_, f32[32,8,128]{2,1,0:T(8,128)S(1)} %collective-permute-done.14.refs_1_, f32[32,8,128]{2,1,0:T(8,128)S(1)} %collective-permute-done.15.refs_2_, f32[32,8,128]{2,1,0:T(8,128)S(1)} %collective-permute-done.16.refs_3_, ...), custom_call_target="tpu_custom_call" | custom-call | tf_op jit(solution)/shard_map/pallas_call | solution.py:598
  51.9 0.0 collective-permute-done.11.refs_0_
  51.9 1.9 %collective-permute-done.12.refs_1_ = f32[32,8,128]{2,1,0:T(8,128)S(1)} collective-permute-done((f32[32,8,128]{2,1,0:T(8,128)S(1)}, f32[32,8,128]{2,1,0:T(8,128)S(1)}, u32[]{:S(2)}, u32[]{:S(2)}) %collective-permute-start.12) | collective-permute-done | bytes 131104 | tf_op jit(solution)/shard_map/ppermute | solution.py:491
  53.7 0.0 collective-permute-done.13.refs_2_
  53.7 0.8 %shard_map.68 = f32[2,128,8,128]{3,2,1,0:T(8,128)} custom-call(f32[32,8,128]{2,1,0:T(8,128)S(1)} %collective-permute-done.11.refs_0_, f32[32,8,128]{2,1,0:T(8,128)S(1)} %collective-permute-done.12.refs_1_, f32[32,8,128]{2,1,0:T(8,128)S(1)} %collective-permute-done.13.refs_2_, f32[2,128,8,128]{3,2,1,0:T(8,128)} %shard_map.67.refs_3_), custom_call_target="tpu_custom_call", output_to_operand_aliasing={{}: (3, {})} | custom-call | tf_op jit(solution)/shard_map/pallas_call | solution.py:598
Async XLA Ops:
  1.0 6.9 %collective-permute-start = (f32[2,4,8,8,128]{4,3,2,1,0:T(8,128)S(1)}, f32[2,4,8,8,128]{4,3,2,1,0:T(8,128)S(1)}, u32[]{:S(2)}, u32[]{:S(2)}) collective-permute-start(f32[2,4,8,8,128]{4,3,2,1,0:T(8,128)S(1)} %get-tuple-element.45), channel_id=1, source_target_pairs={{0,1},{1,0},{2,3},{3,2},{4,5},{5,4},{6,7},{7,6},{8,9},{9,8},{10,11... | collective-permute-start | bytes 786440 | tf_op jit(solution)/shard_map/ppermute | solution.py:481
  1.5 6.4 %collective-permute-start.1 = (f32[4,8,128]{2,1,0:T(8,128)S(1)}, f32[4,8,128]{2,1,0:T(8,128)S(1)}, u32[]{:S(2)}, u32[]{:S(2)}) collective-permute-start(f32[4,8,128]{2,1,0:T(8,128)S(1)} %get-tuple-element.42._.roots), channel_id=1, source_target_pairs={{0,16},{2,18},{4,20},{6,22},{8,24},{10,26},{12,28},{14,30},{16,0},... | collective-permute-start | bytes 49160 | tf_op jit(solution)/shard_map/ppermute | solution.py:481
  8.3 6.6 %collective-permute-start.2 = (f32[40,8,128]{2,1,0:T(8,128)S(1)}, f32[40,8,128]{2,1,0:T(8,128)S(1)}, u32[]{:S(2)}, u32[]{:S(2)}) collective-permute-start(f32[40,8,128]{2,1,0:T(8,128)S(1)} %get-tuple-element.53), channel_id=1, source_target_pairs={{0,2},{1,13},{2,0},{3,15},{4,6},{5,9},{6,4},{7,11},{8,10},{9,5},{1... | collective-permute-start | bytes 491528 | tf_op jit(solution)/shard_map/ppermute | solution.py:491
  9.8 9.2 %collective-permute-start.3 = (f32[40,8,128]{2,1,0:T(8,128)S(1)}, f32[40,8,128]{2,1,0:T(8,128)S(1)}, u32[]{:S(2)}, u32[]{:S(2)}) collective-permute-start(f32[40,8,128]{2,1,0:T(8,128)S(1)} %get-tuple-element.54), channel_id=1, source_target_pairs={{0,12},{1,3},{2,14},{3,1},{4,8},{5,7},{6,10},{7,5},{8,4},{9,11},{1... | collective-permute-start | bytes 491528 | tf_op jit(solution)/shard_map/ppermute | solution.py:491
  12.4 9.0 %collective-permute-start.4 = (f32[40,8,128]{2,1,0:T(8,128)S(1)}, f32[40,8,128]{2,1,0:T(8,128)S(1)}, u32[]{:S(2)}, u32[]{:S(2)}) collective-permute-start(f32[40,8,128]{2,1,0:T(8,128)S(1)} %get-tuple-element.55), channel_id=1, source_target_pairs={{0,4},{1,11},{2,6},{3,9},{4,0},{5,15},{6,2},{7,13},{8,12},{9,3},{1... | collective-permute-start | bytes 491528 | tf_op jit(solution)/shard_map/ppermute | solution.py:491
  12.9 8.5 %collective-permute-start.5 = (f32[40,8,128]{2,1,0:T(8,128)S(1)}, f32[40,8,128]{2,1,0:T(8,128)S(1)}, u32[]{:S(2)}, u32[]{:S(2)}) collective-permute-start(f32[40,8,128]{2,1,0:T(8,128)S(1)} %get-tuple-element.56), channel_id=1, source_target_pairs={{0,10},{1,5},{2,8},{3,7},{4,14},{5,1},{6,12},{7,3},{8,2},{9,13},{1... | collective-permute-start | bytes 491528 | tf_op jit(solution)/shard_map/ppermute | solution.py:491
  13.3 10.6 %collective-permute-start.6 = (f32[40,8,128]{2,1,0:T(8,128)S(1)}, f32[40,8,128]{2,1,0:T(8,128)S(1)}, u32[]{:S(2)}, u32[]{:S(2)}) collective-permute-start(f32[40,8,128]{2,1,0:T(8,128)S(1)} %get-tuple-element.57), channel_id=1, source_target_pairs={{0,8},{1,7},{2,10},{3,5},{4,12},{5,3},{6,14},{7,1},{8,0},{9,15},{1... | collective-permute-start | bytes 491528 | tf_op jit(solution)/shard_map/ppermute | solution.py:491
  14.9 9.8 %collective-permute-start.7 = (f32[40,8,128]{2,1,0:T(8,128)S(1)}, f32[40,8,128]{2,1,0:T(8,128)S(1)}, u32[]{:S(2)}, u32[]{:S(2)}) collective-permute-start(f32[40,8,128]{2,1,0:T(8,128)S(1)} %get-tuple-element.58), channel_id=1, source_target_pairs={{0,6},{1,9},{2,4},{3,11},{4,2},{5,13},{6,0},{7,15},{8,14},{9,1},{1... | collective-permute-start | bytes 491528 | tf_op jit(solution)/shard_map/ppermute | solution.py:491
  19.1 8.0 %collective-permute-start.8 = (f32[40,8,128]{2,1,0:T(8,128)S(1)}, f32[40,8,128]{2,1,0:T(8,128)S(1)}, u32[]{:S(2)}, u32[]{:S(2)}) collective-permute-start(f32[40,8,128]{2,1,0:T(8,128)S(1)} %get-tuple-element.59), channel_id=1, source_target_pairs={{0,14},{1,15},{2,12},{3,13},{4,10},{5,11},{6,8},{7,9},{8,6},{9,7},... | collective-permute-start | bytes 491528 | tf_op jit(solution)/shard_map/ppermute | solution.py:491
  28.1 5.8 %collective-permute-start.10 = (f32[2,8,8,128]{3,2,1,0:T(8,128)S(1)}, f32[2,8,8,128]{3,2,1,0:T(8,128)S(1)}, u32[]{:S(2)}, u32[]{:S(2)}) collective-permute-start(f32[2,8,8,128]{3,2,1,0:T(8,128)S(1)} %get-tuple-element.70.sent), channel_id=1, source_target_pairs={{0,16},{2,18},{4,20},{6,22},{8,24},{10,26},{12,28},{14,30},{16,0},... | collective-permute-start | bytes 196616 | tf_op jit(solution)/shard_map/ppermute | solution.py:481
  30.9 5.2 %collective-permute-start.9 = (f32[2,8,8,128]{3,2,1,0:T(8,128)S(1)}, f32[2,8,8,128]{3,2,1,0:T(8,128)S(1)}, u32[]{:S(2)}, u32[]{:S(2)}) collective-permute-start(f32[2,8,8,128]{3,2,1,0:T(8,128)S(1)} %get-tuple-element.68.sent), channel_id=1, source_target_pairs={{0,16},{2,18},{4,20},{6,22},{8,24},{10,26},{12,28},{14,30},{16,0},... | collective-permute-start | bytes 196616 | tf_op jit(solution)/shard_map/ppermute | solution.py:481
  37.2 7.8 %collective-permute-start.14 = (f32[32,8,128]{2,1,0:T(8,128)S(1)}, f32[32,8,128]{2,1,0:T(8,128)S(1)}, u32[]{:S(2)}, u32[]{:S(2)}) collective-permute-start(f32[32,8,128]{2,1,0:T(8,128)S(1)} %get-tuple-element.75), channel_id=1, source_target_pairs={{0,2},{1,13},{2,0},{3,15},{4,6},{5,9},{6,4},{7,11},{8,10},{9,5},{1... | collective-permute-start | bytes 393224 | tf_op jit(solution)/shard_map/ppermute | solution.py:491
  38.3 7.8 %collective-permute-start.15 = (f32[32,8,128]{2,1,0:T(8,128)S(1)}, f32[32,8,128]{2,1,0:T(8,128)S(1)}, u32[]{:S(2)}, u32[]{:S(2)}) collective-permute-start(f32[32,8,128]{2,1,0:T(8,128)S(1)} %get-tuple-element.76), channel_id=1, source_target_pairs={{0,12},{1,3},{2,14},{3,1},{4,8},{5,7},{6,10},{7,5},{8,4},{9,11},{1... | collective-permute-start | bytes 393224 | tf_op jit(solution)/shard_map/ppermute | solution.py:491
  41.0 10.9 %collective-permute-start.11 = (f32[32,8,128]{2,1,0:T(8,128)S(1)}, f32[32,8,128]{2,1,0:T(8,128)S(1)}, u32[]{:S(2)}, u32[]{:S(2)}) collective-permute-start(f32[32,8,128]{2,1,0:T(8,128)S(1)} %get-tuple-element.71), channel_id=1, source_target_pairs={{0,8},{1,7},{2,10},{3,5},{4,12},{5,3},{6,14},{7,1},{8,0},{9,15},{1... | collective-permute-start | bytes 393224 | tf_op jit(solution)/shard_map/ppermute | solution.py:491
  41.5 8.0 %collective-permute-start.16 = (f32[32,8,128]{2,1,0:T(8,128)S(1)}, f32[32,8,128]{2,1,0:T(8,128)S(1)}, u32[]{:S(2)}, u32[]{:S(2)}) collective-permute-start(f32[32,8,128]{2,1,0:T(8,128)S(1)} %get-tuple-element.77), channel_id=1, source_target_pairs={{0,4},{1,11},{2,6},{3,9},{4,0},{5,15},{6,2},{7,13},{8,12},{9,3},{1... | collective-permute-start | bytes 393224 | tf_op jit(solution)/shard_map/ppermute | solution.py:491
  41.8 9.2 %collective-permute-start.17 = (f32[32,8,128]{2,1,0:T(8,128)S(1)}, f32[32,8,128]{2,1,0:T(8,128)S(1)}, u32[]{:S(2)}, u32[]{:S(2)}) collective-permute-start(f32[32,8,128]{2,1,0:T(8,128)S(1)} %get-tuple-element.78), channel_id=1, source_target_pairs={{0,10},{1,5},{2,8},{3,7},{4,14},{5,1},{6,12},{7,3},{8,2},{9,13},{1... | collective-permute-start | bytes 393224 | tf_op jit(solution)/shard_map/ppermute | solution.py:491
  45.0 8.8 %collective-permute-start.12 = (f32[32,8,128]{2,1,0:T(8,128)S(1)}, f32[32,8,128]{2,1,0:T(8,128)S(1)}, u32[]{:S(2)}, u32[]{:S(2)}) collective-permute-start(f32[32,8,128]{2,1,0:T(8,128)S(1)} %get-tuple-element.72), channel_id=1, source_target_pairs={{0,6},{1,9},{2,4},{3,11},{4,2},{5,13},{6,0},{7,15},{8,14},{9,1},{1... | collective-permute-start | bytes 393224 | tf_op jit(solution)/shard_map/ppermute | solution.py:491
  46.1 7.6 %collective-permute-start.13 = (f32[32,8,128]{2,1,0:T(8,128)S(1)}, f32[32,8,128]{2,1,0:T(8,128)S(1)}, u32[]{:S(2)}, u32[]{:S(2)}) collective-permute-start(f32[32,8,128]{2,1,0:T(8,128)S(1)} %get-tuple-element.73), channel_id=1, source_target_pairs={{0,14},{1,15},{2,12},{3,13},{4,10},{5,11},{6,8},{7,9},{8,6},{9,7},... | collective-permute-start | bytes 393224 | tf_op jit(solution)/shard_map/ppermute | solution.py:491

commit v5 on v4

--- a/solution.py
+++ b/solution.py
@@ -482,7 +482,8 @@
 
     first = exchange_order(groups)
     second = [m ^ (groups - 1) or groups - 1 for m in first]
-    pairs = [(0, 0), *zip(first, second)]
+    pairs_in = [(0, 0), *zip(first, second)]
+    pairs_out = [(m, m) for m in (0, *first)]
 
     def across_pair(array, pair):
         moves = [
@@ -490,7 +491,7 @@
         ]
         return lax.ppermute(array, ("gz", "gy"), moves)
 
-    def exchange(array):
+    def exchange(array, pairs):
         kernel = functools.partial(split_kernel, pairs)
         parts = call(kernel, [array.shape[1:]] * groups, [], [array])
         return [parts[0]] + [across_pair(*part) for part in zip(parts[1:], pairs[1:])]
@@ -565,8 +566,8 @@
         [],
         [*matrices[2:], edge, pieces, roots, other_roots, low],
     )
-    kernel = functools.partial(merge_kernel, pairs)
-    (pieces,) = call(kernel, [piece], [], exchange(pieces))
+    kernel = functools.partial(merge_kernel, pairs_in)
+    (pieces,) = call(kernel, [piece], [], exchange(pieces, pairs_in))
 
     all_rows, wide = count * SUB, columns + 2 * LANES
     shared = (count, *tile)
@@ -590,13 +591,13 @@
             [message] + scratch,
             [*part, high, low, *coefficients, *out],
         )
-    pieces = exchange(out[0])
+    pieces = exchange(out[0], pairs_out)
     out, half = [], groups // 2 + 1
     for part in (slice(0, half), slice(half, groups)):
         arrays = [pltpu.with_memory_space_constraint(a, pltpu.VMEM) for a in pieces[part]]
         out = [
             pl.pallas_call(
-                functools.partial(place_kernel, pairs[part]),
+                functools.partial(place_kernel, pairs_out[part]),
                 out_shape=pltpu.HBM((planes, tiles * blocks, *tile), jnp.float32),
                 in_specs=[vmem] * len(arrays) + [hbm] * len(out),
                 out_specs=hbm,

time: 54.7 us -> 54 us (0.987)
  starting transfers between devices: 32.6 us -> 31.6 us
    ppermute x14, starting transfers between devices: 25.4 us -> 24.4 us  [across_pair(): return lax.ppermute(array, ('gz', 'gy'), moves)]
  transfers between devices with their start and end apart: 18 -> 18, of which waited for: 7 -> 8; matrix products, arithmetic and copies ran while one was open for 0% -> 0% of each run, Pallas kernels for 10% -> 10%
where the time goes in v5:
time: 54 us; the launch traced here: 53.8 us
  starting transfers between devices  31.6 us (59%)
  waiting for transfers between devices  12.5 us (23%)
  Pallas kernels  9.52 us (18%)
    ppermute x14, starting transfers between devices, across_pair(): return lax.ppermute(array, ('gz', 'gy'), moves)  24.4 us
    ppermute x14, waiting for transfers between devices, across_pair(): return lax.ppermute(array, ('gz', 'gy'), moves)  9.36 us
    ppermute x4, starting transfers between devices, across(): lax.ppermute(array, axis, [(i, i ^ m) for i in range(lax.axis_size(axis))])  7.23 us
    pallas_call x10, Pallas kernels, call(): pl.pallas_call(kernel, out_shape=[pltpu.VMEM(shape, dtype) for shape, dty...  5.66 us
    ppermute x4, waiting for transfers between devices, across(): lax.ppermute(array, axis, [(i, i ^ m) for i in range(lax.axis_size(axis))])  3.16 us
    pallas_call x2, Pallas kernels, grouped_body(): pl.pallas_call(functools.partial(place_kernel, pairs_out[part]), out_shap...  1.62 us
    pallas_call x1, Pallas kernels, grouped_body(): pl.pallas_call(load_kernel, out_shape=[pltpu.VMEM((planes, tiles, blocks,...  1.23 us
  transfers between devices with their start and end apart: 18, of which 8 were waited for; matrix products, arithmetic and copies ran while one was open for 0% of the time, Pallas kernels for 10%

profile of v5, /device:TPU:0, one launch (start us, length us, event | category | flops | bytes accessed | tf_op | source)
XLA Modules:
  0.0 53.8 jit_solution(18148010681097162551)
XLA Ops:
  0.0 1.0 %shard_map.55 = (f32[2,4,8,8,128]{4,3,2,1,0:T(8,128)S(1)}, f32[4,8,128]{2,1,0:T(8,128)S(1)}) custom-call(f32[2,16,8,8,128]{4,3,2,1,0:T(8,128)} %bitcast.8, f32[2,1024]{1,0:T(2,128)} %one_ref.1, f32[2,1024]{1,0:T(2,128)} %two_ref.1), custom_call_target="tpu_custom_call" | custom-call | tf_op jit(solution)/shard_map/pallas_call | solution.py:509
  1.0 0.5 collective-permute-start
  1.5 3.7 %collective-permute-start.1 = (f32[4,8,128]{2,1,0:T(8,128)S(1)}, f32[4,8,128]{2,1,0:T(8,128)S(1)}, u32[]{:S(2)}, u32[]{:S(2)}) collective-permute-start(f32[4,8,128]{2,1,0:T(8,128)S(1)} %get-tuple-element.42._.roots), channel_id=1, source_target_pairs={{0,16},{2,18},{4,20},{6,22},{8,24},{10,26},{12,28},{14,30},{16,0},... | collective-permute-start | bytes 49160 | tf_op jit(solution)/shard_map/ppermute | solution.py:481
  5.2 1.2 %shard_map.56 = (f32[2,16,8,8,128]{4,3,2,1,0:T(8,128)S(1)}, bf16[128,128]{1,0:T(8,128)(2,1)S(1)}, bf16[128,128]{1,0:T(8,128)(2,1)S(1)}, bf16[32,32]{1,0:T(8,128)...) custom-call(f32[2,16,8,8,128]{4,3,2,1,0:T(8,128)} %bitcast.9, s32[2]{0:T(128)} %dilations_ref.1, ...), custom_call_target="tpu_custom_call" | custom-call | tf_op jit(solution)/shard_map/pallas_call | solution.py:524
  6.4 0.9 %shard_map.58 = (bf16[3,512,256]{2,1,0:T(8,128)(2,1)S(1)}, bf16[3,512,256]{2,1,0:T(8,128)(2,1)S(1)}) custom-call(s32[8,128]{1,0:T(8,128)S(1)} %get-tuple-element.49.x_step, f32[8,128]{1,0:T(8,128)S(1)} %get-tuple-element.50.x_taps), custom_call_target="tpu_custom_call" | custom-call | tf_op jit(solution)/shard_map/pallas_call | solution.py:105
  7.3 0.6 %shard_map.57.given = f32[8,32,8,128]{3,2,1,0:T(8,128)S(1)} custom-call(bf16[128,128]{1,0:T(8,128)(2,1)S(1)} %get-tuple-element.46.high, bf16[128,128]{1,0:T(8,128)(2,1)S(1)} %get-tuple-element.47.low, f32[2,16,8,8,128]{4,3,2,1,0:T(8,128)S(1)} %get-tuple-element.48.x_ref), custom_call_target="tpu_custom_call" | custom-call | tf_op jit(solution)/shard_map/pallas_call | solution.py:105
  7.9 0.0 collective-permute-done.1.other_roots
  7.9 0.0 collective-permute-done.edge
  7.9 0.3 shard_map.59.pieces
  8.2 0.1 shard_map.60
  8.3 1.6 %collective-permute-start.2 = (f32[40,8,128]{2,1,0:T(8,128)S(1)}, f32[40,8,128]{2,1,0:T(8,128)S(1)}, u32[]{:S(2)}, u32[]{:S(2)}) collective-permute-start(f32[40,8,128]{2,1,0:T(8,128)S(1)} %get-tuple-element.53), channel_id=1, source_target_pairs={{0,2},{1,13},{2,0},{3,15},{4,6},{5,9},{6,4},{7,11},{8,10},{9,5},{1... | collective-permute-start | bytes 491528 | tf_op jit(solution)/shard_map/ppermute | solution.py:492
  9.8 2.5 %collective-permute-start.3 = (f32[40,8,128]{2,1,0:T(8,128)S(1)}, f32[40,8,128]{2,1,0:T(8,128)S(1)}, u32[]{:S(2)}, u32[]{:S(2)}) collective-permute-start(f32[40,8,128]{2,1,0:T(8,128)S(1)} %get-tuple-element.54), channel_id=1, source_target_pairs={{0,12},{1,3},{2,14},{3,1},{4,8},{5,7},{6,10},{7,5},{8,4},{9,11},{1... | collective-permute-start | bytes 491528 | tf_op jit(solution)/shard_map/ppermute | solution.py:492
  12.4 0.5 collective-permute-start.4
  12.9 0.4 collective-permute-start.5
  13.3 1.6 %collective-permute-start.6 = (f32[40,8,128]{2,1,0:T(8,128)S(1)}, f32[40,8,128]{2,1,0:T(8,128)S(1)}, u32[]{:S(2)}, u32[]{:S(2)}) collective-permute-start(f32[40,8,128]{2,1,0:T(8,128)S(1)} %get-tuple-element.57), channel_id=1, source_target_pairs={{0,8},{1,7},{2,10},{3,5},{4,12},{5,3},{6,14},{7,1},{8,0},{9,15},{1... | collective-permute-start | bytes 491528 | tf_op jit(solution)/shard_map/ppermute | solution.py:492
  14.9 0.0 collective-permute-done.2.refs_1_
  14.9 4.2 %collective-permute-start.7 = (f32[40,8,128]{2,1,0:T(8,128)S(1)}, f32[40,8,128]{2,1,0:T(8,128)S(1)}, u32[]{:S(2)}, u32[]{:S(2)}) collective-permute-start(f32[40,8,128]{2,1,0:T(8,128)S(1)} %get-tuple-element.58), channel_id=1, source_target_pairs={{0,6},{1,9},{2,4},{3,11},{4,2},{5,13},{6,0},{7,15},{8,14},{9,1},{1... | collective-permute-start | bytes 491528 | tf_op jit(solution)/shard_map/ppermute | solution.py:492
  19.1 0.0 collective-permute-done.3.refs_2_
  19.1 2.3 %collective-permute-start.8 = (f32[40,8,128]{2,1,0:T(8,128)S(1)}, f32[40,8,128]{2,1,0:T(8,128)S(1)}, u32[]{:S(2)}, u32[]{:S(2)}) collective-permute-start(f32[40,8,128]{2,1,0:T(8,128)S(1)} %get-tuple-element.59), channel_id=1, source_target_pairs={{0,14},{1,15},{2,12},{3,13},{4,10},{5,11},{6,8},{7,9},{8,6},{9,7},... | collective-permute-start | bytes 491528 | tf_op jit(solution)/shard_map/ppermute | solution.py:492
  21.4 0.0 collective-permute-done.4.refs_3_
  21.4 0.0 collective-permute-done.5.refs_4_
  21.4 2.5 %collective-permute-done.6.refs_5_ = f32[40,8,128]{2,1,0:T(8,128)S(1)} collective-permute-done((f32[40,8,128]{2,1,0:T(8,128)S(1)}, f32[40,8,128]{2,1,0:T(8,128)S(1)}, u32[]{:S(2)}, u32[]{:S(2)}) %collective-permute-start.6) | collective-permute-done | bytes 163872 | tf_op jit(solution)/shard_map/ppermute | solution.py:492
  23.9 0.7 %collective-permute-done.7.refs_6_ = f32[40,8,128]{2,1,0:T(8,128)S(1)} collective-permute-done((f32[40,8,128]{2,1,0:T(8,128)S(1)}, f32[40,8,128]{2,1,0:T(8,128)S(1)}, u32[]{:S(2)}, u32[]{:S(2)}) %collective-permute-start.7) | collective-permute-done | bytes 163872 | tf_op jit(solution)/shard_map/ppermute | solution.py:492
  24.6 2.4 %collective-permute-done.8.refs_7_ = f32[40,8,128]{2,1,0:T(8,128)S(1)} collective-permute-done((f32[40,8,128]{2,1,0:T(8,128)S(1)}, f32[40,8,128]{2,1,0:T(8,128)S(1)}, u32[]{:S(2)}, u32[]{:S(2)}) %collective-permute-start.8) | collective-permute-done | bytes 163872 | tf_op jit(solution)/shard_map/ppermute | solution.py:492
  27.1 0.1 shard_map.61.refs_0_
  27.2 0.9 %shard_map.62 = (f32[8,16,8,128]{3,2,1,0:T(8,128)S(1)}, f32[2,8,8,128]{3,2,1,0:T(8,128)S(1)}, f32[16,8,128]{2,1,0:T(8,128)S(1)}, f32[16,8,128]{2,1,0:T(8,128)S(1...) custom-call(f32[8,40,8,128]{3,2,1,0:T(8,128)S(1)} %shard_map.61.refs, ...), custom_call_target="tpu_custom_call" | custom-call | tf_op jit(solution)/shard_map/pallas_call | solution.py:105
  28.1 1.9 %collective-permute-start.10 = (f32[2,8,8,128]{3,2,1,0:T(8,128)S(1)}, f32[2,8,8,128]{3,2,1,0:T(8,128)S(1)}, u32[]{:S(2)}, u32[]{:S(2)}) collective-permute-start(f32[2,8,8,128]{3,2,1,0:T(8,128)S(1)} %get-tuple-element.70.sent), channel_id=1, source_target_pairs={{0,16},{2,18},{4,20},{6,22},{8,24},{10,26},{12,28},{14,30},{16,0},... | collective-permute-start | bytes 196616 | tf_op jit(solution)/shard_map/ppermute | solution.py:481
  30.0 0.9 %shard_map.63 = (f32[8,16,8,128]{3,2,1,0:T(8,128)S(1)}, f32[2,8,8,128]{3,2,1,0:T(8,128)S(1)}) custom-call(f32[8,40,8,128]{3,2,1,0:T(8,128)S(1)} %shard_map.61.refs_0_, bf16[3,512,256]{2,1,0:T(8,128)(2,1)S(1)} %get-tuple-element.60.refs_1_.high, bf16[3,512,256]{2,1,0:T(8,128)(2,1)S(1)} %get-tuple-element.51._.refs_2_.low, ...), custom_call_target="tpu_custom_call" | custom-call | tf_op jit(solution)/shard_map/pallas_call | solution.py:105
  30.9 1.2 %collective-permute-start.9 = (f32[2,8,8,128]{3,2,1,0:T(8,128)S(1)}, f32[2,8,8,128]{3,2,1,0:T(8,128)S(1)}, u32[]{:S(2)}, u32[]{:S(2)}) collective-permute-start(f32[2,8,8,128]{3,2,1,0:T(8,128)S(1)} %get-tuple-element.68.sent), channel_id=1, source_target_pairs={{0,16},{2,18},{4,20},{6,22},{8,24},{10,26},{12,28},{14,30},{16,0},... | collective-permute-start | bytes 196616 | tf_op jit(solution)/shard_map/ppermute | solution.py:481
  32.1 1.8 %collective-permute-done.10.received = f32[2,8,8,128]{3,2,1,0:T(8,128)S(1)} collective-permute-done((f32[2,8,8,128]{3,2,1,0:T(8,128)S(1)}, f32[2,8,8,128]{3,2,1,0:T(8,128)S(1)}, u32[]{:S(2)}, u32[]{:S(2)}) %collective-permute-start.10) | collective-permute-done | bytes 65568 | tf_op jit(solution)/shard_map/ppermute | solution.py:481
  33.9 0.9 %shard_map.64.refs_6_ = f32[8,32,8,128]{3,2,1,0:T(8,128)S(1)} custom-call(f32[8,16,8,128]{3,2,1,0:T(8,128)S(1)} %get-tuple-element.69.local, f32[2,8,8,128]{3,2,1,0:T(8,128)S(1)} %get-tuple-element.70.sent, f32[2,8,8,128]{3,2,1,0:T(8,128)S(1)} %collective-permute-done.10.received, bf16[3,512,256]{2,1,0:T(8,128)(2,1)S(1)} %get-tuple-element.60.refs_1_.high, ...), custom_call_target="tpu_custom_call" | custom-call | tf_op jit(solution)/shard_map/pallas_call | solution.py:105
  34.8 1.3 %collective-permute-done.9.received = f32[2,8,8,128]{3,2,1,0:T(8,128)S(1)} collective-permute-done((f32[2,8,8,128]{3,2,1,0:T(8,128)S(1)}, f32[2,8,8,128]{3,2,1,0:T(8,128)S(1)}, u32[]{:S(2)}, u32[]{:S(2)}) %collective-permute-start.9) | collective-permute-done | bytes 65568 | tf_op jit(solution)/shard_map/ppermute | solution.py:481
  36.1 0.9 %shard_map.65.pieces = f32[8,32,8,128]{3,2,1,0:T(8,128)S(1)} custom-call(f32[8,16,8,128]{3,2,1,0:T(8,128)S(1)} %get-tuple-element.67.local, f32[2,8,8,128]{3,2,1,0:T(8,128)S(1)} %get-tuple-element.68.sent, f32[2,8,8,128]{3,2,1,0:T(8,128)S(1)} %collective-permute-done.9.received, bf16[3,512,256]{2,1,0:T(8,128)(2,1)S(1)} %get-tuple-element.60.refs_1_.high, ...), custom_call_target="tpu_custom_call" | custom-call | tf_op jit(solution)/shard_map/pallas_call | solution.py:105
  37.1 0.1 shard_map.66
  37.2 1.1 %collective-permute-start.14 = (f32[32,8,128]{2,1,0:T(8,128)S(1)}, f32[32,8,128]{2,1,0:T(8,128)S(1)}, u32[]{:S(2)}, u32[]{:S(2)}) collective-permute-start(f32[32,8,128]{2,1,0:T(8,128)S(1)} %get-tuple-element.75), channel_id=1, source_target_pairs={{0,2},{1,3},{2,0},{3,1},{4,6},{5,7},{6,4},{7,5},{8,10},{9,11},{10,... | collective-permute-start | bytes 393224 | tf_op jit(solution)/shard_map/ppermute | solution.py:492
  38.3 2.7 %collective-permute-start.15 = (f32[32,8,128]{2,1,0:T(8,128)S(1)}, f32[32,8,128]{2,1,0:T(8,128)S(1)}, u32[]{:S(2)}, u32[]{:S(2)}) collective-permute-start(f32[32,8,128]{2,1,0:T(8,128)S(1)} %get-tuple-element.76), channel_id=1, source_target_pairs={{0,12},{1,13},{2,14},{3,15},{4,8},{5,9},{6,10},{7,11},{8,4},{9,5},... | collective-permute-start | bytes 393224 | tf_op jit(solution)/shard_map/ppermute | solution.py:492
  41.0 0.5 collective-permute-start.11
  41.5 0.3 collective-permute-start.16
  41.8 3.2 %collective-permute-start.17 = (f32[32,8,128]{2,1,0:T(8,128)S(1)}, f32[32,8,128]{2,1,0:T(8,128)S(1)}, u32[]{:S(2)}, u32[]{:S(2)}) collective-permute-start(f32[32,8,128]{2,1,0:T(8,128)S(1)} %get-tuple-element.78), channel_id=1, source_target_pairs={{0,10},{1,11},{2,8},{3,9},{4,14},{5,15},{6,12},{7,13},{8,2},{9,3},... | collective-permute-start | bytes 393224 | tf_op jit(solution)/shard_map/ppermute | solution.py:492
  45.0 0.0 collective-permute-done.14.refs_1_
  45.0 1.0 %collective-permute-start.12 = (f32[32,8,128]{2,1,0:T(8,128)S(1)}, f32[32,8,128]{2,1,0:T(8,128)S(1)}, u32[]{:S(2)}, u32[]{:S(2)}) collective-permute-start(f32[32,8,128]{2,1,0:T(8,128)S(1)} %get-tuple-element.72), channel_id=1, source_target_pairs={{0,6},{1,7},{2,4},{3,5},{4,2},{5,3},{6,0},{7,1},{8,14},{9,15},{10,... | collective-permute-start | bytes 393224 | tf_op jit(solution)/shard_map/ppermute | solution.py:492
  46.0 0.0 collective-permute-done.15.refs_2_
  46.0 2.5 %collective-permute-start.13 = (f32[32,8,128]{2,1,0:T(8,128)S(1)}, f32[32,8,128]{2,1,0:T(8,128)S(1)}, u32[]{:S(2)}, u32[]{:S(2)}) collective-permute-start(f32[32,8,128]{2,1,0:T(8,128)S(1)} %get-tuple-element.73), channel_id=1, source_target_pairs={{0,14},{1,15},{2,12},{3,13},{4,10},{5,11},{6,8},{7,9},{8,6},{9,7},... | collective-permute-start | bytes 393224 | tf_op jit(solution)/shard_map/ppermute | solution.py:492
  48.5 0.4 collective-permute-done.16.refs_3_
  48.9 2.1 %collective-permute-done.17.refs_4_ = f32[32,8,128]{2,1,0:T(8,128)S(1)} collective-permute-done((f32[32,8,128]{2,1,0:T(8,128)S(1)}, f32[32,8,128]{2,1,0:T(8,128)S(1)}, u32[]{:S(2)}, u32[]{:S(2)}) %collective-permute-start.17) | collective-permute-done | bytes 131104 | tf_op jit(solution)/shard_map/ppermute | solution.py:492
  51.0 0.9 %shard_map.67.refs_3_ = f32[2,128,8,128]{3,2,1,0:T(8,128)} custom-call(f32[32,8,128]{2,1,0:T(8,128)S(1)} %get-tuple-element.74.refs_0_, f32[32,8,128]{2,1,0:T(8,128)S(1)} %collective-permute-done.14.refs_1_, f32[32,8,128]{2,1,0:T(8,128)S(1)} %collective-permute-done.15.refs_2_, f32[32,8,128]{2,1,0:T(8,128)S(1)} %collective-permute-done.16.refs_3_, ...), custom_call_target="tpu_custom_call" | custom-call | tf_op jit(solution)/shard_map/pallas_call | solution.py:599
  51.9 0.0 collective-permute-done.11.refs_0_
  51.9 1.1 %collective-permute-done.12.refs_1_ = f32[32,8,128]{2,1,0:T(8,128)S(1)} collective-permute-done((f32[32,8,128]{2,1,0:T(8,128)S(1)}, f32[32,8,128]{2,1,0:T(8,128)S(1)}, u32[]{:S(2)}, u32[]{:S(2)}) %collective-permute-start.12) | collective-permute-done | bytes 131104 | tf_op jit(solution)/shard_map/ppermute | solution.py:492
  53.0 0.0 collective-permute-done.13.refs_2_
  53.0 0.8 %shard_map.68 = f32[2,128,8,128]{3,2,1,0:T(8,128)} custom-call(f32[32,8,128]{2,1,0:T(8,128)S(1)} %collective-permute-done.11.refs_0_, f32[32,8,128]{2,1,0:T(8,128)S(1)} %collective-permute-done.12.refs_1_, f32[32,8,128]{2,1,0:T(8,128)S(1)} %collective-permute-done.13.refs_2_, f32[2,128,8,128]{3,2,1,0:T(8,128)} %shard_map.67.refs_3_), custom_call_target="tpu_custom_call", output_to_operand_aliasing={{}: (3, {})} | custom-call | tf_op jit(solution)/shard_map/pallas_call | solution.py:599
Async XLA Ops:
  1.0 6.9 %collective-permute-start = (f32[2,4,8,8,128]{4,3,2,1,0:T(8,128)S(1)}, f32[2,4,8,8,128]{4,3,2,1,0:T(8,128)S(1)}, u32[]{:S(2)}, u32[]{:S(2)}) collective-permute-start(f32[2,4,8,8,128]{4,3,2,1,0:T(8,128)S(1)} %get-tuple-element.45), channel_id=1, source_target_pairs={{0,1},{1,0},{2,3},{3,2},{4,5},{5,4},{6,7},{7,6},{8,9},{9,8},{10,11... | collective-permute-start | bytes 786440 | tf_op jit(solution)/shard_map/ppermute | solution.py:481
  1.5 6.4 %collective-permute-start.1 = (f32[4,8,128]{2,1,0:T(8,128)S(1)}, f32[4,8,128]{2,1,0:T(8,128)S(1)}, u32[]{:S(2)}, u32[]{:S(2)}) collective-permute-start(f32[4,8,128]{2,1,0:T(8,128)S(1)} %get-tuple-element.42._.roots), channel_id=1, source_target_pairs={{0,16},{2,18},{4,20},{6,22},{8,24},{10,26},{12,28},{14,30},{16,0},... | collective-permute-start | bytes 49160 | tf_op jit(solution)/shard_map/ppermute | solution.py:481
  8.3 6.6 %collective-permute-start.2 = (f32[40,8,128]{2,1,0:T(8,128)S(1)}, f32[40,8,128]{2,1,0:T(8,128)S(1)}, u32[]{:S(2)}, u32[]{:S(2)}) collective-permute-start(f32[40,8,128]{2,1,0:T(8,128)S(1)} %get-tuple-element.53), channel_id=1, source_target_pairs={{0,2},{1,13},{2,0},{3,15},{4,6},{5,9},{6,4},{7,11},{8,10},{9,5},{1... | collective-permute-start | bytes 491528 | tf_op jit(solution)/shard_map/ppermute | solution.py:492
  9.8 9.2 %collective-permute-start.3 = (f32[40,8,128]{2,1,0:T(8,128)S(1)}, f32[40,8,128]{2,1,0:T(8,128)S(1)}, u32[]{:S(2)}, u32[]{:S(2)}) collective-permute-start(f32[40,8,128]{2,1,0:T(8,128)S(1)} %get-tuple-element.54), channel_id=1, source_target_pairs={{0,12},{1,3},{2,14},{3,1},{4,8},{5,7},{6,10},{7,5},{8,4},{9,11},{1... | collective-permute-start | bytes 491528 | tf_op jit(solution)/shard_map/ppermute | solution.py:492
  12.4 9.0 %collective-permute-start.4 = (f32[40,8,128]{2,1,0:T(8,128)S(1)}, f32[40,8,128]{2,1,0:T(8,128)S(1)}, u32[]{:S(2)}, u32[]{:S(2)}) collective-permute-start(f32[40,8,128]{2,1,0:T(8,128)S(1)} %get-tuple-element.55), channel_id=1, source_target_pairs={{0,4},{1,11},{2,6},{3,9},{4,0},{5,15},{6,2},{7,13},{8,12},{9,3},{1... | collective-permute-start | bytes 491528 | tf_op jit(solution)/shard_map/ppermute | solution.py:492
  12.9 8.5 %collective-permute-start.5 = (f32[40,8,128]{2,1,0:T(8,128)S(1)}, f32[40,8,128]{2,1,0:T(8,128)S(1)}, u32[]{:S(2)}, u32[]{:S(2)}) collective-permute-start(f32[40,8,128]{2,1,0:T(8,128)S(1)} %get-tuple-element.56), channel_id=1, source_target_pairs={{0,10},{1,5},{2,8},{3,7},{4,14},{5,1},{6,12},{7,3},{8,2},{9,13},{1... | collective-permute-start | bytes 491528 | tf_op jit(solution)/shard_map/ppermute | solution.py:492
  13.3 10.6 %collective-permute-start.6 = (f32[40,8,128]{2,1,0:T(8,128)S(1)}, f32[40,8,128]{2,1,0:T(8,128)S(1)}, u32[]{:S(2)}, u32[]{:S(2)}) collective-permute-start(f32[40,8,128]{2,1,0:T(8,128)S(1)} %get-tuple-element.57), channel_id=1, source_target_pairs={{0,8},{1,7},{2,10},{3,5},{4,12},{5,3},{6,14},{7,1},{8,0},{9,15},{1... | collective-permute-start | bytes 491528 | tf_op jit(solution)/shard_map/ppermute | solution.py:492
  14.9 9.8 %collective-permute-start.7 = (f32[40,8,128]{2,1,0:T(8,128)S(1)}, f32[40,8,128]{2,1,0:T(8,128)S(1)}, u32[]{:S(2)}, u32[]{:S(2)}) collective-permute-start(f32[40,8,128]{2,1,0:T(8,128)S(1)} %get-tuple-element.58), channel_id=1, source_target_pairs={{0,6},{1,9},{2,4},{3,11},{4,2},{5,13},{6,0},{7,15},{8,14},{9,1},{1... | collective-permute-start | bytes 491528 | tf_op jit(solution)/shard_map/ppermute | solution.py:492
  19.1 8.0 %collective-permute-start.8 = (f32[40,8,128]{2,1,0:T(8,128)S(1)}, f32[40,8,128]{2,1,0:T(8,128)S(1)}, u32[]{:S(2)}, u32[]{:S(2)}) collective-permute-start(f32[40,8,128]{2,1,0:T(8,128)S(1)} %get-tuple-element.59), channel_id=1, source_target_pairs={{0,14},{1,15},{2,12},{3,13},{4,10},{5,11},{6,8},{7,9},{8,6},{9,7},... | collective-permute-start | bytes 491528 | tf_op jit(solution)/shard_map/ppermute | solution.py:492
  28.1 5.8 %collective-permute-start.10 = (f32[2,8,8,128]{3,2,1,0:T(8,128)S(1)}, f32[2,8,8,128]{3,2,1,0:T(8,128)S(1)}, u32[]{:S(2)}, u32[]{:S(2)}) collective-permute-start(f32[2,8,8,128]{3,2,1,0:T(8,128)S(1)} %get-tuple-element.70.sent), channel_id=1, source_target_pairs={{0,16},{2,18},{4,20},{6,22},{8,24},{10,26},{12,28},{14,30},{16,0},... | collective-permute-start | bytes 196616 | tf_op jit(solution)/shard_map/ppermute | solution.py:481
  30.9 5.2 %collective-permute-start.9 = (f32[2,8,8,128]{3,2,1,0:T(8,128)S(1)}, f32[2,8,8,128]{3,2,1,0:T(8,128)S(1)}, u32[]{:S(2)}, u32[]{:S(2)}) collective-permute-start(f32[2,8,8,128]{3,2,1,0:T(8,128)S(1)} %get-tuple-element.68.sent), channel_id=1, source_target_pairs={{0,16},{2,18},{4,20},{6,22},{8,24},{10,26},{12,28},{14,30},{16,0},... | collective-permute-start | bytes 196616 | tf_op jit(solution)/shard_map/ppermute | solution.py:481
  37.2 7.8 %collective-permute-start.14 = (f32[32,8,128]{2,1,0:T(8,128)S(1)}, f32[32,8,128]{2,1,0:T(8,128)S(1)}, u32[]{:S(2)}, u32[]{:S(2)}) collective-permute-start(f32[32,8,128]{2,1,0:T(8,128)S(1)} %get-tuple-element.75), channel_id=1, source_target_pairs={{0,2},{1,3},{2,0},{3,1},{4,6},{5,7},{6,4},{7,5},{8,10},{9,11},{10,... | collective-permute-start | bytes 393224 | tf_op jit(solution)/shard_map/ppermute | solution.py:492
  38.3 7.7 %collective-permute-start.15 = (f32[32,8,128]{2,1,0:T(8,128)S(1)}, f32[32,8,128]{2,1,0:T(8,128)S(1)}, u32[]{:S(2)}, u32[]{:S(2)}) collective-permute-start(f32[32,8,128]{2,1,0:T(8,128)S(1)} %get-tuple-element.76), channel_id=1, source_target_pairs={{0,12},{1,13},{2,14},{3,15},{4,8},{5,9},{6,10},{7,11},{8,4},{9,5},... | collective-permute-start | bytes 393224 | tf_op jit(solution)/shard_map/ppermute | solution.py:492
  41.0 10.9 %collective-permute-start.11 = (f32[32,8,128]{2,1,0:T(8,128)S(1)}, f32[32,8,128]{2,1,0:T(8,128)S(1)}, u32[]{:S(2)}, u32[]{:S(2)}) collective-permute-start(f32[32,8,128]{2,1,0:T(8,128)S(1)} %get-tuple-element.71), channel_id=1, source_target_pairs={{0,8},{1,9},{2,10},{3,11},{4,12},{5,13},{6,14},{7,15},{8,0},{9,1},... | collective-permute-start | bytes 393224 | tf_op jit(solution)/shard_map/ppermute | solution.py:492
  41.5 7.4 %collective-permute-start.16 = (f32[32,8,128]{2,1,0:T(8,128)S(1)}, f32[32,8,128]{2,1,0:T(8,128)S(1)}, u32[]{:S(2)}, u32[]{:S(2)}) collective-permute-start(f32[32,8,128]{2,1,0:T(8,128)S(1)} %get-tuple-element.77), channel_id=1, source_target_pairs={{0,4},{1,5},{2,6},{3,7},{4,0},{5,1},{6,2},{7,3},{8,12},{9,13},{10,... | collective-permute-start | bytes 393224 | tf_op jit(solution)/shard_map/ppermute | solution.py:492
  41.8 9.2 %collective-permute-start.17 = (f32[32,8,128]{2,1,0:T(8,128)S(1)}, f32[32,8,128]{2,1,0:T(8,128)S(1)}, u32[]{:S(2)}, u32[]{:S(2)}) collective-permute-start(f32[32,8,128]{2,1,0:T(8,128)S(1)} %get-tuple-element.78), channel_id=1, source_target_pairs={{0,10},{1,11},{2,8},{3,9},{4,14},{5,15},{6,12},{7,13},{8,2},{9,3},... | collective-permute-start | bytes 393224 | tf_op jit(solution)/shard_map/ppermute | solution.py:492
  45.0 8.0 %collective-permute-start.12 = (f32[32,8,128]{2,1,0:T(8,128)S(1)}, f32[32,8,128]{2,1,0:T(8,128)S(1)}, u32[]{:S(2)}, u32[]{:S(2)}) collective-permute-start(f32[32,8,128]{2,1,0:T(8,128)S(1)} %get-tuple-element.72), channel_id=1, source_target_pairs={{0,6},{1,7},{2,4},{3,5},{4,2},{5,3},{6,0},{7,1},{8,14},{9,15},{10,... | collective-permute-start | bytes 393224 | tf_op jit(solution)/shard_map/ppermute | solution.py:492
  46.0 7.0 %collective-permute-start.13 = (f32[32,8,128]{2,1,0:T(8,128)S(1)}, f32[32,8,128]{2,1,0:T(8,128)S(1)}, u32[]{:S(2)}, u32[]{:S(2)}) collective-permute-start(f32[32,8,128]{2,1,0:T(8,128)S(1)} %get-tuple-element.73), channel_id=1, source_target_pairs={{0,14},{1,15},{2,12},{3,13},{4,10},{5,11},{6,8},{7,9},{8,6},{9,7},... | collective-permute-start | bytes 393224 | tf_op jit(solution)/shard_map/ppermute | solution.py:492

commit v6 on v5

--- a/solution.py
+++ b/solution.py
@@ -224,14 +224,13 @@
                     pieces[i // chunks, (p * chunks + i % chunks) * blocks + b + w] = tile
 
 
-def y_outer_kernel(groups, tiles, high, low, edge, given, roots, other_roots, _, pieces):
+def y_outer_kernel(groups, tiles, high, low, edge, given, roots, pieces):
     planes, halo, blocks = edge.shape[:3]
     chunks, width = tiles // groups, 2
     base = chunks * planes * blocks
     pieces[:, :base] = given[...]
     for i in range(groups):
-        pieces[i, base : base + 2 * planes] = roots[...]
-        pieces[i, base + 2 * planes :] = other_roots[...]
+        pieces[i, base:] = roots[...]
     first = jnp.where(lax.axis_index("gy") == 0, (tiles - halo) // chunks, 0)
     for p in range(planes):
         for b in range(0, blocks, width):
@@ -359,77 +358,120 @@
     gain[k] = (1.0 - one) * (1.0 - two)
 
 
-def local_kernel(groups, planes, chunks, chunk, *refs):
-    if chunk == 0:
-        pieces, high, low, local, message, *coefficients, field, middle, halves = refs
-    else:
-        pieces, high, low, *coefficients, local, message, field, middle, halves = refs
+def hand_on_kernel(value, *refs):
+    refs[-1][...] = value[...]
+
+
+def own_kernel(base, pieces, first, second, gain, half_roots):
+    groups = pieces.shape[0]
+    planes = gain.shape[0] // groups
+    row_at = lax.axis_index("gy")
+    upper_rows = lax.broadcasted_iota(jnp.int32, (SUB, LANES), 0) < SUB // 2
+    for d in range(groups):
+        for p in range(planes):
+            k = d * planes + p
+            one, two = (pieces[d, base + i * planes + p] for i in range(2))
+            store_coefficients(k, one, two, first, second, gain)
+            front = jnp.where(upper_rows, one, pltpu.roll(two, SUB // 2, 0))
+            back = jnp.where(upper_rows, pltpu.roll(one, SUB // 2, 0), two)
+            half_roots[k] = jnp.where(row_at == 0, front, back)
+
+
+def lower_kernel(groups, own_first, own_second, own_gain, mine, other, first, second, gain):
+    half, row_at = lax.axis_index("gz") // groups, lax.axis_index("gy")
+
+    @pl.when(half == 0)
+    def _():
+        first[...] = own_first[...]
+        second[...] = own_second[...]
+        gain[...] = own_gain[...]
+
+    @pl.when(half > 0)
+    def _():
+        upper_rows = lax.broadcasted_iota(jnp.int32, (SUB, LANES), 0) < SUB // 2
+        for k in range(gain.shape[0]):
+            front = jnp.where(row_at == 0, mine[k], other[k])
+            back = jnp.where(row_at == 0, other[k], mine[k])
+            one = jnp.where(upper_rows, front, pltpu.roll(back, SUB // 2, 0))
+            two = jnp.where(upper_rows, pltpu.roll(front, SUB // 2, 0), back)
+            store_coefficients(k, one, two, first, second, gain)
+
+
+def chunk_of(ref, chunk, chunks):
+    rows = ref.shape[0] // chunks
+    return ref.at[chunk * rows : (chunk + 1) * rows]
+
+
+def local_kernel(
+    groups, planes, chunks, pieces, high, low, first, second, gain,
+    local, message, field, middle, parts,
+):
     half = lax.axis_index("gz") // groups
-    blocks = message.shape[1]
+    blocks = message.shape[2]
     count = groups * planes
-    own = coefficients[:3]
-    if chunk == 0:
-        base = chunks * planes * blocks
-        for d in range(groups):
-            for p in range(planes):
-                k = d * planes + p
-                one, two = (pieces[d, base + i * planes + p] for i in range(2))
-                store_coefficients(k, one, two, *own)
-                other_one, other_two = (pieces[d, base + (2 + i) * planes + p] for i in range(2))
-                one = jnp.where(half == 0, one, other_one)
-                two = jnp.where(half == 0, two, other_two)
-                store_coefficients(k, one, two, *coefficients[3:])
+    own = (first, second, gain)
     clear_sides(field)
     zeros = [field[0:SUB, 0:LANES]] * blocks
-
-    def source(d, p):
-        return [pieces[d, (p * chunks + chunk) * blocks + b] for b in range(blocks)]
-
-    ahead, pending = filter_back(count, planes, source, own, field, (zeros, zeros))
-    x_twice(field, middle, high, low, halves)
-
-    def finish(d, p, value):
-        for b, v in enumerate(value):
-            local[d, p * blocks + b] = v
-
-    latest, earlier = filter_forth(count, planes, middle, own, (zeros, zeros), finish)
-    for b in range(blocks):
-        message[0, b] = jnp.where(half > 0, ahead[b], latest[b])
-        message[1, b] = jnp.where(half > 0, pending[b], earlier[b])
-
-
-def join_kernel(groups, planes, chunks, chunk, local, sent, received, high, low, *refs):
-    own, lower, before = refs[:3], refs[3:6], refs[6:-5]
-    out, carried, field, middle, halves = refs[-5:]
+    carries = []
+    for chunk in range(chunks):
+
+        def source(d, p):
+            return [pieces[d, (p * chunks + chunk) * blocks + b] for b in range(blocks)]
+
+        rows = chunk_of(field, chunk, chunks)
+        carries.append(filter_back(count, planes, source, own, rows, (zeros, zeros)))
+        put(message, carries[-1][0], chunk, 0)
+        put(message, carries[-1][1], chunk, 1)
+    x_twice(field, middle, high, low, parts)
+    for chunk in range(chunks):
+
+        def finish(d, p, value):
+            for b, v in enumerate(value):
+                local[d, (p * chunks + chunk) * blocks + b] = v
+
+        rows = chunk_of(middle, chunk, chunks)
+        latest, earlier = filter_forth(count, planes, rows, own, (zeros, zeros), finish)
+
+        @pl.when(half == 0)
+        def _():
+            put(message, latest, chunk, 0)
+            put(message, earlier, chunk, 1)
+
+
+def join_kernel(
+    groups, planes, chunks, local, sent, received, high, low, *refs
+):
+    own, lower = refs[:3], refs[3:6]
+    out, carried, field, middle, parts = refs[6:]
     half = lax.axis_index("gz") // groups
-    blocks = sent.shape[1]
+    blocks = sent.shape[2]
     count = groups * planes
-    for ref in before:
-        out[...] = ref[...]
-    for i in range(2):
-        for b in range(blocks):
-            carried[i, b] = jnp.where(half == 0, received[i, b], sent[i, b])
+    carried[...] = jnp.where(half == 0, received[...], sent[...])
     clear_sides(field)
     zeros = [field[0:SUB, 0:LANES]] * blocks
-    start = (tiles_of(carried, 0), tiles_of(carried, 1))
-    filter_back(count, planes, None, lower, field, start)
-    x_twice(field, middle, high, low, halves)
-
-    def finish(d, p, value):
-        for b, v in enumerate(value):
-            out[d, (p * chunks + chunk) * blocks + b] = v + local[d, p * blocks + b]
-
-    latest, earlier = filter_forth(count, planes, middle, lower, (zeros, zeros), finish)
-    put(carried, latest, 0)
-    put(carried, earlier, 1)
-
-    @pl.when(half > 0)
-    def _():
-        begin = (
-            add(tiles_of(carried, 0), tiles_of(received, 0)),
-            add(tiles_of(carried, 1), tiles_of(received, 1)),
-        )
-        filter_forth(count, planes, None, own, begin, finish)
+    for chunk in range(chunks):
+        start = (tiles_of(carried, chunk, 0), tiles_of(carried, chunk, 1))
+        filter_back(count, planes, None, lower, chunk_of(field, chunk, chunks), start)
+    x_twice(field, middle, high, low, parts)
+    for chunk in range(chunks):
+
+        def finish(d, p, value):
+            for b, v in enumerate(value):
+                at = (p * chunks + chunk) * blocks + b
+                out[d, at] = v + local[d, at]
+
+        rows = chunk_of(middle, chunk, chunks)
+        latest, earlier = filter_forth(count, planes, rows, lower, (zeros, zeros), finish)
+        put(carried, latest, chunk, 0)
+        put(carried, earlier, chunk, 1)
+
+        @pl.when(half > 0)
+        def _():
+            begin = (
+                add(tiles_of(carried, chunk, 0), tiles_of(received, chunk, 0)),
+                add(tiles_of(carried, chunk, 1), tiles_of(received, chunk, 1)),
+            )
+            filter_forth(count, planes, None, own, begin, finish)
 
 
 def partner(pair):
@@ -543,7 +585,6 @@
         *in_hbm(field, dilations, lateral_kernel_taps),
         pltpu.with_memory_space_constraint(roots, pltpu.VMEM),
     )
-    other_roots = across(roots, "gz", groups)
     edge = across(edge, "gy", 1)
 
     width = 2 * LANES
@@ -553,7 +594,7 @@
         functools.partial(band_kernel, columns), [band, band], [], [x_step, x_taps]
     )
     body_tiles = chunks * planes * blocks
-    piece = (groups, body_tiles + 4 * planes, *tile)
+    piece = (groups, body_tiles + 2 * planes, *tile)
     (pieces,) = call(
         functools.partial(y_inner_kernel, groups),
         [(groups, body_tiles, *tile)],
@@ -564,34 +605,34 @@
         functools.partial(y_outer_kernel, groups, tiles),
         [piece],
         [],
-        [*matrices[2:], edge, pieces, roots, other_roots, low],
+        [*matrices[2:], edge, pieces, roots],
     )
     kernel = functools.partial(merge_kernel, pairs_in)
     (pieces,) = call(kernel, [piece], [], exchange(pieces, pairs_in))
 
-    all_rows, wide = count * SUB, columns + 2 * LANES
-    shared = (count, *tile)
+    all_rows, wide = chunks * count * SUB, columns + 2 * LANES
+    shared, message = (count, *tile), (chunks, 2, blocks, *tile)
+    whole = (groups, body_tiles, *tile)
     scratch = [(all_rows, wide), (all_rows, columns), ((2 * all_rows, wide), jnp.bfloat16)]
-    message, local = (2, blocks, *tile), (groups, planes * blocks, *tile)
-    parts, coefficients = [], []
-    for t in range(chunks):
-        results = call(
-            functools.partial(local_kernel, groups, planes, chunks, t),
-            [local, message] + [shared] * (0 if t else 6),
-            scratch,
-            [pieces, high, low, *coefficients],
-        )
-        coefficients = coefficients or results[2:]
-        parts.append((*results[:2], across(results[1], "gz", groups)))
-    out = []
-    for t, part in enumerate(parts):
-        out = call(
-            functools.partial(join_kernel, groups, planes, chunks, t),
-            [(groups, body_tiles, *tile)],
-            [message] + scratch,
-            [*part, high, low, *coefficients, *out],
-        )
-    pieces = exchange(out[0], pairs_out)
+    *own, mine = call(functools.partial(own_kernel, body_tiles), [shared] * 4, [], [pieces])
+    mine = across(mine, "gz", groups)
+    local, sent = call(
+        functools.partial(local_kernel, groups, planes, chunks),
+        [whole, message],
+        scratch,
+        [pieces, high, low, *own],
+    )
+    received = across(sent, "gz", groups)
+    (mine,) = call(hand_on_kernel, [shared], [], [mine, *[sent]])
+    other = across(mine, "gy", 1)
+    lower = call(functools.partial(lower_kernel, groups), [shared] * 3, [], [*own, mine, other])
+    (out,) = call(
+        functools.partial(join_kernel, groups, planes, chunks),
+        [whole],
+        [message] + scratch,
+        [local, sent, received, high, low, *own, *lower],
+    )
+    pieces = exchange(out, pairs_out)
     out, half = [], groups // 2 + 1
     for part in (slice(0, half), slice(half, groups)):
         arrays = [pltpu.with_memory_space_constraint(a, pltpu.VMEM) for a in pieces[part]]

time: 54 us -> 53.2 us (0.985)
  starting transfers between devices: 31.6 us -> 26.2 us
  waiting for transfers between devices: 12.5 us -> 17.7 us
    ppermute x4, waiting for transfers between devices: 3.16 us -> 7.74 us  [across(): lax.ppermute(array, axis, [(i, i ^ m) for i in range(lax.axis_size(axis))])]
    ppermute x4, starting transfers between devices: 7.23 us -> 3.57 us  [across(): lax.ppermute(array, axis, [(i, i ^ m) for i in range(lax.axis_size(axis))])]
    ppermute x14, starting transfers between devices: 24.4 us -> 22.6 us  [across_pair(): return lax.ppermute(array, ('gz', 'gy'), moves)]
    ppermute x14, waiting for transfers between devices: 9.36 us -> 9.92 us  [across_pair(): return lax.ppermute(array, ('gz', 'gy'), moves)]
    pallas_call x10 -> x11, Pallas kernels: 5.66 us -> 5.21 us  [call(): pl.pallas_call(kernel, out_shape=[pltpu.VMEM(shape, dtype) for shape, dty...]
  transfers between devices with their start and end apart: 18 -> 18, of which waited for: 8 -> 9; matrix products, arithmetic and copies ran while one was open for 0% -> 0% of each run, Pallas kernels for 10% -> 10%
where the time goes in v6:
time: 53.2 us; the launch traced here: 53 us
  starting transfers between devices  26.2 us (49%)
  waiting for transfers between devices  17.7 us (33%)
  Pallas kernels  9.07 us (17%)
    ppermute x14, starting transfers between devices, across_pair(): return lax.ppermute(array, ('gz', 'gy'), moves)  22.6 us
    ppermute x14, waiting for transfers between devices, across_pair(): return lax.ppermute(array, ('gz', 'gy'), moves)  9.92 us
    ppermute x4, waiting for transfers between devices, across(): lax.ppermute(array, axis, [(i, i ^ m) for i in range(lax.axis_size(axis))])  7.74 us
    pallas_call x11, Pallas kernels, call(): pl.pallas_call(kernel, out_shape=[pltpu.VMEM(shape, dtype) for shape, dty...  5.21 us
    ppermute x4, starting transfers between devices, across(): lax.ppermute(array, axis, [(i, i ^ m) for i in range(lax.axis_size(axis))])  3.57 us
    pallas_call x2, Pallas kernels, grouped_body(): pl.pallas_call(functools.partial(place_kernel, pairs_out[part]), out_shap...  1.62 us
    pallas_call x1, Pallas kernels, grouped_body(): pl.pallas_call(load_kernel, out_shape=[pltpu.VMEM((planes, tiles, blocks,...  1.23 us
  transfers between devices with their start and end apart: 18, of which 9 were waited for; matrix products, arithmetic and copies ran while one was open for 0% of the time, Pallas kernels for 10%

profile of v6, /device:TPU:0, one launch (start us, length us, event | category | flops | bytes accessed | tf_op | source)
XLA Modules:
  0.0 53.0 jit_solution(3309437191806510775)
XLA Ops:
  0.0 1.0 %shard_map.55 = (f32[2,4,8,8,128]{4,3,2,1,0:T(8,128)S(1)}, f32[4,8,128]{2,1,0:T(8,128)S(1)}) custom-call(f32[2,16,8,8,128]{4,3,2,1,0:T(8,128)} %bitcast.8, f32[2,1024]{1,0:T(2,128)} %one_ref.1, f32[2,1024]{1,0:T(2,128)} %two_ref.1), custom_call_target="tpu_custom_call" | custom-call | tf_op jit(solution)/shard_map/pallas_call | solution.py:551
  1.0 0.5 collective-permute-start
  1.5 1.2 %shard_map.56 = (f32[2,16,8,8,128]{4,3,2,1,0:T(8,128)S(1)}, bf16[128,128]{1,0:T(8,128)(2,1)S(1)}, bf16[128,128]{1,0:T(8,128)(2,1)S(1)}, bf16[32,32]{1,0:T(8,128)...) custom-call(f32[2,16,8,8,128]{4,3,2,1,0:T(8,128)} %bitcast.9, s32[2]{0:T(128)} %dilations_ref.1, ...), custom_call_target="tpu_custom_call" | custom-call | tf_op jit(solution)/shard_map/pallas_call | solution.py:566
  2.8 0.6 %shard_map.57.given = f32[8,32,8,128]{3,2,1,0:T(8,128)S(1)} custom-call(bf16[128,128]{1,0:T(8,128)(2,1)S(1)} %get-tuple-element.45.high, bf16[128,128]{1,0:T(8,128)(2,1)S(1)} %get-tuple-element.46.low, f32[2,16,8,8,128]{4,3,2,1,0:T(8,128)S(1)} %get-tuple-element.47.x_ref), custom_call_target="tpu_custom_call" | custom-call | tf_op jit(solution)/shard_map/pallas_call | solution.py:105
  3.3 0.0 collective-permute-done.edge
  3.4 0.3 shard_map.58.pieces
  3.6 0.1 shard_map.59
  3.7 2.6 %collective-permute-start.1 = (f32[36,8,128]{2,1,0:T(8,128)S(1)}, f32[36,8,128]{2,1,0:T(8,128)S(1)}, u32[]{:S(2)}, u32[]{:S(2)}) collective-permute-start(f32[36,8,128]{2,1,0:T(8,128)S(1)} %get-tuple-element.49), channel_id=1, source_target_pairs={{0,2},{1,13},{2,0},{3,15},{4,6},{5,9},{6,4},{7,11},{8,10},{9,5},{1... | collective-permute-start | bytes 442376 | tf_op jit(solution)/shard_map/ppermute | solution.py:534
  6.3 2.5 %collective-permute-start.2 = (f32[36,8,128]{2,1,0:T(8,128)S(1)}, f32[36,8,128]{2,1,0:T(8,128)S(1)}, u32[]{:S(2)}, u32[]{:S(2)}) collective-permute-start(f32[36,8,128]{2,1,0:T(8,128)S(1)} %get-tuple-element.50), channel_id=1, source_target_pairs={{0,12},{1,3},{2,14},{3,1},{4,8},{5,7},{6,10},{7,5},{8,4},{9,11},{1... | collective-permute-start | bytes 442376 | tf_op jit(solution)/shard_map/ppermute | solution.py:534
  8.8 0.5 collective-permute-start.3
  9.3 0.0 collective-permute-start.4
  9.3 2.0 %collective-permute-start.5 = (f32[36,8,128]{2,1,0:T(8,128)S(1)}, f32[36,8,128]{2,1,0:T(8,128)S(1)}, u32[]{:S(2)}, u32[]{:S(2)}) collective-permute-start(f32[36,8,128]{2,1,0:T(8,128)S(1)} %get-tuple-element.53), channel_id=1, source_target_pairs={{0,8},{1,7},{2,10},{3,5},{4,12},{5,3},{6,14},{7,1},{8,0},{9,15},{1... | collective-permute-start | bytes 442376 | tf_op jit(solution)/shard_map/ppermute | solution.py:534
  11.3 0.0 collective-permute-done.1.refs_1_
  11.3 2.5 %collective-permute-start.6 = (f32[36,8,128]{2,1,0:T(8,128)S(1)}, f32[36,8,128]{2,1,0:T(8,128)S(1)}, u32[]{:S(2)}, u32[]{:S(2)}) collective-permute-start(f32[36,8,128]{2,1,0:T(8,128)S(1)} %get-tuple-element.54), channel_id=1, source_target_pairs={{0,6},{1,9},{2,4},{3,11},{4,2},{5,13},{6,0},{7,15},{8,14},{9,1},{1... | collective-permute-start | bytes 442376 | tf_op jit(solution)/shard_map/ppermute | solution.py:534
  13.8 0.0 collective-permute-done.2.refs_2_
  13.8 3.5 %collective-permute-start.7 = (f32[36,8,128]{2,1,0:T(8,128)S(1)}, f32[36,8,128]{2,1,0:T(8,128)S(1)}, u32[]{:S(2)}, u32[]{:S(2)}) collective-permute-start(f32[36,8,128]{2,1,0:T(8,128)S(1)} %get-tuple-element.55), channel_id=1, source_target_pairs={{0,14},{1,15},{2,12},{3,13},{4,10},{5,11},{6,8},{7,9},{8,6},{9,7},... | collective-permute-start | bytes 442376 | tf_op jit(solution)/shard_map/ppermute | solution.py:534
  17.3 0.9 %shard_map.61 = (bf16[3,512,256]{2,1,0:T(8,128)(2,1)S(1)}, bf16[3,512,256]{2,1,0:T(8,128)(2,1)S(1)}) custom-call(s32[8,128]{1,0:T(8,128)S(1)} %get-tuple-element.56.x_step, f32[8,128]{1,0:T(8,128)S(1)} %get-tuple-element.57.x_taps), custom_call_target="tpu_custom_call" | custom-call | tf_op jit(solution)/shard_map/pallas_call | solution.py:105
  18.2 0.0 collective-permute-done.3.refs_3_
  18.2 0.0 collective-permute-done.4.refs_4_
  18.2 1.2 %collective-permute-done.5.refs_5_ = f32[36,8,128]{2,1,0:T(8,128)S(1)} collective-permute-done((f32[36,8,128]{2,1,0:T(8,128)S(1)}, f32[36,8,128]{2,1,0:T(8,128)S(1)}, u32[]{:S(2)}, u32[]{:S(2)}) %collective-permute-start.5) | collective-permute-done | bytes 147488 | tf_op jit(solution)/shard_map/ppermute | solution.py:534
  19.4 0.0 collective-permute-done.6.refs_6_
  19.5 3.2 %collective-permute-done.7.refs_7_ = f32[36,8,128]{2,1,0:T(8,128)S(1)} collective-permute-done((f32[36,8,128]{2,1,0:T(8,128)S(1)}, f32[36,8,128]{2,1,0:T(8,128)S(1)}, u32[]{:S(2)}, u32[]{:S(2)}) %collective-permute-start.7) | collective-permute-done | bytes 147488 | tf_op jit(solution)/shard_map/ppermute | solution.py:534
  22.6 0.1 shard_map.60.pieces
  22.8 2.7 %collective-permute-start.9 = (f32[16,8,128]{2,1,0:T(8,128)S(1)}, f32[16,8,128]{2,1,0:T(8,128)S(1)}, u32[]{:S(2)}, u32[]{:S(2)}) collective-permute-start(f32[16,8,128]{2,1,0:T(8,128)S(1)} %get-tuple-element.65), channel_id=1, source_target_pairs={{0,16},{2,18},{4,20},{6,22},{8,24},{10,26},{12,28},{14,30},{16,0},... | collective-permute-start | bytes 196616 | tf_op jit(solution)/shard_map/ppermute | solution.py:523
  25.4 1.6 %shard_map.63 = (f32[8,32,8,128]{3,2,1,0:T(8,128)S(1)}, f32[2,2,8,8,128]{4,3,2,1,0:T(8,128)S(1)}) custom-call(f32[8,36,8,128]{3,2,1,0:T(8,128)S(1)} %shard_map.60.pieces, bf16[3,512,256]{2,1,0:T(8,128)(2,1)S(1)} %get-tuple-element.58.high, bf16[3,512,256]{2,1,0:T(8,128)(2,1)S(1)} %get-tuple-element.59.low, ...), custom_call_target="tpu_custom_call" | custom-call | tf_op jit(solution)/shard_map/pallas_call | solution.py:105
  27.0 0.4 collective-permute-start.8
  27.4 0.6 %collective-permute-done.9.value = f32[16,8,128]{2,1,0:T(8,128)S(1)} collective-permute-done((f32[16,8,128]{2,1,0:T(8,128)S(1)}, f32[16,8,128]{2,1,0:T(8,128)S(1)}, u32[]{:S(2)}, u32[]{:S(2)}) %collective-permute-start.9) | collective-permute-done | bytes 65568 | tf_op jit(solution)/shard_map/ppermute | solution.py:523
  28.0 0.0 collective-permute-start.10
  28.0 1.2 %collective-permute-done.10.other = f32[16,8,128]{2,1,0:T(8,128)S(1)} collective-permute-done((f32[16,8,128]{2,1,0:T(8,128)S(1)}, f32[16,8,128]{2,1,0:T(8,128)S(1)}, u32[]{:S(2)}, u32[]{:S(2)}) %collective-permute-start.10) | collective-permute-done | bytes 65568 | tf_op jit(solution)/shard_map/ppermute | solution.py:523
  29.3 5.9 %collective-permute-done.8.received = f32[2,2,8,8,128]{4,3,2,1,0:T(8,128)S(1)} collective-permute-done((f32[2,2,8,8,128]{4,3,2,1,0:T(8,128)S(1)}, f32[2,2,8,8,128]{4,3,2,1,0:T(8,128)S(1)}, u32[]{:S(2)}, u32[]{:S(2)}) %collective-permute-start.8) | collective-permute-done | bytes 131104 | tf_op jit(solution)/shard_map/ppermute | solution.py:523
  35.2 1.6 %shard_map.66.pieces = f32[8,32,8,128]{3,2,1,0:T(8,128)S(1)} custom-call(f32[8,32,8,128]{3,2,1,0:T(8,128)S(1)} %get-tuple-element.63.local, f32[2,2,8,8,128]{4,3,2,1,0:T(8,128)S(1)} %get-tuple-element.64.refs_0_.sent, f32[2,2,8,8,128]{4,3,2,1,0:T(8,128)S(1)} %collective-permute-done.8.received, bf16[3,512,256]{2,1,0:T(8,128)(2,1)S(1)} %get-tuple-element.58.high, ...), custom_call_target="tpu_custom_call" | custom-call | tf_op jit(solution)/shard_map/pallas_call | solution.py:105
  36.8 0.1 shard_map.67
  36.9 0.1 collective-permute-start.14
  37.0 1.6 %collective-permute-start.15 = (f32[32,8,128]{2,1,0:T(8,128)S(1)}, f32[32,8,128]{2,1,0:T(8,128)S(1)}, u32[]{:S(2)}, u32[]{:S(2)}) collective-permute-start(f32[32,8,128]{2,1,0:T(8,128)S(1)} %get-tuple-element.74), channel_id=1, source_target_pairs={{0,12},{1,13},{2,14},{3,15},{4,8},{5,9},{6,10},{7,11},{8,4},{9,5},... | collective-permute-start | bytes 393224 | tf_op jit(solution)/shard_map/ppermute | solution.py:534
  38.6 2.0 %collective-permute-start.11 = (f32[32,8,128]{2,1,0:T(8,128)S(1)}, f32[32,8,128]{2,1,0:T(8,128)S(1)}, u32[]{:S(2)}, u32[]{:S(2)}) collective-permute-start(f32[32,8,128]{2,1,0:T(8,128)S(1)} %get-tuple-element.69), channel_id=1, source_target_pairs={{0,8},{1,9},{2,10},{3,11},{4,12},{5,13},{6,14},{7,15},{8,0},{9,1},... | collective-permute-start | bytes 393224 | tf_op jit(solution)/shard_map/ppermute | solution.py:534
  40.7 0.0 collective-permute-start.16
  40.7 1.3 %collective-permute-start.17 = (f32[32,8,128]{2,1,0:T(8,128)S(1)}, f32[32,8,128]{2,1,0:T(8,128)S(1)}, u32[]{:S(2)}, u32[]{:S(2)}) collective-permute-start(f32[32,8,128]{2,1,0:T(8,128)S(1)} %get-tuple-element.76), channel_id=1, source_target_pairs={{0,10},{1,11},{2,8},{3,9},{4,14},{5,15},{6,12},{7,13},{8,2},{9,3},... | collective-permute-start | bytes 393224 | tf_op jit(solution)/shard_map/ppermute | solution.py:534
  42.0 0.0 collective-permute-done.14.refs_1_
  42.0 1.6 %collective-permute-start.12 = (f32[32,8,128]{2,1,0:T(8,128)S(1)}, f32[32,8,128]{2,1,0:T(8,128)S(1)}, u32[]{:S(2)}, u32[]{:S(2)}) collective-permute-start(f32[32,8,128]{2,1,0:T(8,128)S(1)} %get-tuple-element.70), channel_id=1, source_target_pairs={{0,6},{1,7},{2,4},{3,5},{4,2},{5,3},{6,0},{7,1},{8,14},{9,15},{10,... | collective-permute-start | bytes 393224 | tf_op jit(solution)/shard_map/ppermute | solution.py:534
  43.6 0.4 collective-permute-done.15.refs_2_
  44.0 2.3 %collective-permute-start.13 = (f32[32,8,128]{2,1,0:T(8,128)S(1)}, f32[32,8,128]{2,1,0:T(8,128)S(1)}, u32[]{:S(2)}, u32[]{:S(2)}) collective-permute-start(f32[32,8,128]{2,1,0:T(8,128)S(1)} %get-tuple-element.71), channel_id=1, source_target_pairs={{0,14},{1,15},{2,12},{3,13},{4,10},{5,11},{6,8},{7,9},{8,6},{9,7},... | collective-permute-start | bytes 393224 | tf_op jit(solution)/shard_map/ppermute | solution.py:534
  46.3 2.6 %collective-permute-done.16.refs_3_ = f32[32,8,128]{2,1,0:T(8,128)S(1)} collective-permute-done((f32[32,8,128]{2,1,0:T(8,128)S(1)}, f32[32,8,128]{2,1,0:T(8,128)S(1)}, u32[]{:S(2)}, u32[]{:S(2)}) %collective-permute-start.16) | collective-permute-done | bytes 131104 | tf_op jit(solution)/shard_map/ppermute | solution.py:534
  49.0 1.2 %collective-permute-done.17.refs_4_ = f32[32,8,128]{2,1,0:T(8,128)S(1)} collective-permute-done((f32[32,8,128]{2,1,0:T(8,128)S(1)}, f32[32,8,128]{2,1,0:T(8,128)S(1)}, u32[]{:S(2)}, u32[]{:S(2)}) %collective-permute-start.17) | collective-permute-done | bytes 131104 | tf_op jit(solution)/shard_map/ppermute | solution.py:534
  50.1 0.9 %shard_map.68.refs_3_ = f32[2,128,8,128]{3,2,1,0:T(8,128)} custom-call(f32[32,8,128]{2,1,0:T(8,128)S(1)} %get-tuple-element.72.refs_0_, f32[32,8,128]{2,1,0:T(8,128)S(1)} %collective-permute-done.14.refs_1_, f32[32,8,128]{2,1,0:T(8,128)S(1)} %collective-permute-done.15.refs_2_, f32[32,8,128]{2,1,0:T(8,128)S(1)} %collective-permute-done.16.refs_3_, ...), custom_call_target="tpu_custom_call" | custom-call | tf_op jit(solution)/shard_map/pallas_call | solution.py:640
  51.0 0.0 collective-permute-done.11.refs_0_
  51.0 1.3 %collective-permute-done.12.refs_1_ = f32[32,8,128]{2,1,0:T(8,128)S(1)} collective-permute-done((f32[32,8,128]{2,1,0:T(8,128)S(1)}, f32[32,8,128]{2,1,0:T(8,128)S(1)}, u32[]{:S(2)}, u32[]{:S(2)}) %collective-permute-start.12) | collective-permute-done | bytes 131104 | tf_op jit(solution)/shard_map/ppermute | solution.py:534
  52.3 0.0 collective-permute-done.13.refs_2_
  52.3 0.8 %shard_map.69 = f32[2,128,8,128]{3,2,1,0:T(8,128)} custom-call(f32[32,8,128]{2,1,0:T(8,128)S(1)} %collective-permute-done.11.refs_0_, f32[32,8,128]{2,1,0:T(8,128)S(1)} %collective-permute-done.12.refs_1_, f32[32,8,128]{2,1,0:T(8,128)S(1)} %collective-permute-done.13.refs_2_, f32[2,128,8,128]{3,2,1,0:T(8,128)} %shard_map.68.refs_3_), custom_call_target="tpu_custom_call", output_to_operand_aliasing={{}: (3, {})} | custom-call | tf_op jit(solution)/shard_map/pallas_call | solution.py:640
  (3 shorter events, 0.0 us)
Async XLA Ops:
  1.0 2.3 %collective-permute-start = (f32[2,4,8,8,128]{4,3,2,1,0:T(8,128)S(1)}, f32[2,4,8,8,128]{4,3,2,1,0:T(8,128)S(1)}, u32[]{:S(2)}, u32[]{:S(2)}) collective-permute-start(f32[2,4,8,8,128]{4,3,2,1,0:T(8,128)S(1)} %get-tuple-element.44), channel_id=1, source_target_pairs={{0,1},{1,0},{2,3},{3,2},{4,5},{5,4},{6,7},{7,6},{8,9},{9,8},{10,11... | collective-permute-start | bytes 786440 | tf_op jit(solution)/shard_map/ppermute | solution.py:523
  3.7 7.6 %collective-permute-start.1 = (f32[36,8,128]{2,1,0:T(8,128)S(1)}, f32[36,8,128]{2,1,0:T(8,128)S(1)}, u32[]{:S(2)}, u32[]{:S(2)}) collective-permute-start(f32[36,8,128]{2,1,0:T(8,128)S(1)} %get-tuple-element.49), channel_id=1, source_target_pairs={{0,2},{1,13},{2,0},{3,15},{4,6},{5,9},{6,4},{7,11},{8,10},{9,5},{1... | collective-permute-start | bytes 442376 | tf_op jit(solution)/shard_map/ppermute | solution.py:534
  6.3 7.6 %collective-permute-start.2 = (f32[36,8,128]{2,1,0:T(8,128)S(1)}, f32[36,8,128]{2,1,0:T(8,128)S(1)}, u32[]{:S(2)}, u32[]{:S(2)}) collective-permute-start(f32[36,8,128]{2,1,0:T(8,128)S(1)} %get-tuple-element.50), channel_id=1, source_target_pairs={{0,12},{1,3},{2,14},{3,1},{4,8},{5,7},{6,10},{7,5},{8,4},{9,11},{1... | collective-permute-start | bytes 442376 | tf_op jit(solution)/shard_map/ppermute | solution.py:534
  8.8 9.4 %collective-permute-start.3 = (f32[36,8,128]{2,1,0:T(8,128)S(1)}, f32[36,8,128]{2,1,0:T(8,128)S(1)}, u32[]{:S(2)}, u32[]{:S(2)}) collective-permute-start(f32[36,8,128]{2,1,0:T(8,128)S(1)} %get-tuple-element.51), channel_id=1, source_target_pairs={{0,4},{1,11},{2,6},{3,9},{4,0},{5,15},{6,2},{7,13},{8,12},{9,3},{1... | collective-permute-start | bytes 442376 | tf_op jit(solution)/shard_map/ppermute | solution.py:534
  9.3 8.9 %collective-permute-start.4 = (f32[36,8,128]{2,1,0:T(8,128)S(1)}, f32[36,8,128]{2,1,0:T(8,128)S(1)}, u32[]{:S(2)}, u32[]{:S(2)}) collective-permute-start(f32[36,8,128]{2,1,0:T(8,128)S(1)} %get-tuple-element.52), channel_id=1, source_target_pairs={{0,10},{1,5},{2,8},{3,7},{4,14},{5,1},{6,12},{7,3},{8,2},{9,13},{1... | collective-permute-start | bytes 442376 | tf_op jit(solution)/shard_map/ppermute | solution.py:534
  9.3 10.1 %collective-permute-start.5 = (f32[36,8,128]{2,1,0:T(8,128)S(1)}, f32[36,8,128]{2,1,0:T(8,128)S(1)}, u32[]{:S(2)}, u32[]{:S(2)}) collective-permute-start(f32[36,8,128]{2,1,0:T(8,128)S(1)} %get-tuple-element.53), channel_id=1, source_target_pairs={{0,8},{1,7},{2,10},{3,5},{4,12},{5,3},{6,14},{7,1},{8,0},{9,15},{1... | collective-permute-start | bytes 442376 | tf_op jit(solution)/shard_map/ppermute | solution.py:534
  11.3 8.1 %collective-permute-start.6 = (f32[36,8,128]{2,1,0:T(8,128)S(1)}, f32[36,8,128]{2,1,0:T(8,128)S(1)}, u32[]{:S(2)}, u32[]{:S(2)}) collective-permute-start(f32[36,8,128]{2,1,0:T(8,128)S(1)} %get-tuple-element.54), channel_id=1, source_target_pairs={{0,6},{1,9},{2,4},{3,11},{4,2},{5,13},{6,0},{7,15},{8,14},{9,1},{1... | collective-permute-start | bytes 442376 | tf_op jit(solution)/shard_map/ppermute | solution.py:534
  13.8 8.8 %collective-permute-start.7 = (f32[36,8,128]{2,1,0:T(8,128)S(1)}, f32[36,8,128]{2,1,0:T(8,128)S(1)}, u32[]{:S(2)}, u32[]{:S(2)}) collective-permute-start(f32[36,8,128]{2,1,0:T(8,128)S(1)} %get-tuple-element.55), channel_id=1, source_target_pairs={{0,14},{1,15},{2,12},{3,13},{4,10},{5,11},{6,8},{7,9},{8,6},{9,7},... | collective-permute-start | bytes 442376 | tf_op jit(solution)/shard_map/ppermute | solution.py:534
  22.8 5.2 %collective-permute-start.9 = (f32[16,8,128]{2,1,0:T(8,128)S(1)}, f32[16,8,128]{2,1,0:T(8,128)S(1)}, u32[]{:S(2)}, u32[]{:S(2)}) collective-permute-start(f32[16,8,128]{2,1,0:T(8,128)S(1)} %get-tuple-element.65), channel_id=1, source_target_pairs={{0,16},{2,18},{4,20},{6,22},{8,24},{10,26},{12,28},{14,30},{16,0},... | collective-permute-start | bytes 196616 | tf_op jit(solution)/shard_map/ppermute | solution.py:523
  27.0 8.2 %collective-permute-start.8 = (f32[2,2,8,8,128]{4,3,2,1,0:T(8,128)S(1)}, f32[2,2,8,8,128]{4,3,2,1,0:T(8,128)S(1)}, u32[]{:S(2)}, u32[]{:S(2)}) collective-permute-start(f32[2,2,8,8,128]{4,3,2,1,0:T(8,128)S(1)} %get-tuple-element.64.refs_0_.sent), channel_id=1, source_target_pairs={{0,16},{2,18},{4,20},{6,22},{8,24},{10,26},{12,28},{14,30},{16,0},... | collective-permute-start | bytes 393224 | tf_op jit(solution)/shard_map/ppermute | solution.py:523
  28.0 1.3 %collective-permute-start.10 = (f32[16,8,128]{2,1,0:T(8,128)S(1)}, f32[16,8,128]{2,1,0:T(8,128)S(1)}, u32[]{:S(2)}, u32[]{:S(2)}) collective-permute-start(f32[16,8,128]{2,1,0:T(8,128)S(1)} %shard_map.64.mine), channel_id=1, source_target_pairs={{0,1},{1,0},{2,3},{3,2},{4,5},{5,4},{6,7},{7,6},{8,9},{9,8},{10,11... | collective-permute-start | bytes 196616 | tf_op jit(solution)/shard_map/ppermute | solution.py:523
  36.9 5.1 %collective-permute-start.14 = (f32[32,8,128]{2,1,0:T(8,128)S(1)}, f32[32,8,128]{2,1,0:T(8,128)S(1)}, u32[]{:S(2)}, u32[]{:S(2)}) collective-permute-start(f32[32,8,128]{2,1,0:T(8,128)S(1)} %get-tuple-element.73), channel_id=1, source_target_pairs={{0,2},{1,3},{2,0},{3,1},{4,6},{5,7},{6,4},{7,5},{8,10},{9,11},{10,... | collective-permute-start | bytes 393224 | tf_op jit(solution)/shard_map/ppermute | solution.py:534
  37.0 7.0 %collective-permute-start.15 = (f32[32,8,128]{2,1,0:T(8,128)S(1)}, f32[32,8,128]{2,1,0:T(8,128)S(1)}, u32[]{:S(2)}, u32[]{:S(2)}) collective-permute-start(f32[32,8,128]{2,1,0:T(8,128)S(1)} %get-tuple-element.74), channel_id=1, source_target_pairs={{0,12},{1,13},{2,14},{3,15},{4,8},{5,9},{6,10},{7,11},{8,4},{9,5},... | collective-permute-start | bytes 393224 | tf_op jit(solution)/shard_map/ppermute | solution.py:534
  38.6 12.4 %collective-permute-start.11 = (f32[32,8,128]{2,1,0:T(8,128)S(1)}, f32[32,8,128]{2,1,0:T(8,128)S(1)}, u32[]{:S(2)}, u32[]{:S(2)}) collective-permute-start(f32[32,8,128]{2,1,0:T(8,128)S(1)} %get-tuple-element.69), channel_id=1, source_target_pairs={{0,8},{1,9},{2,10},{3,11},{4,12},{5,13},{6,14},{7,15},{8,0},{9,1},... | collective-permute-start | bytes 393224 | tf_op jit(solution)/shard_map/ppermute | solution.py:534
  40.7 8.3 %collective-permute-start.16 = (f32[32,8,128]{2,1,0:T(8,128)S(1)}, f32[32,8,128]{2,1,0:T(8,128)S(1)}, u32[]{:S(2)}, u32[]{:S(2)}) collective-permute-start(f32[32,8,128]{2,1,0:T(8,128)S(1)} %get-tuple-element.75), channel_id=1, source_target_pairs={{0,4},{1,5},{2,6},{3,7},{4,0},{5,1},{6,2},{7,3},{8,12},{9,13},{10,... | collective-permute-start | bytes 393224 | tf_op jit(solution)/shard_map/ppermute | solution.py:534
  40.7 9.5 %collective-permute-start.17 = (f32[32,8,128]{2,1,0:T(8,128)S(1)}, f32[32,8,128]{2,1,0:T(8,128)S(1)}, u32[]{:S(2)}, u32[]{:S(2)}) collective-permute-start(f32[32,8,128]{2,1,0:T(8,128)S(1)} %get-tuple-element.76), channel_id=1, source_target_pairs={{0,10},{1,11},{2,8},{3,9},{4,14},{5,15},{6,12},{7,13},{8,2},{9,3},... | collective-permute-start | bytes 393224 | tf_op jit(solution)/shard_map/ppermute | solution.py:534
  42.0 10.3 %collective-permute-start.12 = (f32[32,8,128]{2,1,0:T(8,128)S(1)}, f32[32,8,128]{2,1,0:T(8,128)S(1)}, u32[]{:S(2)}, u32[]{:S(2)}) collective-permute-start(f32[32,8,128]{2,1,0:T(8,128)S(1)} %get-tuple-element.70), channel_id=1, source_target_pairs={{0,6},{1,7},{2,4},{3,5},{4,2},{5,3},{6,0},{7,1},{8,14},{9,15},{10,... | collective-permute-start | bytes 393224 | tf_op jit(solution)/shard_map/ppermute | solution.py:534
  44.0 8.3 %collective-permute-start.13 = (f32[32,8,128]{2,1,0:T(8,128)S(1)}, f32[32,8,128]{2,1,0:T(8,128)S(1)}, u32[]{:S(2)}, u32[]{:S(2)}) collective-permute-start(f32[32,8,128]{2,1,0:T(8,128)S(1)} %get-tuple-element.71), channel_id=1, source_target_pairs={{0,14},{1,15},{2,12},{3,13},{4,10},{5,11},{6,8},{7,9},{8,6},{9,7},... | collective-permute-start | bytes 393224 | tf_op jit(solution)/shard_map/ppermute | solution.py:534

commit v7 on v6

--- a/solution.py
+++ b/solution.py
@@ -525,7 +525,7 @@
     first = exchange_order(groups)
     second = [m ^ (groups - 1) or groups - 1 for m in first]
     pairs_in = [(0, 0), *zip(first, second)]
-    pairs_out = [(m, m) for m in (0, *first)]
+    pairs_out = [(m, m) for m in (0, *first[-2::-1], first[-1])]
 
     def across_pair(array, pair):
         moves = [

time: 53.2 us -> 52.9 us (level)
  starting transfers between devices: 26.2 us -> 24 us
  waiting for transfers between devices: 17.7 us -> 19.4 us
    ppermute x14, starting transfers between devices: 22.6 us -> 20.5 us  [across_pair(): return lax.ppermute(array, ('gz', 'gy'), moves)]
    ppermute x14, waiting for transfers between devices: 9.92 us -> 11.7 us  [across_pair(): return lax.ppermute(array, ('gz', 'gy'), moves)]
  transfers between devices with their start and end apart: 18 -> 18, of which waited for: 9 -> 11; matrix products, arithmetic and copies ran while one was open for 0% -> 0% of each run, Pallas kernels for 10% -> 10%
where the time goes in v7:
time: 52.9 us; the launch traced here: 52.7 us
  starting transfers between devices  24 us (45%)
  waiting for transfers between devices  19.4 us (37%)
  Pallas kernels  9.07 us (17%)
    ppermute x14, starting transfers between devices, across_pair(): return lax.ppermute(array, ('gz', 'gy'), moves)  20.5 us
    ppermute x14, waiting for transfers between devices, across_pair(): return lax.ppermute(array, ('gz', 'gy'), moves)  11.7 us
    ppermute x4, waiting for transfers between devices, across(): lax.ppermute(array, axis, [(i, i ^ m) for i in range(lax.axis_size(axis))])  7.74 us
    pallas_call x11, Pallas kernels, call(): pl.pallas_call(kernel, out_shape=[pltpu.VMEM(shape, dtype) for shape, dty...  5.21 us
    ppermute x4, starting transfers between devices, across(): lax.ppermute(array, axis, [(i, i ^ m) for i in range(lax.axis_size(axis))])  3.57 us
    pallas_call x2, Pallas kernels, grouped_body(): pl.pallas_call(functools.partial(place_kernel, pairs_out[part]), out_shap...  1.62 us
    pallas_call x1, Pallas kernels, grouped_body(): pl.pallas_call(load_kernel, out_shape=[pltpu.VMEM((planes, tiles, blocks,...  1.23 us
  transfers between devices with their start and end apart: 18, of which 11 were waited for; matrix products, arithmetic and copies ran while one was open for 0% of the time, Pallas kernels for 10%

profile of v7, /device:TPU:0, one launch (start us, length us, event | category | flops | bytes accessed | tf_op | source)
XLA Modules:
  0.0 52.7 jit_solution(684202328357850630)
XLA Ops:
  0.0 1.0 %shard_map.55 = (f32[2,4,8,8,128]{4,3,2,1,0:T(8,128)S(1)}, f32[4,8,128]{2,1,0:T(8,128)S(1)}) custom-call(f32[2,16,8,8,128]{4,3,2,1,0:T(8,128)} %bitcast.8, f32[2,1024]{1,0:T(2,128)} %one_ref.1, f32[2,1024]{1,0:T(2,128)} %two_ref.1), custom_call_target="tpu_custom_call" | custom-call | tf_op jit(solution)/shard_map/pallas_call | solution.py:551
  1.0 0.5 collective-permute-start
  1.5 1.2 %shard_map.56 = (f32[2,16,8,8,128]{4,3,2,1,0:T(8,128)S(1)}, bf16[128,128]{1,0:T(8,128)(2,1)S(1)}, bf16[128,128]{1,0:T(8,128)(2,1)S(1)}, bf16[32,32]{1,0:T(8,128)...) custom-call(f32[2,16,8,8,128]{4,3,2,1,0:T(8,128)} %bitcast.9, s32[2]{0:T(128)} %dilations_ref.1, ...), custom_call_target="tpu_custom_call" | custom-call | tf_op jit(solution)/shard_map/pallas_call | solution.py:566
  2.8 0.6 %shard_map.57.given = f32[8,32,8,128]{3,2,1,0:T(8,128)S(1)} custom-call(bf16[128,128]{1,0:T(8,128)(2,1)S(1)} %get-tuple-element.45.high, bf16[128,128]{1,0:T(8,128)(2,1)S(1)} %get-tuple-element.46.low, f32[2,16,8,8,128]{4,3,2,1,0:T(8,128)S(1)} %get-tuple-element.47.x_ref), custom_call_target="tpu_custom_call" | custom-call | tf_op jit(solution)/shard_map/pallas_call | solution.py:105
  3.3 0.0 collective-permute-done.edge
  3.4 0.3 shard_map.58.pieces
  3.6 0.1 shard_map.59
  3.7 2.6 %collective-permute-start.1 = (f32[36,8,128]{2,1,0:T(8,128)S(1)}, f32[36,8,128]{2,1,0:T(8,128)S(1)}, u32[]{:S(2)}, u32[]{:S(2)}) collective-permute-start(f32[36,8,128]{2,1,0:T(8,128)S(1)} %get-tuple-element.49), channel_id=1, source_target_pairs={{0,2},{1,13},{2,0},{3,15},{4,6},{5,9},{6,4},{7,11},{8,10},{9,5},{1... | collective-permute-start | bytes 442376 | tf_op jit(solution)/shard_map/ppermute | solution.py:534
  6.3 2.5 %collective-permute-start.2 = (f32[36,8,128]{2,1,0:T(8,128)S(1)}, f32[36,8,128]{2,1,0:T(8,128)S(1)}, u32[]{:S(2)}, u32[]{:S(2)}) collective-permute-start(f32[36,8,128]{2,1,0:T(8,128)S(1)} %get-tuple-element.50), channel_id=1, source_target_pairs={{0,12},{1,3},{2,14},{3,1},{4,8},{5,7},{6,10},{7,5},{8,4},{9,11},{1... | collective-permute-start | bytes 442376 | tf_op jit(solution)/shard_map/ppermute | solution.py:534
  8.8 0.5 collective-permute-start.3
  9.3 0.0 collective-permute-start.4
  9.3 2.0 %collective-permute-start.5 = (f32[36,8,128]{2,1,0:T(8,128)S(1)}, f32[36,8,128]{2,1,0:T(8,128)S(1)}, u32[]{:S(2)}, u32[]{:S(2)}) collective-permute-start(f32[36,8,128]{2,1,0:T(8,128)S(1)} %get-tuple-element.53), channel_id=1, source_target_pairs={{0,8},{1,7},{2,10},{3,5},{4,12},{5,3},{6,14},{7,1},{8,0},{9,15},{1... | collective-permute-start | bytes 442376 | tf_op jit(solution)/shard_map/ppermute | solution.py:534
  11.3 0.0 collective-permute-done.1.refs_1_
  11.3 2.5 %collective-permute-start.6 = (f32[36,8,128]{2,1,0:T(8,128)S(1)}, f32[36,8,128]{2,1,0:T(8,128)S(1)}, u32[]{:S(2)}, u32[]{:S(2)}) collective-permute-start(f32[36,8,128]{2,1,0:T(8,128)S(1)} %get-tuple-element.54), channel_id=1, source_target_pairs={{0,6},{1,9},{2,4},{3,11},{4,2},{5,13},{6,0},{7,15},{8,14},{9,1},{1... | collective-permute-start | bytes 442376 | tf_op jit(solution)/shard_map/ppermute | solution.py:534
  13.8 0.0 collective-permute-done.2.refs_2_
  13.8 3.5 %collective-permute-start.7 = (f32[36,8,128]{2,1,0:T(8,128)S(1)}, f32[36,8,128]{2,1,0:T(8,128)S(1)}, u32[]{:S(2)}, u32[]{:S(2)}) collective-permute-start(f32[36,8,128]{2,1,0:T(8,128)S(1)} %get-tuple-element.55), channel_id=1, source_target_pairs={{0,14},{1,15},{2,12},{3,13},{4,10},{5,11},{6,8},{7,9},{8,6},{9,7},... | collective-permute-start | bytes 442376 | tf_op jit(solution)/shard_map/ppermute | solution.py:534
  17.3 0.9 %shard_map.61 = (bf16[3,512,256]{2,1,0:T(8,128)(2,1)S(1)}, bf16[3,512,256]{2,1,0:T(8,128)(2,1)S(1)}) custom-call(s32[8,128]{1,0:T(8,128)S(1)} %get-tuple-element.56.x_step, f32[8,128]{1,0:T(8,128)S(1)} %get-tuple-element.57.x_taps), custom_call_target="tpu_custom_call" | custom-call | tf_op jit(solution)/shard_map/pallas_call | solution.py:105
  18.2 0.0 collective-permute-done.3.refs_3_
  18.2 0.0 collective-permute-done.4.refs_4_
  18.2 1.2 %collective-permute-done.5.refs_5_ = f32[36,8,128]{2,1,0:T(8,128)S(1)} collective-permute-done((f32[36,8,128]{2,1,0:T(8,128)S(1)}, f32[36,8,128]{2,1,0:T(8,128)S(1)}, u32[]{:S(2)}, u32[]{:S(2)}) %collective-permute-start.5) | collective-permute-done | bytes 147488 | tf_op jit(solution)/shard_map/ppermute | solution.py:534
  19.4 0.0 collective-permute-done.6.refs_6_
  19.5 3.2 %collective-permute-done.7.refs_7_ = f32[36,8,128]{2,1,0:T(8,128)S(1)} collective-permute-done((f32[36,8,128]{2,1,0:T(8,128)S(1)}, f32[36,8,128]{2,1,0:T(8,128)S(1)}, u32[]{:S(2)}, u32[]{:S(2)}) %collective-permute-start.7) | collective-permute-done | bytes 147488 | tf_op jit(solution)/shard_map/ppermute | solution.py:534
  22.6 0.1 shard_map.60.pieces
  22.8 2.7 %collective-permute-start.9 = (f32[16,8,128]{2,1,0:T(8,128)S(1)}, f32[16,8,128]{2,1,0:T(8,128)S(1)}, u32[]{:S(2)}, u32[]{:S(2)}) collective-permute-start(f32[16,8,128]{2,1,0:T(8,128)S(1)} %get-tuple-element.65), channel_id=1, source_target_pairs={{0,16},{2,18},{4,20},{6,22},{8,24},{10,26},{12,28},{14,30},{16,0},... | collective-permute-start | bytes 196616 | tf_op jit(solution)/shard_map/ppermute | solution.py:523
  25.4 1.6 %shard_map.63 = (f32[8,32,8,128]{3,2,1,0:T(8,128)S(1)}, f32[2,2,8,8,128]{4,3,2,1,0:T(8,128)S(1)}) custom-call(f32[8,36,8,128]{3,2,1,0:T(8,128)S(1)} %shard_map.60.pieces, bf16[3,512,256]{2,1,0:T(8,128)(2,1)S(1)} %get-tuple-element.58.high, bf16[3,512,256]{2,1,0:T(8,128)(2,1)S(1)} %get-tuple-element.59.low, ...), custom_call_target="tpu_custom_call" | custom-call | tf_op jit(solution)/shard_map/pallas_call | solution.py:105
  27.0 0.4 collective-permute-start.8
  27.4 0.6 %collective-permute-done.9.value = f32[16,8,128]{2,1,0:T(8,128)S(1)} collective-permute-done((f32[16,8,128]{2,1,0:T(8,128)S(1)}, f32[16,8,128]{2,1,0:T(8,128)S(1)}, u32[]{:S(2)}, u32[]{:S(2)}) %collective-permute-start.9) | collective-permute-done | bytes 65568 | tf_op jit(solution)/shard_map/ppermute | solution.py:523
  28.0 0.0 collective-permute-start.10
  28.0 1.2 %collective-permute-done.10.other = f32[16,8,128]{2,1,0:T(8,128)S(1)} collective-permute-done((f32[16,8,128]{2,1,0:T(8,128)S(1)}, f32[16,8,128]{2,1,0:T(8,128)S(1)}, u32[]{:S(2)}, u32[]{:S(2)}) %collective-permute-start.10) | collective-permute-done | bytes 65568 | tf_op jit(solution)/shard_map/ppermute | solution.py:523
  29.3 5.9 %collective-permute-done.8.received = f32[2,2,8,8,128]{4,3,2,1,0:T(8,128)S(1)} collective-permute-done((f32[2,2,8,8,128]{4,3,2,1,0:T(8,128)S(1)}, f32[2,2,8,8,128]{4,3,2,1,0:T(8,128)S(1)}, u32[]{:S(2)}, u32[]{:S(2)}) %collective-permute-start.8) | collective-permute-done | bytes 131104 | tf_op jit(solution)/shard_map/ppermute | solution.py:523
  35.2 1.6 %shard_map.66.pieces = f32[8,32,8,128]{3,2,1,0:T(8,128)S(1)} custom-call(f32[8,32,8,128]{3,2,1,0:T(8,128)S(1)} %get-tuple-element.63.local, f32[2,2,8,8,128]{4,3,2,1,0:T(8,128)S(1)} %get-tuple-element.64.refs_0_.sent, f32[2,2,8,8,128]{4,3,2,1,0:T(8,128)S(1)} %collective-permute-done.8.received, bf16[3,512,256]{2,1,0:T(8,128)(2,1)S(1)} %get-tuple-element.58.high, ...), custom_call_target="tpu_custom_call" | custom-call | tf_op jit(solution)/shard_map/pallas_call | solution.py:105
  36.8 0.1 shard_map.67
  36.9 1.7 %collective-permute-start.14 = (f32[32,8,128]{2,1,0:T(8,128)S(1)}, f32[32,8,128]{2,1,0:T(8,128)S(1)}, u32[]{:S(2)}, u32[]{:S(2)}) collective-permute-start(f32[32,8,128]{2,1,0:T(8,128)S(1)} %get-tuple-element.73), channel_id=1, source_target_pairs={{0,6},{1,7},{2,4},{3,5},{4,2},{5,3},{6,0},{7,1},{8,14},{9,15},{10,... | collective-permute-start | bytes 393224 | tf_op jit(solution)/shard_map/ppermute | solution.py:534
  38.6 0.0 collective-permute-start.15
  38.6 1.2 %collective-permute-start.11 = (f32[32,8,128]{2,1,0:T(8,128)S(1)}, f32[32,8,128]{2,1,0:T(8,128)S(1)}, u32[]{:S(2)}, u32[]{:S(2)}) collective-permute-start(f32[32,8,128]{2,1,0:T(8,128)S(1)} %get-tuple-element.69), channel_id=1, source_target_pairs={{0,12},{1,13},{2,14},{3,15},{4,8},{5,9},{6,10},{7,11},{8,4},{9,5},... | collective-permute-start | bytes 393224 | tf_op jit(solution)/shard_map/ppermute | solution.py:534
  39.9 1.5 %collective-permute-start.16 = (f32[32,8,128]{2,1,0:T(8,128)S(1)}, f32[32,8,128]{2,1,0:T(8,128)S(1)}, u32[]{:S(2)}, u32[]{:S(2)}) collective-permute-start(f32[32,8,128]{2,1,0:T(8,128)S(1)} %get-tuple-element.75), channel_id=1, source_target_pairs={{0,10},{1,11},{2,8},{3,9},{4,14},{5,15},{6,12},{7,13},{8,2},{9,3},... | collective-permute-start | bytes 393224 | tf_op jit(solution)/shard_map/ppermute | solution.py:534
  41.4 1.1 %collective-permute-start.17 = (f32[32,8,128]{2,1,0:T(8,128)S(1)}, f32[32,8,128]{2,1,0:T(8,128)S(1)}, u32[]{:S(2)}, u32[]{:S(2)}) collective-permute-start(f32[32,8,128]{2,1,0:T(8,128)S(1)} %get-tuple-element.76), channel_id=1, source_target_pairs={{0,4},{1,5},{2,6},{3,7},{4,0},{5,1},{6,2},{7,3},{8,12},{9,13},{10,... | collective-permute-start | bytes 393224 | tf_op jit(solution)/shard_map/ppermute | solution.py:534
  42.5 1.2 %collective-permute-done.14.refs_1_ = f32[32,8,128]{2,1,0:T(8,128)S(1)} collective-permute-done((f32[32,8,128]{2,1,0:T(8,128)S(1)}, f32[32,8,128]{2,1,0:T(8,128)S(1)}, u32[]{:S(2)}, u32[]{:S(2)}) %collective-permute-start.14) | collective-permute-done | bytes 131104 | tf_op jit(solution)/shard_map/ppermute | solution.py:534
  43.7 0.0 collective-permute-start.12
  43.7 1.3 %collective-permute-done.15.refs_2_ = f32[32,8,128]{2,1,0:T(8,128)S(1)} collective-permute-done((f32[32,8,128]{2,1,0:T(8,128)S(1)}, f32[32,8,128]{2,1,0:T(8,128)S(1)}, u32[]{:S(2)}, u32[]{:S(2)}) %collective-permute-start.15) | collective-permute-done | bytes 131104 | tf_op jit(solution)/shard_map/ppermute | solution.py:534
  45.1 1.2 %collective-permute-start.13 = (f32[32,8,128]{2,1,0:T(8,128)S(1)}, f32[32,8,128]{2,1,0:T(8,128)S(1)}, u32[]{:S(2)}, u32[]{:S(2)}) collective-permute-start(f32[32,8,128]{2,1,0:T(8,128)S(1)} %get-tuple-element.71), channel_id=1, source_target_pairs={{0,14},{1,15},{2,12},{3,13},{4,10},{5,11},{6,8},{7,9},{8,6},{9,7},... | collective-permute-start | bytes 393224 | tf_op jit(solution)/shard_map/ppermute | solution.py:534
  46.3 1.9 %collective-permute-done.16.refs_3_ = f32[32,8,128]{2,1,0:T(8,128)S(1)} collective-permute-done((f32[32,8,128]{2,1,0:T(8,128)S(1)}, f32[32,8,128]{2,1,0:T(8,128)S(1)}, u32[]{:S(2)}, u32[]{:S(2)}) %collective-permute-start.16) | collective-permute-done | bytes 131104 | tf_op jit(solution)/shard_map/ppermute | solution.py:534
  48.2 1.6 %collective-permute-done.17.refs_4_ = f32[32,8,128]{2,1,0:T(8,128)S(1)} collective-permute-done((f32[32,8,128]{2,1,0:T(8,128)S(1)}, f32[32,8,128]{2,1,0:T(8,128)S(1)}, u32[]{:S(2)}, u32[]{:S(2)}) %collective-permute-start.17) | collective-permute-done | bytes 131104 | tf_op jit(solution)/shard_map/ppermute | solution.py:534
  49.8 0.9 %shard_map.68.refs_3_ = f32[2,128,8,128]{3,2,1,0:T(8,128)} custom-call(f32[32,8,128]{2,1,0:T(8,128)S(1)} %get-tuple-element.72.refs_0_, f32[32,8,128]{2,1,0:T(8,128)S(1)} %collective-permute-done.14.refs_1_, f32[32,8,128]{2,1,0:T(8,128)S(1)} %collective-permute-done.15.refs_2_, f32[32,8,128]{2,1,0:T(8,128)S(1)} %collective-permute-done.16.refs_3_, ...), custom_call_target="tpu_custom_call" | custom-call | tf_op jit(solution)/shard_map/pallas_call | solution.py:640
  50.7 0.0 collective-permute-done.11.refs_0_
  50.7 0.4 collective-permute-done.12.refs_1_
  51.1 0.8 %collective-permute-done.13.refs_2_ = f32[32,8,128]{2,1,0:T(8,128)S(1)} collective-permute-done((f32[32,8,128]{2,1,0:T(8,128)S(1)}, f32[32,8,128]{2,1,0:T(8,128)S(1)}, u32[]{:S(2)}, u32[]{:S(2)}) %collective-permute-start.13) | collective-permute-done | bytes 131104 | tf_op jit(solution)/shard_map/ppermute | solution.py:534
  51.9 0.8 %shard_map.69 = f32[2,128,8,128]{3,2,1,0:T(8,128)} custom-call(f32[32,8,128]{2,1,0:T(8,128)S(1)} %collective-permute-done.11.refs_0_, f32[32,8,128]{2,1,0:T(8,128)S(1)} %collective-permute-done.12.refs_1_, f32[32,8,128]{2,1,0:T(8,128)S(1)} %collective-permute-done.13.refs_2_, f32[2,128,8,128]{3,2,1,0:T(8,128)} %shard_map.68.refs_3_), custom_call_target="tpu_custom_call", output_to_operand_aliasing={{}: (3, {})} | custom-call | tf_op jit(solution)/shard_map/pallas_call | solution.py:640
  (3 shorter events, 0.0 us)
Async XLA Ops:
  1.0 2.3 %collective-permute-start = (f32[2,4,8,8,128]{4,3,2,1,0:T(8,128)S(1)}, f32[2,4,8,8,128]{4,3,2,1,0:T(8,128)S(1)}, u32[]{:S(2)}, u32[]{:S(2)}) collective-permute-start(f32[2,4,8,8,128]{4,3,2,1,0:T(8,128)S(1)} %get-tuple-element.44), channel_id=1, source_target_pairs={{0,1},{1,0},{2,3},{3,2},{4,5},{5,4},{6,7},{7,6},{8,9},{9,8},{10,11... | collective-permute-start | bytes 786440 | tf_op jit(solution)/shard_map/ppermute | solution.py:523
  3.7 7.6 %collective-permute-start.1 = (f32[36,8,128]{2,1,0:T(8,128)S(1)}, f32[36,8,128]{2,1,0:T(8,128)S(1)}, u32[]{:S(2)}, u32[]{:S(2)}) collective-permute-start(f32[36,8,128]{2,1,0:T(8,128)S(1)} %get-tuple-element.49), channel_id=1, source_target_pairs={{0,2},{1,13},{2,0},{3,15},{4,6},{5,9},{6,4},{7,11},{8,10},{9,5},{1... | collective-permute-start | bytes 442376 | tf_op jit(solution)/shard_map/ppermute | solution.py:534
  6.3 7.6 %collective-permute-start.2 = (f32[36,8,128]{2,1,0:T(8,128)S(1)}, f32[36,8,128]{2,1,0:T(8,128)S(1)}, u32[]{:S(2)}, u32[]{:S(2)}) collective-permute-start(f32[36,8,128]{2,1,0:T(8,128)S(1)} %get-tuple-element.50), channel_id=1, source_target_pairs={{0,12},{1,3},{2,14},{3,1},{4,8},{5,7},{6,10},{7,5},{8,4},{9,11},{1... | collective-permute-start | bytes 442376 | tf_op jit(solution)/shard_map/ppermute | solution.py:534
  8.8 9.4 %collective-permute-start.3 = (f32[36,8,128]{2,1,0:T(8,128)S(1)}, f32[36,8,128]{2,1,0:T(8,128)S(1)}, u32[]{:S(2)}, u32[]{:S(2)}) collective-permute-start(f32[36,8,128]{2,1,0:T(8,128)S(1)} %get-tuple-element.51), channel_id=1, source_target_pairs={{0,4},{1,11},{2,6},{3,9},{4,0},{5,15},{6,2},{7,13},{8,12},{9,3},{1... | collective-permute-start | bytes 442376 | tf_op jit(solution)/shard_map/ppermute | solution.py:534
  9.3 8.9 %collective-permute-start.4 = (f32[36,8,128]{2,1,0:T(8,128)S(1)}, f32[36,8,128]{2,1,0:T(8,128)S(1)}, u32[]{:S(2)}, u32[]{:S(2)}) collective-permute-start(f32[36,8,128]{2,1,0:T(8,128)S(1)} %get-tuple-element.52), channel_id=1, source_target_pairs={{0,10},{1,5},{2,8},{3,7},{4,14},{5,1},{6,12},{7,3},{8,2},{9,13},{1... | collective-permute-start | bytes 442376 | tf_op jit(solution)/shard_map/ppermute | solution.py:534
  9.3 10.1 %collective-permute-start.5 = (f32[36,8,128]{2,1,0:T(8,128)S(1)}, f32[36,8,128]{2,1,0:T(8,128)S(1)}, u32[]{:S(2)}, u32[]{:S(2)}) collective-permute-start(f32[36,8,128]{2,1,0:T(8,128)S(1)} %get-tuple-element.53), channel_id=1, source_target_pairs={{0,8},{1,7},{2,10},{3,5},{4,12},{5,3},{6,14},{7,1},{8,0},{9,15},{1... | collective-permute-start | bytes 442376 | tf_op jit(solution)/shard_map/ppermute | solution.py:534
  11.3 8.1 %collective-permute-start.6 = (f32[36,8,128]{2,1,0:T(8,128)S(1)}, f32[36,8,128]{2,1,0:T(8,128)S(1)}, u32[]{:S(2)}, u32[]{:S(2)}) collective-permute-start(f32[36,8,128]{2,1,0:T(8,128)S(1)} %get-tuple-element.54), channel_id=1, source_target_pairs={{0,6},{1,9},{2,4},{3,11},{4,2},{5,13},{6,0},{7,15},{8,14},{9,1},{1... | collective-permute-start | bytes 442376 | tf_op jit(solution)/shard_map/ppermute | solution.py:534
  13.8 8.8 %collective-permute-start.7 = (f32[36,8,128]{2,1,0:T(8,128)S(1)}, f32[36,8,128]{2,1,0:T(8,128)S(1)}, u32[]{:S(2)}, u32[]{:S(2)}) collective-permute-start(f32[36,8,128]{2,1,0:T(8,128)S(1)} %get-tuple-element.55), channel_id=1, source_target_pairs={{0,14},{1,15},{2,12},{3,13},{4,10},{5,11},{6,8},{7,9},{8,6},{9,7},... | collective-permute-start | bytes 442376 | tf_op jit(solution)/shard_map/ppermute | solution.py:534
  22.8 5.2 %collective-permute-start.9 = (f32[16,8,128]{2,1,0:T(8,128)S(1)}, f32[16,8,128]{2,1,0:T(8,128)S(1)}, u32[]{:S(2)}, u32[]{:S(2)}) collective-permute-start(f32[16,8,128]{2,1,0:T(8,128)S(1)} %get-tuple-element.65), channel_id=1, source_target_pairs={{0,16},{2,18},{4,20},{6,22},{8,24},{10,26},{12,28},{14,30},{16,0},... | collective-permute-start | bytes 196616 | tf_op jit(solution)/shard_map/ppermute | solution.py:523
  27.0 8.2 %collective-permute-start.8 = (f32[2,2,8,8,128]{4,3,2,1,0:T(8,128)S(1)}, f32[2,2,8,8,128]{4,3,2,1,0:T(8,128)S(1)}, u32[]{:S(2)}, u32[]{:S(2)}) collective-permute-start(f32[2,2,8,8,128]{4,3,2,1,0:T(8,128)S(1)} %get-tuple-element.64.refs_0_.sent), channel_id=1, source_target_pairs={{0,16},{2,18},{4,20},{6,22},{8,24},{10,26},{12,28},{14,30},{16,0},... | collective-permute-start | bytes 393224 | tf_op jit(solution)/shard_map/ppermute | solution.py:523
  28.0 1.3 %collective-permute-start.10 = (f32[16,8,128]{2,1,0:T(8,128)S(1)}, f32[16,8,128]{2,1,0:T(8,128)S(1)}, u32[]{:S(2)}, u32[]{:S(2)}) collective-permute-start(f32[16,8,128]{2,1,0:T(8,128)S(1)} %shard_map.64.mine), channel_id=1, source_target_pairs={{0,1},{1,0},{2,3},{3,2},{4,5},{5,4},{6,7},{7,6},{8,9},{9,8},{10,11... | collective-permute-start | bytes 196616 | tf_op jit(solution)/shard_map/ppermute | solution.py:523
  36.9 6.8 %collective-permute-start.14 = (f32[32,8,128]{2,1,0:T(8,128)S(1)}, f32[32,8,128]{2,1,0:T(8,128)S(1)}, u32[]{:S(2)}, u32[]{:S(2)}) collective-permute-start(f32[32,8,128]{2,1,0:T(8,128)S(1)} %get-tuple-element.73), channel_id=1, source_target_pairs={{0,6},{1,7},{2,4},{3,5},{4,2},{5,3},{6,0},{7,1},{8,14},{9,15},{10,... | collective-permute-start | bytes 393224 | tf_op jit(solution)/shard_map/ppermute | solution.py:534
  38.6 6.4 %collective-permute-start.15 = (f32[32,8,128]{2,1,0:T(8,128)S(1)}, f32[32,8,128]{2,1,0:T(8,128)S(1)}, u32[]{:S(2)}, u32[]{:S(2)}) collective-permute-start(f32[32,8,128]{2,1,0:T(8,128)S(1)} %get-tuple-element.74), channel_id=1, source_target_pairs={{0,8},{1,9},{2,10},{3,11},{4,12},{5,13},{6,14},{7,15},{8,0},{9,1},... | collective-permute-start | bytes 393224 | tf_op jit(solution)/shard_map/ppermute | solution.py:534
  38.6 12.1 %collective-permute-start.11 = (f32[32,8,128]{2,1,0:T(8,128)S(1)}, f32[32,8,128]{2,1,0:T(8,128)S(1)}, u32[]{:S(2)}, u32[]{:S(2)}) collective-permute-start(f32[32,8,128]{2,1,0:T(8,128)S(1)} %get-tuple-element.69), channel_id=1, source_target_pairs={{0,12},{1,13},{2,14},{3,15},{4,8},{5,9},{6,10},{7,11},{8,4},{9,5},... | collective-permute-start | bytes 393224 | tf_op jit(solution)/shard_map/ppermute | solution.py:534
  39.9 8.3 %collective-permute-start.16 = (f32[32,8,128]{2,1,0:T(8,128)S(1)}, f32[32,8,128]{2,1,0:T(8,128)S(1)}, u32[]{:S(2)}, u32[]{:S(2)}) collective-permute-start(f32[32,8,128]{2,1,0:T(8,128)S(1)} %get-tuple-element.75), channel_id=1, source_target_pairs={{0,10},{1,11},{2,8},{3,9},{4,14},{5,15},{6,12},{7,13},{8,2},{9,3},... | collective-permute-start | bytes 393224 | tf_op jit(solution)/shard_map/ppermute | solution.py:534
  41.4 8.5 %collective-permute-start.17 = (f32[32,8,128]{2,1,0:T(8,128)S(1)}, f32[32,8,128]{2,1,0:T(8,128)S(1)}, u32[]{:S(2)}, u32[]{:S(2)}) collective-permute-start(f32[32,8,128]{2,1,0:T(8,128)S(1)} %get-tuple-element.76), channel_id=1, source_target_pairs={{0,4},{1,5},{2,6},{3,7},{4,0},{5,1},{6,2},{7,3},{8,12},{9,13},{10,... | collective-permute-start | bytes 393224 | tf_op jit(solution)/shard_map/ppermute | solution.py:534
  43.7 7.4 %collective-permute-start.12 = (f32[32,8,128]{2,1,0:T(8,128)S(1)}, f32[32,8,128]{2,1,0:T(8,128)S(1)}, u32[]{:S(2)}, u32[]{:S(2)}) collective-permute-start(f32[32,8,128]{2,1,0:T(8,128)S(1)} %get-tuple-element.70), channel_id=1, source_target_pairs={{0,2},{1,3},{2,0},{3,1},{4,6},{5,7},{6,4},{7,5},{8,10},{9,11},{10,... | collective-permute-start | bytes 393224 | tf_op jit(solution)/shard_map/ppermute | solution.py:534
  45.1 6.8 %collective-permute-start.13 = (f32[32,8,128]{2,1,0:T(8,128)S(1)}, f32[32,8,128]{2,1,0:T(8,128)S(1)}, u32[]{:S(2)}, u32[]{:S(2)}) collective-permute-start(f32[32,8,128]{2,1,0:T(8,128)S(1)} %get-tuple-element.71), channel_id=1, source_target_pairs={{0,14},{1,15},{2,12},{3,13},{4,10},{5,11},{6,8},{7,9},{8,6},{9,7},... | collective-permute-start | bytes 393224 | tf_op jit(solution)/shard_map/ppermute | solution.py:534

commit v8 on v7

--- a/solution.py
+++ b/solution.py
@@ -12,6 +12,7 @@
 MARGIN = RADIUS * DMAX
 LANES = 128
 SUB = 8
+LOADS = 4
 
 
 def padded_y(array, width):
@@ -182,13 +183,19 @@
 ):
     row_at, row_places = lax.axis_index("gy"), lax.axis_size("gy")
     planes, tiles = x_ref.shape[:2]
-    rows = tiles * SUB
+    rows, part = tiles * SUB, tiles // LOADS
     copies = [
         pltpu.make_async_copy(dilations_ref, dilations, sems.at[0]),
         pltpu.make_async_copy(taps_ref, taps, sems.at[1]),
     ]
     copies += [
-        pltpu.make_async_copy(x_ref.at[p], whole.at[p], sems.at[2 + p]) for p in range(planes)
+        pltpu.make_async_copy(
+            x_ref.at[p, i * part : (i + 1) * part],
+            whole.at[p, i * part : (i + 1) * part],
+            sems.at[2 + p * LOADS + i],
+        )
+        for p in range(planes)
+        for i in range(LOADS)
     ]
     for copy in copies:
         copy.start()
@@ -577,7 +584,7 @@
         scratch_shapes=[
             pltpu.SMEM(dilations.shape, jnp.int32),
             pltpu.SMEM(lateral_kernel_taps.shape, jnp.float32),
-            pltpu.SemaphoreType.DMA((2 + planes,)),
+            pltpu.SemaphoreType.DMA((2 + planes * LOADS,)),
         ],
         compiler_params=params,
         cost_estimate=NO_COST,
@@ -663,6 +670,7 @@
         and places & (places - 1) == 0
         and rows % (SUB * (places // 2)) == 0
         and rows >= 4 * MARGIN
+        and rows % (SUB * LOADS) == 0
         and columns == SUB * LANES
         and planes * places >= 4
     )

time: 52.9 us -> 53 us (level)
  no operation moved by 1% of the time
where the time goes in v8:
time: 53 us; the launch traced here: 52.8 us
  starting transfers between devices  24 us (45%)
  waiting for transfers between devices  19.4 us (37%)
  Pallas kernels  9.2 us (17%)
    ppermute x14, starting transfers between devices, across_pair(): return lax.ppermute(array, ('gz', 'gy'), moves)  20.5 us
    ppermute x14, waiting for transfers between devices, across_pair(): return lax.ppermute(array, ('gz', 'gy'), moves)  11.7 us
    ppermute x4, waiting for transfers between devices, across(): lax.ppermute(array, axis, [(i, i ^ m) for i in range(lax.axis_size(axis))])  7.74 us
    pallas_call x11, Pallas kernels, call(): pl.pallas_call(kernel, out_shape=[pltpu.VMEM(shape, dtype) for shape, dty...  5.21 us
    ppermute x4, starting transfers between devices, across(): lax.ppermute(array, axis, [(i, i ^ m) for i in range(lax.axis_size(axis))])  3.57 us
    pallas_call x2, Pallas kernels, grouped_body(): pl.pallas_call(functools.partial(place_kernel, pairs_out[part]), out_shap...  1.62 us
    pallas_call x1, Pallas kernels, grouped_body(): pl.pallas_call(load_kernel, out_shape=[pltpu.VMEM((planes, tiles, blocks,...  1.37 us
  transfers between devices with their start and end apart: 18, of which 11 were waited for; matrix products, arithmetic and copies ran while one was open for 0% of the time, Pallas kernels for 10%

profile of v8, /device:TPU:0, one launch (start us, length us, event | category | flops | bytes accessed | tf_op | source)
XLA Modules:
  0.0 52.8 jit_solution(12304976916938611859)
XLA Ops:
  0.0 1.0 %shard_map.55 = (f32[2,4,8,8,128]{4,3,2,1,0:T(8,128)S(1)}, f32[4,8,128]{2,1,0:T(8,128)S(1)}) custom-call(f32[2,16,8,8,128]{4,3,2,1,0:T(8,128)} %bitcast.8, f32[2,1024]{1,0:T(2,128)} %one_ref.1, f32[2,1024]{1,0:T(2,128)} %two_ref.1), custom_call_target="tpu_custom_call" | custom-call | tf_op jit(solution)/shard_map/pallas_call | solution.py:558
  1.0 0.5 collective-permute-start
  1.5 1.4 %shard_map.56 = (f32[2,16,8,8,128]{4,3,2,1,0:T(8,128)S(1)}, bf16[128,128]{1,0:T(8,128)(2,1)S(1)}, bf16[128,128]{1,0:T(8,128)(2,1)S(1)}, bf16[32,32]{1,0:T(8,128)...) custom-call(f32[2,16,8,8,128]{4,3,2,1,0:T(8,128)} %bitcast.9, s32[2]{0:T(128)} %dilations_ref.1, ...), custom_call_target="tpu_custom_call" | custom-call | tf_op jit(solution)/shard_map/pallas_call | solution.py:573
  2.9 0.6 %shard_map.57.given = f32[8,32,8,128]{3,2,1,0:T(8,128)S(1)} custom-call(bf16[128,128]{1,0:T(8,128)(2,1)S(1)} %get-tuple-element.45.high, bf16[128,128]{1,0:T(8,128)(2,1)S(1)} %get-tuple-element.46.low, f32[2,16,8,8,128]{4,3,2,1,0:T(8,128)S(1)} %get-tuple-element.47.x_ref), custom_call_target="tpu_custom_call" | custom-call | tf_op jit(solution)/shard_map/pallas_call | solution.py:106
  3.5 0.0 collective-permute-done.edge
  3.5 0.3 shard_map.58.pieces
  3.7 0.1 shard_map.59
  3.8 2.6 %collective-permute-start.1 = (f32[36,8,128]{2,1,0:T(8,128)S(1)}, f32[36,8,128]{2,1,0:T(8,128)S(1)}, u32[]{:S(2)}, u32[]{:S(2)}) collective-permute-start(f32[36,8,128]{2,1,0:T(8,128)S(1)} %get-tuple-element.49), channel_id=1, source_target_pairs={{0,2},{1,13},{2,0},{3,15},{4,6},{5,9},{6,4},{7,11},{8,10},{9,5},{1... | collective-permute-start | bytes 442376 | tf_op jit(solution)/shard_map/ppermute | solution.py:541
  6.4 2.5 %collective-permute-start.2 = (f32[36,8,128]{2,1,0:T(8,128)S(1)}, f32[36,8,128]{2,1,0:T(8,128)S(1)}, u32[]{:S(2)}, u32[]{:S(2)}) collective-permute-start(f32[36,8,128]{2,1,0:T(8,128)S(1)} %get-tuple-element.50), channel_id=1, source_target_pairs={{0,12},{1,3},{2,14},{3,1},{4,8},{5,7},{6,10},{7,5},{8,4},{9,11},{1... | collective-permute-start | bytes 442376 | tf_op jit(solution)/shard_map/ppermute | solution.py:541
  8.9 0.5 collective-permute-start.3
  9.4 0.0 collective-permute-start.4
  9.5 2.0 %collective-permute-start.5 = (f32[36,8,128]{2,1,0:T(8,128)S(1)}, f32[36,8,128]{2,1,0:T(8,128)S(1)}, u32[]{:S(2)}, u32[]{:S(2)}) collective-permute-start(f32[36,8,128]{2,1,0:T(8,128)S(1)} %get-tuple-element.53), channel_id=1, source_target_pairs={{0,8},{1,7},{2,10},{3,5},{4,12},{5,3},{6,14},{7,1},{8,0},{9,15},{1... | collective-permute-start | bytes 442376 | tf_op jit(solution)/shard_map/ppermute | solution.py:541
  11.4 0.0 collective-permute-done.1.refs_1_
  11.4 2.5 %collective-permute-start.6 = (f32[36,8,128]{2,1,0:T(8,128)S(1)}, f32[36,8,128]{2,1,0:T(8,128)S(1)}, u32[]{:S(2)}, u32[]{:S(2)}) collective-permute-start(f32[36,8,128]{2,1,0:T(8,128)S(1)} %get-tuple-element.54), channel_id=1, source_target_pairs={{0,6},{1,9},{2,4},{3,11},{4,2},{5,13},{6,0},{7,15},{8,14},{9,1},{1... | collective-permute-start | bytes 442376 | tf_op jit(solution)/shard_map/ppermute | solution.py:541
  14.0 0.0 collective-permute-done.2.refs_2_
  14.0 3.5 %collective-permute-start.7 = (f32[36,8,128]{2,1,0:T(8,128)S(1)}, f32[36,8,128]{2,1,0:T(8,128)S(1)}, u32[]{:S(2)}, u32[]{:S(2)}) collective-permute-start(f32[36,8,128]{2,1,0:T(8,128)S(1)} %get-tuple-element.55), channel_id=1, source_target_pairs={{0,14},{1,15},{2,12},{3,13},{4,10},{5,11},{6,8},{7,9},{8,6},{9,7},... | collective-permute-start | bytes 442376 | tf_op jit(solution)/shard_map/ppermute | solution.py:541
  17.4 0.9 %shard_map.61 = (bf16[3,512,256]{2,1,0:T(8,128)(2,1)S(1)}, bf16[3,512,256]{2,1,0:T(8,128)(2,1)S(1)}) custom-call(s32[8,128]{1,0:T(8,128)S(1)} %get-tuple-element.56.x_step, f32[8,128]{1,0:T(8,128)S(1)} %get-tuple-element.57.x_taps), custom_call_target="tpu_custom_call" | custom-call | tf_op jit(solution)/shard_map/pallas_call | solution.py:106
  18.3 0.0 collective-permute-done.3.refs_3_
  18.3 0.0 collective-permute-done.4.refs_4_
  18.3 1.2 %collective-permute-done.5.refs_5_ = f32[36,8,128]{2,1,0:T(8,128)S(1)} collective-permute-done((f32[36,8,128]{2,1,0:T(8,128)S(1)}, f32[36,8,128]{2,1,0:T(8,128)S(1)}, u32[]{:S(2)}, u32[]{:S(2)}) %collective-permute-start.5) | collective-permute-done | bytes 147488 | tf_op jit(solution)/shard_map/ppermute | solution.py:541
  19.6 0.0 collective-permute-done.6.refs_6_
  19.6 3.2 %collective-permute-done.7.refs_7_ = f32[36,8,128]{2,1,0:T(8,128)S(1)} collective-permute-done((f32[36,8,128]{2,1,0:T(8,128)S(1)}, f32[36,8,128]{2,1,0:T(8,128)S(1)}, u32[]{:S(2)}, u32[]{:S(2)}) %collective-permute-start.7) | collective-permute-done | bytes 147488 | tf_op jit(solution)/shard_map/ppermute | solution.py:541
  22.8 0.1 shard_map.60.pieces
  22.9 2.7 %collective-permute-start.9 = (f32[16,8,128]{2,1,0:T(8,128)S(1)}, f32[16,8,128]{2,1,0:T(8,128)S(1)}, u32[]{:S(2)}, u32[]{:S(2)}) collective-permute-start(f32[16,8,128]{2,1,0:T(8,128)S(1)} %get-tuple-element.65), channel_id=1, source_target_pairs={{0,16},{2,18},{4,20},{6,22},{8,24},{10,26},{12,28},{14,30},{16,0},... | collective-permute-start | bytes 196616 | tf_op jit(solution)/shard_map/ppermute | solution.py:530
  25.6 1.6 %shard_map.63 = (f32[8,32,8,128]{3,2,1,0:T(8,128)S(1)}, f32[2,2,8,8,128]{4,3,2,1,0:T(8,128)S(1)}) custom-call(f32[8,36,8,128]{3,2,1,0:T(8,128)S(1)} %shard_map.60.pieces, bf16[3,512,256]{2,1,0:T(8,128)(2,1)S(1)} %get-tuple-element.58.high, bf16[3,512,256]{2,1,0:T(8,128)(2,1)S(1)} %get-tuple-element.59.low, ...), custom_call_target="tpu_custom_call" | custom-call | tf_op jit(solution)/shard_map/pallas_call | solution.py:106
  27.2 0.4 collective-permute-start.8
  27.6 0.6 %collective-permute-done.9.value = f32[16,8,128]{2,1,0:T(8,128)S(1)} collective-permute-done((f32[16,8,128]{2,1,0:T(8,128)S(1)}, f32[16,8,128]{2,1,0:T(8,128)S(1)}, u32[]{:S(2)}, u32[]{:S(2)}) %collective-permute-start.9) | collective-permute-done | bytes 65568 | tf_op jit(solution)/shard_map/ppermute | solution.py:530
  28.1 0.0 collective-permute-start.10
  28.1 1.2 %collective-permute-done.10.other = f32[16,8,128]{2,1,0:T(8,128)S(1)} collective-permute-done((f32[16,8,128]{2,1,0:T(8,128)S(1)}, f32[16,8,128]{2,1,0:T(8,128)S(1)}, u32[]{:S(2)}, u32[]{:S(2)}) %collective-permute-start.10) | collective-permute-done | bytes 65568 | tf_op jit(solution)/shard_map/ppermute | solution.py:530
  29.4 5.9 %collective-permute-done.8.received = f32[2,2,8,8,128]{4,3,2,1,0:T(8,128)S(1)} collective-permute-done((f32[2,2,8,8,128]{4,3,2,1,0:T(8,128)S(1)}, f32[2,2,8,8,128]{4,3,2,1,0:T(8,128)S(1)}, u32[]{:S(2)}, u32[]{:S(2)}) %collective-permute-start.8) | collective-permute-done | bytes 131104 | tf_op jit(solution)/shard_map/ppermute | solution.py:530
  35.4 1.6 %shard_map.66.pieces = f32[8,32,8,128]{3,2,1,0:T(8,128)S(1)} custom-call(f32[8,32,8,128]{3,2,1,0:T(8,128)S(1)} %get-tuple-element.63.local, f32[2,2,8,8,128]{4,3,2,1,0:T(8,128)S(1)} %get-tuple-element.64.refs_0_.sent, f32[2,2,8,8,128]{4,3,2,1,0:T(8,128)S(1)} %collective-permute-done.8.received, bf16[3,512,256]{2,1,0:T(8,128)(2,1)S(1)} %get-tuple-element.58.high, ...), custom_call_target="tpu_custom_call" | custom-call | tf_op jit(solution)/shard_map/pallas_call | solution.py:106
  36.9 0.1 shard_map.67
  37.0 1.7 %collective-permute-start.14 = (f32[32,8,128]{2,1,0:T(8,128)S(1)}, f32[32,8,128]{2,1,0:T(8,128)S(1)}, u32[]{:S(2)}, u32[]{:S(2)}) collective-permute-start(f32[32,8,128]{2,1,0:T(8,128)S(1)} %get-tuple-element.73), channel_id=1, source_target_pairs={{0,6},{1,7},{2,4},{3,5},{4,2},{5,3},{6,0},{7,1},{8,14},{9,15},{10,... | collective-permute-start | bytes 393224 | tf_op jit(solution)/shard_map/ppermute | solution.py:541
  38.8 0.0 collective-permute-start.15
  38.8 1.2 %collective-permute-start.11 = (f32[32,8,128]{2,1,0:T(8,128)S(1)}, f32[32,8,128]{2,1,0:T(8,128)S(1)}, u32[]{:S(2)}, u32[]{:S(2)}) collective-permute-start(f32[32,8,128]{2,1,0:T(8,128)S(1)} %get-tuple-element.69), channel_id=1, source_target_pairs={{0,12},{1,13},{2,14},{3,15},{4,8},{5,9},{6,10},{7,11},{8,4},{9,5},... | collective-permute-start | bytes 393224 | tf_op jit(solution)/shard_map/ppermute | solution.py:541
  40.0 1.5 %collective-permute-start.16 = (f32[32,8,128]{2,1,0:T(8,128)S(1)}, f32[32,8,128]{2,1,0:T(8,128)S(1)}, u32[]{:S(2)}, u32[]{:S(2)}) collective-permute-start(f32[32,8,128]{2,1,0:T(8,128)S(1)} %get-tuple-element.75), channel_id=1, source_target_pairs={{0,10},{1,11},{2,8},{3,9},{4,14},{5,15},{6,12},{7,13},{8,2},{9,3},... | collective-permute-start | bytes 393224 | tf_op jit(solution)/shard_map/ppermute | solution.py:541
  41.5 1.1 %collective-permute-start.17 = (f32[32,8,128]{2,1,0:T(8,128)S(1)}, f32[32,8,128]{2,1,0:T(8,128)S(1)}, u32[]{:S(2)}, u32[]{:S(2)}) collective-permute-start(f32[32,8,128]{2,1,0:T(8,128)S(1)} %get-tuple-element.76), channel_id=1, source_target_pairs={{0,4},{1,5},{2,6},{3,7},{4,0},{5,1},{6,2},{7,3},{8,12},{9,13},{10,... | collective-permute-start | bytes 393224 | tf_op jit(solution)/shard_map/ppermute | solution.py:541
  42.6 1.2 %collective-permute-done.14.refs_1_ = f32[32,8,128]{2,1,0:T(8,128)S(1)} collective-permute-done((f32[32,8,128]{2,1,0:T(8,128)S(1)}, f32[32,8,128]{2,1,0:T(8,128)S(1)}, u32[]{:S(2)}, u32[]{:S(2)}) %collective-permute-start.14) | collective-permute-done | bytes 131104 | tf_op jit(solution)/shard_map/ppermute | solution.py:541
  43.9 0.0 collective-permute-start.12
  43.9 1.3 %collective-permute-done.15.refs_2_ = f32[32,8,128]{2,1,0:T(8,128)S(1)} collective-permute-done((f32[32,8,128]{2,1,0:T(8,128)S(1)}, f32[32,8,128]{2,1,0:T(8,128)S(1)}, u32[]{:S(2)}, u32[]{:S(2)}) %collective-permute-start.15) | collective-permute-done | bytes 131104 | tf_op jit(solution)/shard_map/ppermute | solution.py:541
  45.2 1.3 %collective-permute-start.13 = (f32[32,8,128]{2,1,0:T(8,128)S(1)}, f32[32,8,128]{2,1,0:T(8,128)S(1)}, u32[]{:S(2)}, u32[]{:S(2)}) collective-permute-start(f32[32,8,128]{2,1,0:T(8,128)S(1)} %get-tuple-element.71), channel_id=1, source_target_pairs={{0,14},{1,15},{2,12},{3,13},{4,10},{5,11},{6,8},{7,9},{8,6},{9,7},... | collective-permute-start | bytes 393224 | tf_op jit(solution)/shard_map/ppermute | solution.py:541
  46.5 1.9 %collective-permute-done.16.refs_3_ = f32[32,8,128]{2,1,0:T(8,128)S(1)} collective-permute-done((f32[32,8,128]{2,1,0:T(8,128)S(1)}, f32[32,8,128]{2,1,0:T(8,128)S(1)}, u32[]{:S(2)}, u32[]{:S(2)}) %collective-permute-start.16) | collective-permute-done | bytes 131104 | tf_op jit(solution)/shard_map/ppermute | solution.py:541
  48.3 1.7 %collective-permute-done.17.refs_4_ = f32[32,8,128]{2,1,0:T(8,128)S(1)} collective-permute-done((f32[32,8,128]{2,1,0:T(8,128)S(1)}, f32[32,8,128]{2,1,0:T(8,128)S(1)}, u32[]{:S(2)}, u32[]{:S(2)}) %collective-permute-start.17) | collective-permute-done | bytes 131104 | tf_op jit(solution)/shard_map/ppermute | solution.py:541
  50.0 0.9 %shard_map.68.refs_3_ = f32[2,128,8,128]{3,2,1,0:T(8,128)} custom-call(f32[32,8,128]{2,1,0:T(8,128)S(1)} %get-tuple-element.72.refs_0_, f32[32,8,128]{2,1,0:T(8,128)S(1)} %collective-permute-done.14.refs_1_, f32[32,8,128]{2,1,0:T(8,128)S(1)} %collective-permute-done.15.refs_2_, f32[32,8,128]{2,1,0:T(8,128)S(1)} %collective-permute-done.16.refs_3_, ...), custom_call_target="tpu_custom_call" | custom-call | tf_op jit(solution)/shard_map/pallas_call | solution.py:647
  50.8 0.0 collective-permute-done.11.refs_0_
  50.9 0.4 collective-permute-done.12.refs_1_
  51.3 0.7 %collective-permute-done.13.refs_2_ = f32[32,8,128]{2,1,0:T(8,128)S(1)} collective-permute-done((f32[32,8,128]{2,1,0:T(8,128)S(1)}, f32[32,8,128]{2,1,0:T(8,128)S(1)}, u32[]{:S(2)}, u32[]{:S(2)}) %collective-permute-start.13) | collective-permute-done | bytes 131104 | tf_op jit(solution)/shard_map/ppermute | solution.py:541
  52.0 0.8 %shard_map.69 = f32[2,128,8,128]{3,2,1,0:T(8,128)} custom-call(f32[32,8,128]{2,1,0:T(8,128)S(1)} %collective-permute-done.11.refs_0_, f32[32,8,128]{2,1,0:T(8,128)S(1)} %collective-permute-done.12.refs_1_, f32[32,8,128]{2,1,0:T(8,128)S(1)} %collective-permute-done.13.refs_2_, f32[2,128,8,128]{3,2,1,0:T(8,128)} %shard_map.68.refs_3_), custom_call_target="tpu_custom_call", output_to_operand_aliasing={{}: (3, {})} | custom-call | tf_op jit(solution)/shard_map/pallas_call | solution.py:647
  (3 shorter events, 0.0 us)
Async XLA Ops:
  1.0 2.5 %collective-permute-start = (f32[2,4,8,8,128]{4,3,2,1,0:T(8,128)S(1)}, f32[2,4,8,8,128]{4,3,2,1,0:T(8,128)S(1)}, u32[]{:S(2)}, u32[]{:S(2)}) collective-permute-start(f32[2,4,8,8,128]{4,3,2,1,0:T(8,128)S(1)} %get-tuple-element.44), channel_id=1, source_target_pairs={{0,1},{1,0},{2,3},{3,2},{4,5},{5,4},{6,7},{7,6},{8,9},{9,8},{10,11... | collective-permute-start | bytes 786440 | tf_op jit(solution)/shard_map/ppermute | solution.py:530
  3.8 7.6 %collective-permute-start.1 = (f32[36,8,128]{2,1,0:T(8,128)S(1)}, f32[36,8,128]{2,1,0:T(8,128)S(1)}, u32[]{:S(2)}, u32[]{:S(2)}) collective-permute-start(f32[36,8,128]{2,1,0:T(8,128)S(1)} %get-tuple-element.49), channel_id=1, source_target_pairs={{0,2},{1,13},{2,0},{3,15},{4,6},{5,9},{6,4},{7,11},{8,10},{9,5},{1... | collective-permute-start | bytes 442376 | tf_op jit(solution)/shard_map/ppermute | solution.py:541
  6.4 7.6 %collective-permute-start.2 = (f32[36,8,128]{2,1,0:T(8,128)S(1)}, f32[36,8,128]{2,1,0:T(8,128)S(1)}, u32[]{:S(2)}, u32[]{:S(2)}) collective-permute-start(f32[36,8,128]{2,1,0:T(8,128)S(1)} %get-tuple-element.50), channel_id=1, source_target_pairs={{0,12},{1,3},{2,14},{3,1},{4,8},{5,7},{6,10},{7,5},{8,4},{9,11},{1... | collective-permute-start | bytes 442376 | tf_op jit(solution)/shard_map/ppermute | solution.py:541
  8.9 9.4 %collective-permute-start.3 = (f32[36,8,128]{2,1,0:T(8,128)S(1)}, f32[36,8,128]{2,1,0:T(8,128)S(1)}, u32[]{:S(2)}, u32[]{:S(2)}) collective-permute-start(f32[36,8,128]{2,1,0:T(8,128)S(1)} %get-tuple-element.51), channel_id=1, source_target_pairs={{0,4},{1,11},{2,6},{3,9},{4,0},{5,15},{6,2},{7,13},{8,12},{9,3},{1... | collective-permute-start | bytes 442376 | tf_op jit(solution)/shard_map/ppermute | solution.py:541
  9.4 8.9 %collective-permute-start.4 = (f32[36,8,128]{2,1,0:T(8,128)S(1)}, f32[36,8,128]{2,1,0:T(8,128)S(1)}, u32[]{:S(2)}, u32[]{:S(2)}) collective-permute-start(f32[36,8,128]{2,1,0:T(8,128)S(1)} %get-tuple-element.52), channel_id=1, source_target_pairs={{0,10},{1,5},{2,8},{3,7},{4,14},{5,1},{6,12},{7,3},{8,2},{9,13},{1... | collective-permute-start | bytes 442376 | tf_op jit(solution)/shard_map/ppermute | solution.py:541
  9.5 10.1 %collective-permute-start.5 = (f32[36,8,128]{2,1,0:T(8,128)S(1)}, f32[36,8,128]{2,1,0:T(8,128)S(1)}, u32[]{:S(2)}, u32[]{:S(2)}) collective-permute-start(f32[36,8,128]{2,1,0:T(8,128)S(1)} %get-tuple-element.53), channel_id=1, source_target_pairs={{0,8},{1,7},{2,10},{3,5},{4,12},{5,3},{6,14},{7,1},{8,0},{9,15},{1... | collective-permute-start | bytes 442376 | tf_op jit(solution)/shard_map/ppermute | solution.py:541
  11.4 8.1 %collective-permute-start.6 = (f32[36,8,128]{2,1,0:T(8,128)S(1)}, f32[36,8,128]{2,1,0:T(8,128)S(1)}, u32[]{:S(2)}, u32[]{:S(2)}) collective-permute-start(f32[36,8,128]{2,1,0:T(8,128)S(1)} %get-tuple-element.54), channel_id=1, source_target_pairs={{0,6},{1,9},{2,4},{3,11},{4,2},{5,13},{6,0},{7,15},{8,14},{9,1},{1... | collective-permute-start | bytes 442376 | tf_op jit(solution)/shard_map/ppermute | solution.py:541
  14.0 8.8 %collective-permute-start.7 = (f32[36,8,128]{2,1,0:T(8,128)S(1)}, f32[36,8,128]{2,1,0:T(8,128)S(1)}, u32[]{:S(2)}, u32[]{:S(2)}) collective-permute-start(f32[36,8,128]{2,1,0:T(8,128)S(1)} %get-tuple-element.55), channel_id=1, source_target_pairs={{0,14},{1,15},{2,12},{3,13},{4,10},{5,11},{6,8},{7,9},{8,6},{9,7},... | collective-permute-start | bytes 442376 | tf_op jit(solution)/shard_map/ppermute | solution.py:541
  22.9 5.2 %collective-permute-start.9 = (f32[16,8,128]{2,1,0:T(8,128)S(1)}, f32[16,8,128]{2,1,0:T(8,128)S(1)}, u32[]{:S(2)}, u32[]{:S(2)}) collective-permute-start(f32[16,8,128]{2,1,0:T(8,128)S(1)} %get-tuple-element.65), channel_id=1, source_target_pairs={{0,16},{2,18},{4,20},{6,22},{8,24},{10,26},{12,28},{14,30},{16,0},... | collective-permute-start | bytes 196616 | tf_op jit(solution)/shard_map/ppermute | solution.py:530
  27.2 8.2 %collective-permute-start.8 = (f32[2,2,8,8,128]{4,3,2,1,0:T(8,128)S(1)}, f32[2,2,8,8,128]{4,3,2,1,0:T(8,128)S(1)}, u32[]{:S(2)}, u32[]{:S(2)}) collective-permute-start(f32[2,2,8,8,128]{4,3,2,1,0:T(8,128)S(1)} %get-tuple-element.64.refs_0_.sent), channel_id=1, source_target_pairs={{0,16},{2,18},{4,20},{6,22},{8,24},{10,26},{12,28},{14,30},{16,0},... | collective-permute-start | bytes 393224 | tf_op jit(solution)/shard_map/ppermute | solution.py:530
  28.1 1.3 %collective-permute-start.10 = (f32[16,8,128]{2,1,0:T(8,128)S(1)}, f32[16,8,128]{2,1,0:T(8,128)S(1)}, u32[]{:S(2)}, u32[]{:S(2)}) collective-permute-start(f32[16,8,128]{2,1,0:T(8,128)S(1)} %shard_map.64.mine), channel_id=1, source_target_pairs={{0,1},{1,0},{2,3},{3,2},{4,5},{5,4},{6,7},{7,6},{8,9},{9,8},{10,11... | collective-permute-start | bytes 196616 | tf_op jit(solution)/shard_map/ppermute | solution.py:530
  37.0 6.8 %collective-permute-start.14 = (f32[32,8,128]{2,1,0:T(8,128)S(1)}, f32[32,8,128]{2,1,0:T(8,128)S(1)}, u32[]{:S(2)}, u32[]{:S(2)}) collective-permute-start(f32[32,8,128]{2,1,0:T(8,128)S(1)} %get-tuple-element.73), channel_id=1, source_target_pairs={{0,6},{1,7},{2,4},{3,5},{4,2},{5,3},{6,0},{7,1},{8,14},{9,15},{10,... | collective-permute-start | bytes 393224 | tf_op jit(solution)/shard_map/ppermute | solution.py:541
  38.8 6.4 %collective-permute-start.15 = (f32[32,8,128]{2,1,0:T(8,128)S(1)}, f32[32,8,128]{2,1,0:T(8,128)S(1)}, u32[]{:S(2)}, u32[]{:S(2)}) collective-permute-start(f32[32,8,128]{2,1,0:T(8,128)S(1)} %get-tuple-element.74), channel_id=1, source_target_pairs={{0,8},{1,9},{2,10},{3,11},{4,12},{5,13},{6,14},{7,15},{8,0},{9,1},... | collective-permute-start | bytes 393224 | tf_op jit(solution)/shard_map/ppermute | solution.py:541
  38.8 12.1 %collective-permute-start.11 = (f32[32,8,128]{2,1,0:T(8,128)S(1)}, f32[32,8,128]{2,1,0:T(8,128)S(1)}, u32[]{:S(2)}, u32[]{:S(2)}) collective-permute-start(f32[32,8,128]{2,1,0:T(8,128)S(1)} %get-tuple-element.69), channel_id=1, source_target_pairs={{0,12},{1,13},{2,14},{3,15},{4,8},{5,9},{6,10},{7,11},{8,4},{9,5},... | collective-permute-start | bytes 393224 | tf_op jit(solution)/shard_map/ppermute | solution.py:541
  40.0 8.3 %collective-permute-start.16 = (f32[32,8,128]{2,1,0:T(8,128)S(1)}, f32[32,8,128]{2,1,0:T(8,128)S(1)}, u32[]{:S(2)}, u32[]{:S(2)}) collective-permute-start(f32[32,8,128]{2,1,0:T(8,128)S(1)} %get-tuple-element.75), channel_id=1, source_target_pairs={{0,10},{1,11},{2,8},{3,9},{4,14},{5,15},{6,12},{7,13},{8,2},{9,3},... | collective-permute-start | bytes 393224 | tf_op jit(solution)/shard_map/ppermute | solution.py:541
  41.5 8.4 %collective-permute-start.17 = (f32[32,8,128]{2,1,0:T(8,128)S(1)}, f32[32,8,128]{2,1,0:T(8,128)S(1)}, u32[]{:S(2)}, u32[]{:S(2)}) collective-permute-start(f32[32,8,128]{2,1,0:T(8,128)S(1)} %get-tuple-element.76), channel_id=1, source_target_pairs={{0,4},{1,5},{2,6},{3,7},{4,0},{5,1},{6,2},{7,3},{8,12},{9,13},{10,... | collective-permute-start | bytes 393224 | tf_op jit(solution)/shard_map/ppermute | solution.py:541
  43.9 7.4 %collective-permute-start.12 = (f32[32,8,128]{2,1,0:T(8,128)S(1)}, f32[32,8,128]{2,1,0:T(8,128)S(1)}, u32[]{:S(2)}, u32[]{:S(2)}) collective-permute-start(f32[32,8,128]{2,1,0:T(8,128)S(1)} %get-tuple-element.70), channel_id=1, source_target_pairs={{0,2},{1,3},{2,0},{3,1},{4,6},{5,7},{6,4},{7,5},{8,10},{9,11},{10,... | collective-permute-start | bytes 393224 | tf_op jit(solution)/shard_map/ppermute | solution.py:541
  45.2 6.8 %collective-permute-start.13 = (f32[32,8,128]{2,1,0:T(8,128)S(1)}, f32[32,8,128]{2,1,0:T(8,128)S(1)}, u32[]{:S(2)}, u32[]{:S(2)}) collective-permute-start(f32[32,8,128]{2,1,0:T(8,128)S(1)} %get-tuple-element.71), channel_id=1, source_target_pairs={{0,14},{1,15},{2,12},{3,13},{4,10},{5,11},{6,8},{7,9},{8,6},{9,7},... | collective-permute-start | bytes 393224 | tf_op jit(solution)/shard_map/ppermute | solution.py:541
